TPU v7x, 32 devices: a whole 2x2x4 slice. The times are simulated.
32 devices in a mesh: dp: 4 (over y, core), seq: 8 (over z, x).
Axes of the slice: x: 2, y: 2, z: 4, core: 2. Of those that a mesh axis runs over, the one named last changes fastest.
Arguments:
- feats: bfloat16 [8, 1024, 1024], P('dp', 'seq'), may hold values from -6 to 6
- segments: int32 [8, 1024], P('dp'), may hold values from 0 to 4, as said below
- labels: int32 [8, 1024], P('dp', 'seq'), may hold values from 0 to 31
- conv_weight: bfloat16 [8192, 1024], replicated, may hold values from -0.0625 to 0.0625
- w_qkv: bfloat16 [1024, 3072], replicated, may hold values from -0.1875 to 0.1875
- w_out: bfloat16 [1024, 1024], replicated, may hold values from -1 to 1
- w_up: bfloat16 [1024, 4096], replicated, may hold values from -0.1875 to 0.1875
- w_down: bfloat16 [4096, 1024], replicated, may hold values from -0.09375 to 0.09375
- head_w: bfloat16 [1024, 32], replicated, may hold values from -0.375 to 0.375
- head_b: float32 [32], replicated, may hold values from -3 to 3
- gains: float32 [1024, 2], replicated, may hold values from 0.25 to 1.75
- biases: float32 [1024, 7], replicated, may hold values from -2 to 2
- up_bias: float32 [4096], replicated, may hold values from -2 to 2
Outputs:
- layer_out: bfloat16 [8, 1024, 1024], P('dp', 'seq')
- loss: float32 [], replicated
- grad_feats: float32 [8, 1024, 1024], P('dp', 'seq')
- grad_conv_weight: float32 [8192, 1024], P('seq')
- grad_w_qkv: float32 [1024, 3072], P('seq')
- grad_w_out: float32 [1024, 1024], P('seq')
- grad_w_up: float32 [1024, 4096], P('seq')
- grad_w_down: float32 [4096, 1024], P('seq')
- grad_head_w: float32 [1024, 32], P('seq')
- grad_head_b: float32 [32], replicated
- grad_gains: float32 [1024, 2], P('seq')
- grad_biases: float32 [1024, 7], P('seq')
- grad_up_bias: float32 [4096], P('seq')
Inputs may be any that keep to these rules, and one draw needn't show every extreme that they name: `segments`: along each row the numbers begin at 0 and rise by 0 or 1 from one frame to the next, up to at most 4; of the 2 rows on each index of dp, one, drawn from the seed, is a single utterance (all 0).
All inputs are finite; a program needn't handle non-finite values.
Results may differ from a plain program's by a relative error of at most 0.015.
Values may be sent and summed in bfloat16 or wider, within the bound.
No kernel may reach another device: no remote copies, remote signals or barrier semaphores. Data moves between devices by JAX's collectives and lax.ppermute only.
A program may use at most 576 MiB of HBM per device.

v0:
```python
from functools import partial
import math

import jax
import jax.numpy as jnp
from jax import lax
from jax.sharding import PartitionSpec as P

HEADS = 16
GROUPS = 16
KERNEL = 128
VOCAB = 32


epsilon = 1e-05
masked_score = -1e30
tap_group = 8


def extended(cells, sides, width):
    for axis, dim in sides:
        count = lax.axis_size(axis)
        ends = count - 1
        head = lax.slice_in_dim(cells, 0, width, axis=dim)
        tail = lax.slice_in_dim(cells, cells.shape[dim] - width, cells.shape[dim], axis=dim)
        cells = jnp.concatenate(
            [
                lax.ppermute(tail, axis, [(i, (i + 1) % count) for i in range(ends)]),
                cells,
                lax.ppermute(head, axis, [((i + 1) % count, i) for i in range(ends)]),
            ],
            axis=dim,
        )
    return cells


def layer_norm(values, gain_row, shift_row):
    center = values - jnp.mean(values, axis=-1, keepdims=True)
    spread = jnp.mean(center * center, axis=-1, keepdims=True)
    return center * lax.rsqrt(spread + epsilon) * gain_row + shift_row


def gelu_exact(values):
    return jax.nn.gelu(values, approximate=False)


def outer_sum(left_side, right_side):
    return lax.dot_general(
        left_side, right_side, (((0,), (0,)), ((), ())), preferred_element_type=jnp.float32
    )


def back_product(grad_rows, weight):
    return lax.dot_general(
        grad_rows, weight, (((1,), (1,)), ((), ())), preferred_element_type=jnp.float32
    )


def masked_windows(source, seg_padded, seg_local, offsets, frames):
    windows = []
    for offset in offsets:
        window = lax.dynamic_slice_in_dim(source, offset, frames, 1)
        near_ids = lax.dynamic_slice_in_dim(seg_padded, offset, frames, 1)
        keep_mask = (near_ids == seg_local)[:, :, None]
        windows.append(jnp.where(keep_mask, window, jnp.zeros_like(window)))
    return jnp.stack(windows, axis=2)


def conv_forward(feats_rim, seg_padded, seg_local, conv_weight):
    row_count, frames = seg_local.shape
    features = feats_rim.shape[2]
    group_width = features // GROUPS
    tap_count = conv_weight.shape[0] // group_width
    grouped = conv_weight.reshape(tap_count, group_width, GROUPS, group_width)

    def one_block(tap_block, running):
        offsets = [tap_block * tap_group + tap_inner for tap_inner in range(tap_group)]
        stacked = masked_windows(feats_rim, seg_padded, seg_local, offsets, frames)
        stacked = stacked.reshape(row_count, frames, tap_group, GROUPS, group_width)
        weight_part = lax.dynamic_slice_in_dim(grouped, tap_block * tap_group, tap_group, 0)
        return running + jnp.einsum(
            "rtkgi,kigo->rtgo", stacked, weight_part, preferred_element_type=jnp.float32
        )

    start_sum = jnp.zeros((row_count, frames, GROUPS, group_width), jnp.float32)
    running = lax.fori_loop(0, tap_count // tap_group, one_block, start_sum)
    return running.reshape(row_count, frames, features)


def conv_weight_grad(feats_rim, seg_padded, seg_local, grad_conv_low, tap_count):
    row_count, frames = seg_local.shape
    features = feats_rim.shape[2]
    group_width = features // GROUPS
    grad_grouped = grad_conv_low.reshape(row_count, frames, GROUPS, group_width)

    def one_block(tap_block, running):
        offsets = [tap_block * tap_group + tap_inner for tap_inner in range(tap_group)]
        stacked = masked_windows(feats_rim, seg_padded, seg_local, offsets, frames)
        stacked = stacked.reshape(row_count, frames, tap_group, GROUPS, group_width)
        block_grad = jnp.einsum(
            "rtkgi,rtgo->kigo", stacked, grad_grouped, preferred_element_type=jnp.float32
        )
        return lax.dynamic_update_slice_in_dim(running, block_grad, tap_block * tap_group, 0)

    start_sum = jnp.zeros((tap_count, group_width, GROUPS, group_width), jnp.float32)
    running = lax.fori_loop(0, tap_count // tap_group, one_block, start_sum)
    return running.reshape(tap_count * group_width, features)


def conv_input_grad(grad_rim, seg_padded, seg_local, conv_weight):
    row_count, frames = seg_local.shape
    features = grad_rim.shape[2]
    group_width = features // GROUPS
    tap_count = conv_weight.shape[0] // group_width
    grouped = conv_weight.reshape(tap_count, group_width, GROUPS, group_width)

    def one_block(tap_block, running):
        offsets = [
            tap_count - (tap_block * tap_group + tap_inner) for tap_inner in range(tap_group)
        ]
        stacked = masked_windows(grad_rim, seg_padded, seg_local, offsets, frames)
        stacked = stacked.reshape(row_count, frames, tap_group, GROUPS, group_width)
        weight_part = lax.dynamic_slice_in_dim(grouped, tap_block * tap_group, tap_group, 0)
        return running + jnp.einsum(
            "rtkgo,kigo->rtgi", stacked, weight_part, preferred_element_type=jnp.float32
        )

    start_sum = jnp.zeros((row_count, frames, GROUPS, group_width), jnp.float32)
    running = lax.fori_loop(0, tap_count // tap_group, one_block, start_sum)
    return running.reshape(row_count, frames, features)


def span_size(piece_rows, frames):
    return math.gcd(piece_rows, 8 * frames)


def attend_row(row_state, query_row, key_row, value_row, seg_query, seg_key, score_scale):
    running_max, running_sum, weighted = row_state
    scores = score_scale * jnp.einsum(
        "qhe,khe->qhk", query_row, key_row, preferred_element_type=jnp.float32
    )
    allowed = (seg_query[:, None] == seg_key[None, :])[:, None, :]
    scores = jnp.where(allowed, scores, masked_score)
    new_max = jnp.maximum(running_max, jnp.max(scores, axis=-1))
    rescale = jnp.exp(running_max - new_max)
    weights = jnp.where(allowed, jnp.exp(scores - new_max[:, :, None]), 0.0)
    running_sum = running_sum * rescale + jnp.sum(weights, axis=-1)
    weighted = weighted * rescale[:, :, None] + jnp.einsum(
        "qhk,khe->qhe", weights.astype(jnp.bfloat16), value_row, preferred_element_type=jnp.float32
    )
    return (new_max, running_sum, weighted)


def query_grad_row(
    grad_query,
    query_row,
    key_row,
    value_row,
    seg_query,
    seg_key,
    lse_row,
    dots_row,
    grad_row,
    score_scale,
):
    scores = score_scale * jnp.einsum(
        "qhe,khe->qhk", query_row, key_row, preferred_element_type=jnp.float32
    )
    allowed = (seg_query[:, None] == seg_key[None, :])[:, None, :]
    probs = jnp.where(allowed, jnp.exp(scores - lse_row[:, :, None]), 0.0)
    grad_probs = jnp.einsum("qhe,khe->qhk", grad_row, value_row, preferred_element_type=jnp.float32)
    grad_scores = (probs * (grad_probs - dots_row[:, :, None])).astype(jnp.bfloat16)
    return grad_query + score_scale * jnp.einsum(
        "qhk,khe->qhe", grad_scores, key_row, preferred_element_type=jnp.float32
    )


def key_grad_row(
    grads_pair,
    key_row,
    value_row,
    query_row,
    grad_row,
    lse_row,
    dots_row,
    seg_query,
    seg_key,
    score_scale,
):
    scores = score_scale * jnp.einsum(
        "qhe,khe->qhk", query_row, key_row, preferred_element_type=jnp.float32
    )
    allowed = (seg_query[:, None] == seg_key[None, :])[:, None, :]
    probs = jnp.where(allowed, jnp.exp(scores - lse_row[:, :, None]), 0.0)
    grad_value = jnp.einsum(
        "qhk,qhe->khe", probs.astype(jnp.bfloat16), grad_row, preferred_element_type=jnp.float32
    )
    grad_probs = jnp.einsum("qhe,khe->qhk", grad_row, value_row, preferred_element_type=jnp.float32)
    grad_scores = (probs * (grad_probs - dots_row[:, :, None])).astype(jnp.bfloat16)
    grad_key = score_scale * jnp.einsum(
        "qhk,qhe->khe", grad_scores, query_row, preferred_element_type=jnp.float32
    )
    return (grad_key, grad_value)


def body(
    feats,
    segments,
    labels,
    conv_weight,
    w_qkv,
    w_out,
    w_up,
    w_down,
    head_w,
    head_b,
    gains,
    biases,
    up_bias,
):
    row_count, frames, features = feats.shape
    head_count = HEADS
    head_width = features // head_count
    score_scale = head_width ** (-0.5)
    tokens = row_count * frames
    tap_count = KERNEL
    rim_width = tap_count // 2
    own_first = lax.axis_index("seq") * frames
    seg_local = lax.dynamic_slice_in_dim(segments, own_first, frames, 1)
    seg_wide = jnp.pad(segments, ((0, 0), (rim_width, rim_width)), constant_values=-1)
    seg_padded = lax.dynamic_slice_in_dim(seg_wide, own_first, frames + 2 * rim_width, 1)
    feats_rim = extended(feats, (("seq", 1),), rim_width)
    conv_sum = conv_forward(feats_rim, seg_padded, seg_local, conv_weight) + biases[:, 0]
    activated, conv_pull = jax.vjp(gelu_exact, conv_sum)
    position = feats.astype(jnp.float32) + activated
    normed, first_pull = jax.vjp(layer_norm, position, gains[:, 0], biases[:, 1])
    normed_low = normed.astype(jnp.bfloat16).reshape(tokens, features)
    qkv_bias = jnp.concatenate([biases[:, 2], jnp.zeros((features,), jnp.float32), biases[:, 3]])
    mixed = (jnp.dot(normed_low, w_qkv, preferred_element_type=jnp.float32) + qkv_bias).astype(
        jnp.bfloat16
    )
    queries = mixed[:, :features].reshape(row_count, frames, head_count, head_width)
    keys = mixed[:, features : 2 * features].reshape(row_count, frames, features)
    values = mixed[:, 2 * features :].reshape(row_count, frames, features)
    start_state = (
        jnp.full((row_count, frames, head_count), masked_score, jnp.float32),
        jnp.zeros((row_count, frames, head_count), jnp.float32),
        jnp.zeros((row_count, frames, head_count, head_width), jnp.float32),
    )
    key_shard = lax.all_gather(keys, "seq", axis=1, tiled=True)
    value_shard = lax.all_gather(values, "seq", axis=1, tiled=True)
    piece_rows = key_shard.shape[1]
    span = span_size(piece_rows, frames)

    def forward_one_span(span_index, state):
        offset = span_index * span
        key_part = lax.dynamic_slice_in_dim(key_shard, offset, span, 1)
        value_part = lax.dynamic_slice_in_dim(value_shard, offset, span, 1)
        seg_keys = lax.dynamic_slice_in_dim(segments, offset, span, 1)
        results = []
        for row_index in range(row_count):
            action = partial(
                attend_row,
                query_row=queries[row_index],
                key_row=key_part[row_index].reshape(span, head_count, head_width),
                value_row=value_part[row_index].reshape(span, head_count, head_width),
                seg_query=seg_local[row_index],
                seg_key=seg_keys[row_index],
                score_scale=score_scale,
            )
            row_state = (state[0][row_index], state[1][row_index], state[2][row_index])
            results.append(action(row_state))
        return (
            jnp.stack([item[0] for item in results]),
            jnp.stack([item[1] for item in results]),
            jnp.stack([item[2] for item in results]),
        )

    running_max, running_sum, weighted = lax.fori_loop(
        0, piece_rows // span, forward_one_span, start_state
    )
    attended = weighted / running_sum[:, :, :, None]
    log_total = running_max + jnp.log(running_sum)
    attended_low = attended.reshape(tokens, features).astype(jnp.bfloat16)
    resid = (
        position.reshape(tokens, features)
        + jnp.dot(attended_low, w_out, preferred_element_type=jnp.float32)
        + biases[:, 4]
    )
    normed_second, second_pull = jax.vjp(layer_norm, resid, gains[:, 1], biases[:, 5])
    second_low = normed_second.astype(jnp.bfloat16)
    up_sum = jnp.dot(second_low, w_up, preferred_element_type=jnp.float32) + up_bias
    up_active, up_pull = jax.vjp(gelu_exact, up_sum)
    active_low = up_active.astype(jnp.bfloat16)
    output = resid + jnp.dot(active_low, w_down, preferred_element_type=jnp.float32) + biases[:, 6]
    output_low = output.astype(jnp.bfloat16)
    logits = jnp.dot(output_low, head_w, preferred_element_type=jnp.float32) + head_b
    row_top = jnp.max(logits, axis=-1, keepdims=True)
    shifted = jnp.exp(logits - row_top)
    exp_sums = jnp.sum(shifted, axis=-1, keepdims=True)
    onehot = labels.reshape(tokens)[:, None] == jnp.arange(VOCAB, dtype=jnp.int32)[None, :]
    picked = jnp.sum(jnp.where(onehot, logits, 0.0), axis=-1)
    local_loss = jnp.sum(row_top[:, 0] + jnp.log(exp_sums[:, 0]) - picked)
    grad_logits = (shifted / exp_sums - onehot.astype(jnp.float32)).astype(jnp.bfloat16)
    grad_head_w = outer_sum(output_low, grad_logits)
    grad_head_b = jnp.sum(grad_logits.astype(jnp.float32), axis=0)
    grad_output = back_product(grad_logits, head_w)
    grad_output_low = grad_output.astype(jnp.bfloat16)
    grad_w_down = outer_sum(active_low, grad_output_low)
    grad_down_bias = jnp.sum(grad_output_low.astype(jnp.float32), axis=0)
    grad_active = back_product(grad_output_low, w_down)
    grad_up_low = up_pull(grad_active)[0].astype(jnp.bfloat16)
    grad_w_up = outer_sum(second_low, grad_up_low)
    grad_up_bias = jnp.sum(grad_up_low.astype(jnp.float32), axis=0)
    grad_second = back_product(grad_up_low, w_up)
    grad_resid_part, grad_gain_second, grad_shift_second = second_pull(grad_second)
    grad_resid = grad_output + grad_resid_part
    grad_branch_low = grad_resid.astype(jnp.bfloat16)
    grad_w_out = outer_sum(attended_low, grad_branch_low)
    grad_out_bias = jnp.sum(grad_branch_low.astype(jnp.float32), axis=0)
    grad_attended = back_product(grad_branch_low, w_out).astype(jnp.bfloat16)
    grad_heads = grad_attended.reshape(row_count, frames, head_count, head_width)
    head_dots = jnp.sum(grad_heads.astype(jnp.float32) * attended, axis=-1)
    zero_grads = jnp.zeros((row_count, frames, head_count, head_width), jnp.float32)
    all_keys, all_values = (
        lax.all_gather(keys, "seq", axis=1, tiled=True),
        lax.all_gather(values, "seq", axis=1, tiled=True),
    )
    length = all_keys.shape[1]
    key_span = 8 * frames

    def query_block(block_index, grad_query):
        first_row = block_index * key_span
        key_block = lax.dynamic_slice_in_dim(all_keys, first_row, key_span, 1)
        value_block = lax.dynamic_slice_in_dim(all_values, first_row, key_span, 1)
        seg_keys = lax.dynamic_slice_in_dim(segments, first_row, key_span, 1)
        results = []
        for row_index in range(row_count):
            action = partial(
                query_grad_row,
                query_row=queries[row_index],
                key_row=key_block[row_index].reshape(key_span, head_count, head_width),
                value_row=value_block[row_index].reshape(key_span, head_count, head_width),
                seg_query=seg_local[row_index],
                seg_key=seg_keys[row_index],
                lse_row=log_total[row_index],
                dots_row=head_dots[row_index],
                grad_row=grad_heads[row_index],
                score_scale=score_scale,
            )
            results.append(action(grad_query[row_index]))
        return jnp.stack(results)

    grad_queries = lax.fori_loop(0, length // key_span, query_block, zero_grads)

    def key_term(piece_rows):
        span = math.gcd(piece_rows, key_span)

        def key_one_span(span_index, gathered_terms):
            offset = span_index * span
            key_block = lax.dynamic_slice_in_dim(all_keys, offset, span, 1)
            value_block = lax.dynamic_slice_in_dim(all_values, offset, span, 1)
            seg_keys = lax.dynamic_slice_in_dim(segments, offset, span, 1)
            empty_row = jnp.zeros((span, head_count, head_width), jnp.float32)
            results = []
            for row_index in range(row_count):
                action = partial(
                    key_grad_row,
                    key_row=key_block[row_index].reshape(span, head_count, head_width),
                    value_row=value_block[row_index].reshape(span, head_count, head_width),
                    query_row=queries[row_index],
                    grad_row=grad_heads[row_index],
                    lse_row=log_total[row_index],
                    dots_row=head_dots[row_index],
                    seg_query=seg_local[row_index],
                    seg_key=seg_keys[row_index],
                    score_scale=score_scale,
                )
                results.append(action((empty_row, empty_row)))
            key_part = jnp.stack([item[0] for item in results], axis=1).reshape(
                span, row_count, features
            )
            value_part = jnp.stack([item[1] for item in results], axis=1).reshape(
                span, row_count, features
            )
            both_parts = jnp.concatenate([key_part, value_part], axis=2)
            return lax.dynamic_update_slice_in_dim(gathered_terms, both_parts, offset, 0)

        empty_terms = jnp.zeros((piece_rows, row_count, 2 * features), jnp.float32)
        return lax.fori_loop(0, piece_rows // span, key_one_span, empty_terms)

    both_grads = lax.psum_scatter(
        key_term(frames * lax.axis_size("seq")), "seq", scatter_dimension=0, tiled=True
    )
    grad_keys = jnp.transpose(both_grads[:, :, :features], (1, 0, 2)).reshape(
        row_count, frames, head_count, head_width
    )
    grad_values = jnp.transpose(both_grads[:, :, features:], (1, 0, 2)).reshape(
        row_count, frames, head_count, head_width
    )
    grad_mixed = jnp.concatenate(
        [
            grad_queries.reshape(tokens, features),
            grad_keys.reshape(tokens, features),
            grad_values.reshape(tokens, features),
        ],
        axis=1,
    ).astype(jnp.bfloat16)
    grad_w_qkv = outer_sum(normed_low, grad_mixed)
    mixed_sums = jnp.sum(grad_mixed.astype(jnp.float32), axis=0)
    grad_normed = back_product(grad_mixed, w_qkv).reshape(row_count, frames, features)
    grad_position_part, grad_gain_first, grad_shift_first = first_pull(grad_normed)
    grad_position = grad_resid.reshape(row_count, frames, features) + grad_position_part
    grad_conv_low = conv_pull(grad_position)[0].astype(jnp.bfloat16)
    grad_conv_bias = jnp.sum(grad_conv_low.astype(jnp.float32), axis=(0, 1))
    grad_conv_weight = conv_weight_grad(feats_rim, seg_padded, seg_local, grad_conv_low, tap_count)
    grad_rim = extended(grad_conv_low, (("seq", 1),), rim_width)
    grad_feats = grad_position + conv_input_grad(grad_rim, seg_padded, seg_local, conv_weight)
    grad_gains = jnp.stack([grad_gain_first, grad_gain_second], axis=1)
    grad_biases = jnp.stack(
        [
            grad_conv_bias,
            grad_shift_first,
            mixed_sums[:features],
            mixed_sums[2 * features :],
            grad_out_bias,
            grad_shift_second,
            grad_down_bias,
        ],
        axis=1,
    )
    shared = (
        lax.psum_scatter(grad_conv_weight, "seq", scatter_dimension=0, tiled=True),
        lax.psum_scatter(grad_w_qkv, "seq", scatter_dimension=0, tiled=True),
        lax.psum_scatter(grad_w_out, "seq", scatter_dimension=0, tiled=True),
        lax.psum_scatter(grad_w_up, "seq", scatter_dimension=0, tiled=True),
        lax.psum_scatter(grad_w_down, "seq", scatter_dimension=0, tiled=True),
        lax.psum_scatter(grad_head_w, "seq", scatter_dimension=0, tiled=True),
        lax.psum_scatter(grad_gains, "seq", scatter_dimension=0, tiled=True),
        lax.psum_scatter(grad_biases, "seq", scatter_dimension=0, tiled=True),
        lax.psum_scatter(grad_up_bias, "seq", scatter_dimension=0, tiled=True),
    )
    summed = (
        lax.psum(shared[0].astype(jnp.bfloat16), "dp").astype(jnp.float32),
        lax.psum(shared[1].astype(jnp.bfloat16), "dp").astype(jnp.float32),
        lax.psum(shared[2].astype(jnp.bfloat16), "dp").astype(jnp.float32),
        lax.psum(shared[3].astype(jnp.bfloat16), "dp").astype(jnp.float32),
        lax.psum(shared[4].astype(jnp.bfloat16), "dp").astype(jnp.float32),
        lax.psum(shared[5].astype(jnp.bfloat16), "dp").astype(jnp.float32),
        lax.psum(shared[6].astype(jnp.bfloat16), "dp").astype(jnp.float32),
        lax.psum(shared[7].astype(jnp.bfloat16), "dp").astype(jnp.float32),
        lax.psum(shared[8].astype(jnp.bfloat16), "dp").astype(jnp.float32),
    )
    loss_total, head_bias_total = lax.psum((local_loss, grad_head_b), ("dp", "seq"))
    loss = loss_total / (tokens * lax.axis_size("dp") * lax.axis_size("seq"))
    layer_out = output_low.reshape(row_count, frames, features)
    return (
        layer_out,
        loss,
        grad_feats,
        summed[0],
        summed[1],
        summed[2],
        summed[3],
        summed[4],
        summed[5],
        head_bias_total,
        summed[6],
        summed[7],
        summed[8],
    )


def solution(mesh):
    placed = (
        P("dp", "seq", None),
        P("dp", None),
        P("dp", "seq"),
        P(),
        P(),
        P(),
        P(),
        P(),
        P(),
        P(),
        P(),
        P(),
        P(),
    )
    return jax.shard_map(
        body,
        mesh=mesh,
        in_specs=placed,
        out_specs=(
            P("dp", "seq", None),
            P(),
            P("dp", "seq", None),
            P("seq", None),
            P("seq", None),
            P("seq", None),
            P("seq", None),
            P("seq", None),
            P("seq", None),
            P(),
            P("seq", None),
            P("seq", None),
            P("seq"),
        ),
        check_vma=False,
    )
```

profile of v0, /device:TPU:0, one launch (start us, length us, event | category | flops | bytes accessed | tf_op | source)
XLA Modules:
  0.0 2658.1 jit_solution(15346816068445463920)
XLA Ops:
  9.9 4.9 collective-permute-start
  19.1 43.1 %reshape.513 = bf16[128,64,16,64]{3,2,1,0:T(8,128)(2,1)} reshape(bf16[8192,1024]{1,0:T(8,128)(2,1)} %param.22) | data formatting | bytes 33554432 | tf_op jit(solution)/shard_map/reshape | solution.py:74
  65.1 222.0 %while.66 = (s32[]{:T(128)}, f32[2,128,16,64]{1,3,0,2:T(8,128)}, bf16[128,64,16,64]{3,2,1,0:T(8,128)(2,1)}, s32[2,256]{1,0:T(2,128)S(1)}, s32[2,128]{1,0:T(2,128...) while((s32[]{:T(128)}, f32[2,128,16,64]{1,3,0,2:T(8,128)}, ...), condition=%wide.region_1.2_spmd.clone, body=%wide.region_0.1_spmd.clone.sunk | while | flops 271058976 | bytes 40908548 | solution.py:86
  68.5 4.6 copy.343
  82.4 4.6 copy.343
  96.3 4.6 copy.343
  110.1 4.6 copy.343
  124.0 4.6 copy.343
  137.9 4.6 copy.343
  151.8 4.6 copy.343
  165.6 4.6 copy.343
  179.5 4.6 copy.343
  193.4 4.6 copy.343
  207.2 4.6 copy.343
  221.1 4.6 copy.343
  235.0 4.6 copy.343
  248.8 4.6 copy.343
  262.7 4.6 copy.343
  276.6 4.6 copy.343
  289.8 4.5 fusion.159
  298.5 4.8 fusion.91
  310.3 72.0 %all-gather.3.cloned.1.call-done = bf16[2,1024,1024]{2,1,0:T(8,128)(2,1)} async-done(((bf16[2,128,1024]{2,1,0:T(8,128)(2,1)}), bf16[2,1024,1024]{2,1,0:T(8,128)(2,1)}) %all-gather.3.cloned.1.call-update) | async-done | bytes 4194320 | tf_op jit(solution)/shard_map/all_gather | solution.py:250
  382.3 4.7 fusion.162
  390.9 65.8 %all-gather.5.cloned.1.call-done = bf16[2,1024,1024]{2,1,0:T(8,128)(2,1)} async-done(((bf16[2,128,1024]{2,1,0:T(8,128)(2,1)}), bf16[2,1024,1024]{2,1,0:T(8,128)(2,1)}) %all-gather.5.cloned.1.call-update) | async-done | bytes 4194320 | tf_op jit(solution)/shard_map/all_gather | solution.py:251
  456.7 4.7 fusion.161
  492.7 15.5 multiply_convert_fusion
  512.9 11.7 convert_reduce_fusion
  524.6 7.4 multiply_reduce_fusion
  547.5 7.4 fusion.70
  555.0 5.5 fusion.54
  564.0 5.4 copy.232
  569.5 5.4 copy.236
  574.8 7.4 fusion.68
  582.2 5.4 fusion.52
  591.3 5.3 copy.233
  596.6 5.4 copy.237
  602.1 11.6 maximum_maximum_fusion
  620.9 8.3 fusion.155
  630.4 9.7 fusion.135
  648.5 245.7 %reduce-scatter.12.cloned.1.call-done = f32[128,2,2048]{2,0,1:T(8,128)} async-done(((f32[1024,2,2048]{2,0,1:T(8,128)}), f32[128,2,2048]{2,0,1:T(8,128)}) %reduce-scatter.12.cloned.1.call-update) | async-done | bytes 2097168 | tf_op jit(solution)/shard_map/reduce_scatter | solution.py:392
  896.5 5.8 fusion.175
  911.7 7.5 fusion.153
  919.5 21.2 broadcast_in_dim.599.clone
  940.6 133.1 %while.65 = (s32[]{:T(128)}, f32[128,64,16,64]{3,2,1,0:T(8,128)}, s32[2,256]{1,0:T(2,128)S(1)}, s32[2,128]{1,0:T(2,128)S(1)}, bf16[2,256,1024]{1,2,0:T(8,128)(2,...) while((s32[]{:T(128)}, f32[128,64,16,64]{3,2,1,0:T(8,128)}, ...), condition=%wide.region_24.25_spmd, body=%wide.region_23.24_spmd.sunk | while | flops 270534688 | bytes 29898400 | solution.py:106
  944.6 4.4 copy_dynamic-update-slice_fusion.2
  952.9 4.4 copy_dynamic-update-slice_fusion.2
  961.3 4.5 copy_dynamic-update-slice_fusion.2
  986.2 4.4 copy_dynamic-update-slice_fusion.2
  994.5 4.5 copy_dynamic-update-slice_fusion.2
  1011.1 4.5 copy_dynamic-update-slice_fusion.2
  1027.8 4.4 copy_dynamic-update-slice_fusion.2
  1044.4 4.4 copy_dynamic-update-slice_fusion.2
  1061.0 4.4 copy_dynamic-update-slice_fusion.2
  1073.8 55.6 %reshape.525 = f32[8192,1024]{1,0:T(8,128)} reshape(f32[128,64,16,64]{3,2,1,0:T(8,128)} %get-tuple-element.609) | data formatting | bytes 67108864 | tf_op jit(solution)/shard_map/reshape | solution.py:107
  1136.4 56.3 %all-reduce.2 = (f32[]{:T(128)}, f32[32]{0:T(128)}) all-reduce(f32[]{:T(128)} %subtract_reduce_fusion, f32[32]{0:T(128)S(1)} %copy-done.98), channel_id=1, replica_groups=mesh['dp'=4,'seq'=8] {'dp','seq'}, use_global_device_ids=true, to_apply=%region_14.15 | all-reduce | flops 33 | bytes 264 | tf_op jit(solution)/shard_map/psum | solution.py:454
  1193.3 37.3 %all-reduce.1 = bf16[4096]{0:T(1024)(128)(2,1)S(1)} all-reduce(f32[4096]{0:T(1024)S(1)} %copy-done.84), channel_id=11, replica_groups=mesh['dp'=4,'seq'=8] {'seq'}, use_global_device_ids=true, to_apply=%region_52.53.clone | all-reduce | flops 4096 | bytes 24576
  1233.2 115.6 %reduce-scatter.20.cloned.1.call-done = f32[128,4096]{1,0:T(8,128)} async-done(((f32[1024,4096]{1,0:T(8,128)}), f32[128,4096]{1,0:T(8,128)}) %reduce-scatter.20.cloned.1.call-update) | async-done | bytes 2097168 | tf_op jit(solution)/shard_map/reduce_scatter | solution.py:436
  1351.5 283.4 %reduce-scatter.22.cloned.1.call-done = f32[512,1024]{1,0:T(8,128)} async-done(((f32[4096,1024]{1,0:T(8,128)}), f32[512,1024]{1,0:T(8,128)}) %reduce-scatter.22.cloned.1.call-update) | async-done | bytes 2097168 | tf_op jit(solution)/shard_map/reduce_scatter | solution.py:437
  1637.6 62.2 %reduce-scatter.28.cloned.1.call-done = f32[128,2]{1,0:T(8,128)} async-done(((f32[1024,2]{1,0:T(8,128)}), f32[128,2]{1,0:T(8,128)}) %reduce-scatter.28.cloned.1.call-update) | async-done | bytes 1040
  1700.7 55.1 %reduce-scatter.26.cloned.1.call-done = f32[128,7]{0,1:T(8,128)} async-done(((f32[1024,7]{0,1:T(8,128)}), f32[128,7]{0,1:T(8,128)}) %reduce-scatter.26.cloned.1.call-update) | async-done | bytes 3600 | tf_op jit(solution)/shard_map/reduce_scatter | solution.py:440
  1756.5 10.3 all-reduce.3
  1769.8 196.2 %reduce-scatter.16.cloned.1.call-done = f32[128,3072]{1,0:T(8,128)} async-done(((f32[1024,3072]{1,0:T(8,128)}), f32[128,3072]{1,0:T(8,128)}) %reduce-scatter.16.cloned.1.call-update) | async-done | bytes 1572880 | tf_op jit(solution)/shard_map/reduce_scatter | solution.py:434
  1968.4 544.2 %reduce-scatter.14.cloned.1.call-done = f32[1024,1024]{1,0:T(8,128)} async-done(((f32[8192,1024]{1,0:T(8,128)}), f32[1024,1024]{1,0:T(8,128)}) %reduce-scatter.14.cloned.1.call-update) | async-done | bytes 4194320 | tf_op jit(solution)/shard_map/reduce_scatter | solution.py:433
  2516.5 119.3 %while.67 = (s32[]{:T(128)}, f32[2,128,16,64]{1,3,0,2:T(8,128)}, bf16[128,64,16,64]{3,2,1,0:T(8,128)(2,1)}, s32[2,256]{1,0:T(2,128)S(1)}, s32[2,128]{1,0:T(2,128...) while((s32[]{:T(128)}, f32[2,128,16,64]{1,3,0,2:T(8,128)}, ...), condition=%wide.region_22.23_spmd.clone, body=%wide.region_21.22_spmd.clone.sunk | while | flops 271058976 | bytes 34617112 | solution.py:129
  (1075 shorter events, 509.9 us)
Async XLA Ops:
  7.2 484.4 %copy-start = (bf16[1024,1024]{1,0:T(8,128)(2,1)S(1)}, bf16[1024,1024]{1,0:T(8,128)(2,1)}, u32[]{:S(2)}) copy-start(bf16[1024,1024]{1,0:T(8,128)(2,1)} %param.24) | copy-start | bytes 6291460
  7.2 375.1 %all-gather.3.cloned.1.call-start = ((), (), s32[]{:S(2)}) async-start(), calls=%async_computation.9 | async-start | bytes 4718592 | tf_op jit(solution)/shard_map/all_gather | solution.py:250
  8.7 53.6 %copy-start.19 = (bf16[2,128,1024]{1,2,0:T(8,128)(2,1)}, bf16[2,128,1024]{1,2,0:T(8,128)(2,1)S(1)}, u32[]{:S(2)}) copy-start(bf16[2,128,1024]{1,2,0:T(8,128)(2,1)S(1)} %copy.206) | copy-start | bytes 1572868
  9.9 52.4 %collective-permute-start = (bf16[2,64,1024]{1,2,0:T(8,128)(2,1)}, bf16[2,64,1024]{1,2,0:T(8,128)(2,1)S(1)}, u32[]{:S(2)}, u32[]{:S(2)}) collective-permute-start(bf16[2,64,1024]{1,2,0:T(8,128)(2,1)} %get-tuple-element.889), channel_id=1, source_target_pairs={{0,1},{1,2},{2,3},{3,4},{4,5},{5,6},{6,7},{8,9},{9,10},{10,11},{11... | collective-permute-start | bytes 786440 | tf_op jit(solution)/shard_map/ppermute | solution.py:28
  14.7 48.4 %collective-permute-start.1 = (bf16[2,64,1024]{1,2,0:T(8,128)(2,1)}, bf16[2,64,1024]{1,2,0:T(8,128)(2,1)}, u32[]{:S(2)}, u32[]{:S(2)}) collective-permute-start(bf16[2,64,1024]{1,2,0:T(8,128)(2,1)} %get-tuple-element.890), channel_id=1, source_target_pairs={{1,0},{2,1},{3,2},{4,3},{5,4},{6,5},{7,6},{9,8},{10,9},{11,10},{12... | collective-permute-start | bytes 786440 | tf_op jit(solution)/shard_map/ppermute | solution.py:30
  17.7 271.1 %copy-start.72 = (f32[1024,1]{0,1:T(1,128)}, f32[1024,1]{0,1:T(1,128)S(1)}, u32[]{:S(2)}) copy-start(f32[1024,1]{0,1:T(1,128)S(1)} %get-tuple-element.896) | copy-start | bytes 12292
  19.1 43.2 %copy-start.91 = (f32[1024,2]{0,1:T(2,128)S(1)}, f32[1024,2]{0,1:T(2,128)}, u32[]{:S(2)}) copy-start(f32[1024,2]{0,1:T(2,128)} %param.29) | copy-start | bytes 24580
  62.3 232.1 %copy-start.69 = (f32[1024,1]{0,1:T(1,128)}, f32[1024,1]{0,1:T(1,128)S(1)}, u32[]{:S(2)}) copy-start(f32[1024,1]{0,1:T(1,128)S(1)} %get-tuple-element.913) | copy-start | bytes 12292
  287.1 9.3 copy-start.2
  287.1 9.3 copy-start.25
  287.1 19.4 copy-start.63
  294.4 8.9 copy-start.87
  294.4 8.9 copy-start.78
  298.5 8.1 copy-start.71
  298.5 9.1 copy-start.8
  305.5 151.2 %all-gather.5.cloned.1.call-start = ((), (), s32[]{:S(2)}) async-start(), calls=%async_computation.10 | async-start | bytes 4718592 | tf_op jit(solution)/shard_map/all_gather | solution.py:251
  306.3 587.9 %reduce-scatter.12.cloned.1.call-start = ((), (), s32[]{:S(2)}) async-start(), calls=%async_computation.11 | async-start | bytes 18874368 | tf_op jit(solution)/shard_map/reduce_scatter | solution.py:392
  310.1 168.5 %copy-start.38 = (bf16[128,1024]{0,1:T(8,128)(2,1)}, bf16[128,1024]{0,1:T(8,128)(2,1)S(1)}, u32[]{:S(2)}) copy-start(bf16[128,1024]{0,1:T(8,128)(2,1)S(1)} %copy.215) | copy-start | bytes 786436
  476.6 7.3 copy-start.4
  481.6 5.5 copy-start.5
  491.6 16.7 slice-start
  492.7 15.6 copy-start.93
  492.7 15.6 slice-start.1
  512.7 19.7 copy-start.22
  524.6 7.4 copy-start.51
  547.5 7.4 copy-start.41
  547.5 7.4 copy-start.46
  547.5 7.4 copy-start.57
  547.5 7.4 copy-start.75
  554.9 5.5 copy-start.39
  574.8 7.4 copy-start.44
  574.8 7.4 copy-start.56
  574.8 7.4 copy-start.74
  574.8 7.4 copy-start.92
  613.8 616.9 %reduce-scatter.24.cloned.1.call-start = ((), (), s32[]{:S(2)}) async-start(), calls=%async_computation.17 | async-start | bytes 147456 | tf_op jit(solution)/shard_map/reduce_scatter | solution.py:438
  615.6 615.7 %reduce-scatter.18.cloned.1.call-start = ((), (), s32[]{:S(2)}) async-start(), calls=%async_computation.14 | async-start | bytes 4718592 | tf_op jit(solution)/shard_map/reduce_scatter | solution.py:435
  618.9 729.9 %reduce-scatter.20.cloned.1.call-start = ((), (), s32[]{:S(2)}) async-start(), calls=%async_computation.15 | async-start | bytes 18874368 | tf_op jit(solution)/shard_map/reduce_scatter | solution.py:436
  629.2 1005.7 %reduce-scatter.22.cloned.1.call-start = ((), (), s32[]{:S(2)}) async-start(), calls=%async_computation.16 | async-start | bytes 18874368 | tf_op jit(solution)/shard_map/reduce_scatter | solution.py:437
  640.2 1059.6 %reduce-scatter.28.cloned.1.call-start = ((), (), s32[]{:S(2)}) async-start(), calls=%async_computation.19 | async-start | bytes 589824
  648.5 257.0 %copy-start.27 = (bf16[128,8,2,128]{3,1,2,0:T(8,128)(2,1)}, bf16[128,8,2,128]{3,1,2,0:T(8,128)(2,1)S(1)}, u32[]{:S(2)}) copy-start(bf16[128,8,2,128]{3,1,2,0:T(8,128)(2,1)S(1)} %copy.333) | copy-start | bytes 1572868
  896.2 9.2 copy-start.29
  896.5 5.9 copy-start.31
  896.5 7.4 copy-start.9
  896.5 7.4 copy-start.70
  896.5 7.4 copy-start.77
  896.5 7.4 copy-start.79
  907.3 11.8 copy-start.20
  907.4 848.3 %reduce-scatter.26.cloned.1.call-start = ((), (), s32[]{:S(2)}) async-start(), calls=%async_computation.18 | async-start | bytes 36864 | tf_op jit(solution)/shard_map/reduce_scatter | solution.py:440
  911.6 1054.4 %reduce-scatter.16.cloned.1.call-start = ((), (), s32[]{:S(2)}) async-start(), calls=%async_computation.13 | async-start | bytes 14155776 | tf_op jit(solution)/shard_map/reduce_scatter | solution.py:434
  919.2 21.4 copy-start.3
  919.2 21.4 copy-start.26
  919.2 21.4 copy-start.64
  919.2 1593.4 %reduce-scatter.14.cloned.1.call-start = ((), (), s32[]{:S(2)}) async-start(), calls=%async_computation.12 | async-start | bytes 37748736 | tf_op jit(solution)/shard_map/reduce_scatter | solution.py:433
  1129.3 6.4 copy-start.83
  1129.3 6.4 copy-start.86
  1129.3 6.4 copy-start.95
  1129.3 7.0 copy-start.98
  1129.4 64.0 %copy-start.84 = (f32[4096]{0:T(1024)S(1)}, f32[4096]{0:T(1024)}, u32[]{:S(2)}) copy-start(f32[4096]{0:T(1024)} %get-tuple-element.930) | copy-start | bytes 49156
  1129.4 1510.5 %all-reduce.7.cloned.1.call-start = ((), (), s32[]{:S(2)}) async-start(), calls=%async_computation.20 | async-start | bytes 10485760 | tf_op jit(solution)/shard_map/psum | solution.py:444
  1129.7 639.5 %collective-permute-start.2 = (bf16[2,64,1024]{1,2,0:T(8,128)(2,1)S(1)}, bf16[2,64,1024]{1,2,0:T(8,128)(2,1)S(1)}, u32[]{:S(2)}, u32[]{:S(2)}) collective-permute-start(bf16[2,64,1024]{1,2,0:T(8,128)(2,1)S(1)} %get-tuple-element.885), channel_id=1, source_target_pairs={{0,1},{1,2},{2,3},{3,4},{4,5},{5,6},{6,7},{8,9},{9,10},{10,11},{11... | collective-permute-start | bytes 786440 | tf_op jit(solution)/shard_map/ppermute | solution.py:28
  1133.1 636.0 %collective-permute-start.3 = (bf16[2,64,1024]{1,2,0:T(8,128)(2,1)S(1)}, bf16[2,64,1024]{1,2,0:T(8,128)(2,1)S(1)}, u32[]{:S(2)}, u32[]{:S(2)}) collective-permute-start(bf16[2,64,1024]{1,2,0:T(8,128)(2,1)S(1)} %get-tuple-element.886), channel_id=1, source_target_pairs={{1,0},{2,1},{3,2},{4,3},{5,4},{6,5},{7,6},{9,8},{10,9},{11,10},{12... | collective-permute-start | bytes 786440 | tf_op jit(solution)/shard_map/ppermute | solution.py:30
  2516.5 120.6 %copy-start.21 = (f32[2,128,1024]{1,2,0:T(8,128)S(1)}, f32[2,128,1024]{1,2,0:T(8,128)}, u32[]{:S(2)}) copy-start(f32[2,128,1024]{1,2,0:T(8,128)} %copy-done.20) | copy-start | bytes 3145732
  2516.5 120.6 %copy-start.90 = (f32[2,128]{1,0:T(2,128)S(1)}, f32[2,128]{1,0:T(2,128)}, u32[]{:S(2)}) copy-start(f32[2,128]{1,0:T(2,128)} %copy-done.89) | copy-start | bytes 3076
  2644.3 5.6 copy-start.1
  (131 other events, 240.4 us)
Sparse Core Ops, SparseCore 0:
  305.7 76.5 all-gather.2
  385.0 71.6 all-gather.4
  613.9 280.2 reduce-scatter.11
  897.7 60.2 reduce-scatter.23
  962.5 86.9 reduce-scatter.17
  1053.1 295.6 reduce-scatter.19
  1353.0 281.7 reduce-scatter.21
  1638.8 61.0 reduce-scatter.27
  1703.3 52.4 reduce-scatter.25
  1759.6 206.3 reduce-scatter.15
  1970.2 542.3 reduce-scatter.13
  2516.6 102.3 all-reduce.6
where the time goes:
time: 2670 us; the launch traced here: 2660 us
  waiting for transfers between devices  1640 us (61%)
  local copies, waits for them, and re-layouts  531 us (20%)
  matrix products  181 us (7%)
  other arithmetic  167 us (6%)
  blocking collectives  104 us (4%)
    reduce_scatter x1, waiting for transfers between devices, body(): lax.psum_scatter(grad_conv_weight, 'seq', scatter_dimension=0, tiled=True)  544 us
    reduce_scatter x1, waiting for transfers between devices, body(): lax.psum_scatter(grad_w_down, 'seq', scatter_dimension=0, tiled=True)  283 us
    reduce_scatter x1, waiting for transfers between devices, body(): lax.psum_scatter(key_term(frames * lax.axis_size('seq')), 'seq', scatter_...  246 us
    reduce_scatter x1, waiting for transfers between devices, body(): lax.psum_scatter(grad_w_qkv, 'seq', scatter_dimension=0, tiled=True)  196 us
    dynamic_slice x48, local copies, waits for them, and re-layouts, one_block(): lax.dynamic_slice_in_dim(grouped, tap_block * tap_group, tap_group, 0)  158 us
    reduce_scatter x1, waiting for transfers between devices, body(): lax.psum_scatter(grad_w_up, 'seq', scatter_dimension=0, tiled=True)  116 us
    select_n x48, other arithmetic, masked_windows(): windows.append(jnp.where(keep_mask, window, jnp.zeros_like(window)))  95.2 us
    while x496, local copies, waits for them, and re-layouts  83.4 us
  transfers between devices with their start and end apart: 16, of which 9 were waited for; matrix products, arithmetic and copies ran while one was open for 16% of the time, Pallas kernels for 0%

commit v1 on v0

--- a/solution.py
+++ b/solution.py
@@ -4,12 +4,16 @@
 import jax
 import jax.numpy as jnp
 from jax import lax
-from jax.sharding import PartitionSpec as P
+from jax.experimental import pallas as pl
+from jax.experimental.pallas import tpu as pltpu
+from jax.sharding import Mesh, PartitionSpec as P
 
 HEADS = 16
 GROUPS = 16
 KERNEL = 128
 VOCAB = 32
+TAP_BLOCKS = 33
+VMEM_LIMIT = 56 * 1024 * 1024
 
 
 epsilon = 1e-05
@@ -471,7 +475,7 @@
     )
 
 
-def solution(mesh):
+def whole_solution(mesh):
     placed = (
         P("dp", "seq", None),
         P("dp", None),
@@ -508,3 +512,707 @@
         ),
         check_vma=False,
     )
+
+
+def tile_lists(seg_ext, rise):
+    row_count = seg_ext.shape[0]
+    frames = seg_ext.shape[1] - KERNEL
+    tiles = frames // 64
+    center = seg_ext[:, KERNEL // 2 : KERNEL // 2 + frames].reshape(row_count, tiles, 64)
+    first = center[:, :, 0].reshape(-1)
+    counts = (center[:, :, 63].reshape(-1) - first + 1).astype(jnp.int32)
+    ends = jnp.cumsum(counts)
+    slots = row_count * (tiles + rise)
+    slot = jnp.arange(slots, dtype=jnp.int32)
+    tile = jnp.sum((slot[:, None] >= ends[None, :]).astype(jnp.int32), axis=1)
+    used = tile < row_count * tiles
+    tile = jnp.minimum(tile, row_count * tiles - 1)
+    onehot = tile[:, None] == jnp.arange(row_count * tiles, dtype=jnp.int32)[None, :]
+    begin = jnp.sum(jnp.where(onehot, (ends - counts)[None, :], 0), axis=1)
+    number = jnp.sum(jnp.where(onehot, first[None, :], 0), axis=1) + slot - begin
+    number = jnp.where(used, number, -2)
+    in_block = tile + (tile // tiles) * (KERNEL // 64)
+    return in_block.astype(jnp.int32), tile.astype(jnp.int32), number.astype(jnp.int32)
+
+
+def lane_low(rows):
+    return lax.broadcasted_iota(jnp.int32, (rows, 128), 1) < 64
+
+
+def half_roll(block):
+    return pltpu.roll(block, 64, 1)
+
+
+def quad_rows(src, rows, side):
+    low = lane_low(rows)
+    parts = [src[pl.ds(j, rows, stride=4), :] for j in range(4)]
+    halves = []
+    for a, b in ((0, 1), (2, 3)):
+        if side == 0:
+            halves.append(jnp.where(low, parts[a], half_roll(parts[b])))
+        else:
+            halves.append(jnp.where(low, half_roll(parts[a]), parts[b]))
+    return halves
+
+
+def conv_setup(meta, slots, seg_ref, flat, shifts, masks):
+    rows4 = seg_ref.shape[0]
+    blocks = rows4 // 16
+    flat[0:rows4, :] = seg_ref[...]
+    flat[rows4:, :] = jnp.zeros((16, 256), jnp.float32)
+    for p in range(16):
+        shifts[p] = flat[pl.ds(p, rows4), :].astype(jnp.bfloat16).reshape(blocks, 16, 256)
+
+    @pl.loop(0, slots)
+    def _(v):
+        at = meta[1 + v]
+        number = meta[1 + 2 * slots + v].astype(jnp.float32)
+        row = pl.multiple_of(v * 16, 16)
+        for b in range(TAP_BLOCKS):
+            ids = shifts[b % 16, at + b // 16].astype(jnp.float32)
+            masks[pl.ds(row, 16), b * 256 : (b + 1) * 256] = jnp.where(ids == number, 1.0, 0.0).astype(jnp.bfloat16)
+
+
+def conv_patches(meta, slots, wide, side, flat, shifts, masks, patches):
+    rows4 = shifts.shape[1] * 16
+    halves = quad_rows(wide, rows4, side)
+    flat[0:rows4, 0:128] = halves[0]
+    flat[0:rows4, 128:256] = halves[1]
+    for p in range(16):
+        shifts[p] = flat[pl.ds(p, rows4), :].astype(jnp.bfloat16).reshape(rows4 // 16, 16, 256)
+
+    @pl.loop(0, slots)
+    def _(v):
+        at = meta[1 + v]
+        row = pl.multiple_of(v * 16, 16)
+        for b in range(TAP_BLOCKS):
+            span = slice(b * 256, (b + 1) * 256)
+            patches[pl.ds(row, 16), span] = shifts[b % 16, at + b // 16] * masks[pl.ds(row, 16), span]
+
+
+def conv_taps(w_ref, taps):
+    low = lane_low(64)
+    zero = jnp.zeros((64, 128), jnp.bfloat16)
+    count = w_ref.shape[0] // 64
+    for side in range(2):
+        taps[side, 0:128, :] = jnp.zeros((128, 128), jnp.bfloat16)
+        taps[side, 128 + w_ref.shape[0] + 64 :, :] = jnp.zeros(
+            (taps.shape[1] - 192 - w_ref.shape[0], 128), jnp.bfloat16
+        )
+    first = w_ref[0:64, :]
+    taps[0, 128:192, :] = jnp.where(low, first, zero)
+    taps[1, 128:192, :] = jnp.where(low, half_roll(first), zero)
+    last = w_ref[(count - 1) * 64 :, :]
+    taps[0, 128 + count * 64 : 192 + count * 64, :] = jnp.where(low, zero, half_roll(last))
+    taps[1, 128 + count * 64 : 192 + count * 64, :] = jnp.where(low, zero, last)
+
+    @pl.loop(1, count, unroll=4)
+    def _(k):
+        here = w_ref[pl.ds(pl.multiple_of(k * 64, 64), 64), :]
+        before = w_ref[pl.ds(pl.multiple_of((k - 1) * 64, 64), 64), :]
+        to = pl.ds(pl.multiple_of(128 + k * 64, 64), 64)
+        taps[0, to, :] = jnp.where(low, here, half_roll(before))
+        taps[1, to, :] = jnp.where(low, half_roll(here), before)
+
+
+def conv_kernel(slots, backward, meta, x_ref, seg_ref, w_ref, o_ref, wide, flat, shifts, masks, patches, taps, sums, outs):
+    @pl.when(pl.program_id(0) == 0)
+    def _():
+        conv_setup(meta, slots, seg_ref, flat, shifts, masks)
+
+    wide[...] = x_ref[...].astype(jnp.float32)
+    conv_taps(w_ref, taps)
+    out_rows = o_ref.shape[0] // 4
+    for side in range(2):
+        conv_patches(meta, slots, wide, side, flat, shifts, masks, patches)
+        total = jnp.zeros((slots * 16, 256), jnp.float32)
+        for b in range(TAP_BLOCKS):
+            weight = jnp.concatenate(
+                [taps[side, 128 + b * 256 : 384 + b * 256, :], taps[side, b * 256 : 256 + b * 256, :]], axis=1
+            )
+            if backward:
+                c = TAP_BLOCKS - 1 - b
+                total = total + lax.dot_general(
+                    patches[:, c * 256 : (c + 1) * 256], weight, (((1,), (1,)), ((), ())),
+                    preferred_element_type=jnp.float32,
+                )
+            else:
+                total = total + jnp.dot(
+                    patches[:, b * 256 : (b + 1) * 256], weight, preferred_element_type=jnp.float32
+                )
+        sums[...] = total
+
+        @pl.loop(0, slots)
+        def _(v):
+            to = pl.ds(pl.multiple_of(meta[1 + slots + v] * 16, 16), 16)
+            row = pl.ds(pl.multiple_of(v * 16, 16), 16)
+            keep = masks[row, 16 * 256 : 17 * 256].astype(jnp.float32) > 0.5
+            outs[side, to, :] = jnp.where(keep, sums[row, :], outs[side, to, :])
+
+    low = lane_low(out_rows)
+    for half in range(2):
+        zero_side = outs[0, :, half * 128 : (half + 1) * 128]
+        one_side = outs[1, :, half * 128 : (half + 1) * 128]
+        o_ref[pl.ds(2 * half, out_rows, stride=4), :] = jnp.where(low, zero_side, half_roll(one_side))
+        o_ref[pl.ds(2 * half + 1, out_rows, stride=4), :] = jnp.where(low, half_roll(zero_side), one_side)
+
+
+def seg_quads(seg_ext):
+    quads = seg_ext.astype(jnp.float32).reshape(-1, 4)
+    return jnp.repeat(quads, 64, axis=1)
+
+
+def grouped_conv(x_ext, seg_ext, weight, first_pair, rise, backward):
+    row_count, length, width = x_ext.shape
+    frames = length - KERNEL
+    pairs = width // 128
+    in_block, tile, number = tile_lists(seg_ext, rise)
+    slots = in_block.shape[0]
+    meta = jnp.concatenate([jnp.reshape(first_pair, (1,)).astype(jnp.int32), in_block, tile, number])
+    rows4 = row_count * length // 4
+    out4 = row_count * frames // 4
+    depth = TAP_BLOCKS * 256
+    return pl.pallas_call(
+        partial(conv_kernel, slots, backward),
+        grid_spec=pltpu.PrefetchScalarGridSpec(
+            num_scalar_prefetch=1,
+            grid=(pairs,),
+            in_specs=[
+                pl.BlockSpec((row_count * length, 128), lambda p, meta: (0, p)),
+                pl.BlockSpec((rows4, 256), lambda p, meta: (0, 0)),
+                pl.BlockSpec((weight.shape[0], 128), lambda p, meta: (0, meta[0] + p)),
+            ],
+            out_specs=pl.BlockSpec((row_count * frames, 128), lambda p, meta: (0, p)),
+            scratch_shapes=[
+                pltpu.VMEM((row_count * length, 128), jnp.float32),
+                pltpu.VMEM((rows4 + 16, 256), jnp.float32),
+                pltpu.VMEM((16, rows4 // 16, 16, 256), jnp.bfloat16),
+                pltpu.VMEM((slots * 16, depth), jnp.bfloat16),
+                pltpu.VMEM((slots * 16, depth), jnp.bfloat16),
+                pltpu.VMEM((2, 128 + depth, 128), jnp.bfloat16),
+                pltpu.VMEM((slots * 16, 256), jnp.float32),
+                pltpu.VMEM((2, out4, 256), jnp.float32),
+            ],
+        ),
+        out_shape=jax.ShapeDtypeStruct((row_count * frames, width), jnp.float32),
+        compiler_params=pltpu.CompilerParams(vmem_limit_bytes=VMEM_LIMIT, dimension_semantics=("arbitrary",)),
+        cost_estimate=pl.CostEstimate(
+            flops=2 * pairs * 2 * slots * 16 * 256 * depth, bytes_accessed=pairs * weight.shape[0] * 256, transcendentals=0
+        ),
+        name="conv_back" if backward else "conv_forth",
+    )(meta, x_ext.reshape(row_count * length, width), seg_quads(seg_ext), weight)
+
+
+def conv_weight_kernel(slots, meta, x_ref, seg_ref, g_ref, o_ref, wide, wide_g, flat, shifts, masks, patches, quads, picks, sums):
+    @pl.when(pl.program_id(0) == 0)
+    def _():
+        conv_setup(meta, slots, seg_ref, flat, shifts, masks)
+
+    wide[...] = x_ref[...].astype(jnp.float32)
+    wide_g[...] = g_ref[...].astype(jnp.float32)
+    out_rows = g_ref.shape[0] // 4
+    low = lane_low(64)
+    for side in range(2):
+        conv_patches(meta, slots, wide, side, flat, shifts, masks, patches)
+        halves = quad_rows(wide_g, out_rows, side)
+        quads[:, 0:128] = halves[0].astype(jnp.bfloat16)
+        quads[:, 128:256] = halves[1].astype(jnp.bfloat16)
+
+        @pl.loop(0, slots)
+        def _(v):
+            at = pl.ds(pl.multiple_of(meta[1 + slots + v] * 16, 16), 16)
+            row = pl.ds(pl.multiple_of(v * 16, 16), 16)
+            picks[row, :] = quads[at, :] * masks[row, 16 * 256 : 17 * 256]
+
+        for b in range(TAP_BLOCKS):
+            sums[:, b * 256 : (b + 1) * 256] = lax.dot_general(
+                picks[...], patches[:, b * 256 : (b + 1) * 256], (((0,), (0,)), ((), ())),
+                preferred_element_type=jnp.float32,
+            )
+
+        def piece(j, q):
+            return sums[j * 64 : (j + 1) * 64, q * 128 : (q + 1) * 128]
+
+        def odd(q):
+            return half_roll(piece(1, q) + piece(3, q + 1))
+
+        left = odd(0)
+        for q in range(2 * (TAP_BLOCKS - 1)):
+            right = odd(q + 1)
+            part = piece(0, q) + piece(2, q + 1) + jnp.where(low, left, right)
+            o_ref[side * 64 : (side + 1) * 64, q * 128 : (q + 1) * 128] = part.astype(o_ref.dtype)
+            left = right
+
+
+def grouped_conv_weight(x_ext, seg_ext, grad, rise):
+    row_count, length, width = x_ext.shape
+    frames = length - KERNEL
+    pairs = width // 128
+    in_block, tile, number = tile_lists(seg_ext, rise)
+    slots = in_block.shape[0]
+    meta = jnp.concatenate([jnp.zeros((1,), jnp.int32), in_block, tile, number])
+    rows4 = row_count * length // 4
+    out4 = row_count * frames // 4
+    depth = TAP_BLOCKS * 256
+    return pl.pallas_call(
+        partial(conv_weight_kernel, slots),
+        grid_spec=pltpu.PrefetchScalarGridSpec(
+            num_scalar_prefetch=1,
+            grid=(pairs,),
+            in_specs=[
+                pl.BlockSpec((row_count * length, 128), lambda p, meta: (0, p)),
+                pl.BlockSpec((rows4, 256), lambda p, meta: (0, 0)),
+                pl.BlockSpec((row_count * frames, 128), lambda p, meta: (0, p)),
+            ],
+            out_specs=pl.BlockSpec((128, KERNEL * 64), lambda p, meta: (p, 0)),
+            scratch_shapes=[
+                pltpu.VMEM((row_count * length, 128), jnp.float32),
+                pltpu.VMEM((row_count * frames, 128), jnp.float32),
+                pltpu.VMEM((rows4 + 16, 256), jnp.float32),
+                pltpu.VMEM((16, rows4 // 16, 16, 256), jnp.bfloat16),
+                pltpu.VMEM((slots * 16, depth), jnp.bfloat16),
+                pltpu.VMEM((slots * 16, depth), jnp.bfloat16),
+                pltpu.VMEM((out4, 256), jnp.bfloat16),
+                pltpu.VMEM((slots * 16, 256), jnp.bfloat16),
+                pltpu.VMEM((256, depth), jnp.float32),
+            ],
+        ),
+        out_shape=jax.ShapeDtypeStruct((width, KERNEL * 64), jnp.bfloat16),
+        compiler_params=pltpu.CompilerParams(vmem_limit_bytes=VMEM_LIMIT, dimension_semantics=("arbitrary",)),
+        cost_estimate=pl.CostEstimate(
+            flops=2 * pairs * 2 * slots * 16 * 256 * depth, bytes_accessed=width * KERNEL * 128, transcendentals=0
+        ),
+        name="conv_weight_grad",
+    )(meta, x_ext.reshape(row_count * length, width), seg_quads(seg_ext), grad)
+
+
+def lanes_dot(a, b):
+    return lax.dot_general(a, b, (((1,), (1,)), ((), ())), preferred_element_type=jnp.float32)
+
+
+def rows_dot(a, b):
+    return lax.dot_general(a, b, (((0,), (0,)), ((), ())), preferred_element_type=jnp.float32)
+
+
+def attend_kernel(seg_q_ref, seg_k_ref, q_ref, k_ref, v_ref, out_ref, lse_ref):
+    queries = q_ref[...] * jnp.bfloat16(0.125)
+    key_count, query_count = k_ref.shape[0], q_ref.shape[0]
+    low = lax.broadcasted_iota(jnp.int32, (key_count, 128), 1) < 64
+    keys, values = k_ref[...], v_ref[...]
+    allowed = seg_k_ref[...] == seg_q_ref[...]
+    pieces = []
+    for side in range(2):
+        mine = low if side == 0 else jnp.logical_not(low)
+        scores = lanes_dot(jnp.where(mine, keys, jnp.zeros_like(keys)), queries)
+        scores = jnp.where(allowed, scores, masked_score)
+        top = jnp.max(scores, axis=0, keepdims=True)
+        weights = jnp.exp(scores - top)
+        total = jnp.sum(weights, axis=0, keepdims=True)
+        mixed = rows_dot(values, weights.astype(jnp.bfloat16))
+        pieces.append(mixed[side * 64 : (side + 1) * 64, :] / total)
+        lse_ref[0, side : side + 1, :] = top + jnp.log(total)
+    out_ref[...] = jnp.concatenate(pieces, axis=0).T
+
+
+def attend_heads(queries, keys, values, seg_q, seg_k):
+    frames, width = queries.shape
+    length = keys.shape[0]
+    pairs = width // 128
+    return pl.pallas_call(
+        attend_kernel,
+        grid=(pairs,),
+        in_specs=[
+            pl.BlockSpec((1, frames), lambda p: (0, 0)),
+            pl.BlockSpec((length, 1), lambda p: (0, 0)),
+            pl.BlockSpec((frames, 128), lambda p: (0, p)),
+            pl.BlockSpec((length, 128), lambda p: (0, p)),
+            pl.BlockSpec((length, 128), lambda p: (0, p)),
+        ],
+        out_specs=[
+            pl.BlockSpec((frames, 128), lambda p: (0, p)),
+            pl.BlockSpec((1, 8, frames), lambda p: (p, 0, 0)),
+        ],
+        out_shape=[
+            jax.ShapeDtypeStruct((frames, width), jnp.float32),
+            jax.ShapeDtypeStruct((pairs, 8, frames), jnp.float32),
+        ],
+        compiler_params=pltpu.CompilerParams(vmem_limit_bytes=VMEM_LIMIT),
+        cost_estimate=pl.CostEstimate(
+            flops=8 * pairs * frames * length * 128, bytes_accessed=8 * frames * width, transcendentals=2 * pairs * frames * length
+        ),
+        name="attend",
+    )(seg_q.reshape(1, -1), seg_k.reshape(-1, 1), queries, keys, values)
+
+
+def attend_back_kernel(seg_q_ref, seg_k_ref, q_ref, k_ref, v_ref, g_ref, a_ref, lse_ref, dq_ref, dk_ref, dv_ref):
+    queries = q_ref[...] * jnp.bfloat16(0.125)
+    key_count = k_ref.shape[0]
+    low = lax.broadcasted_iota(jnp.int32, (key_count, 128), 1) < 64
+    keys, values, grads = k_ref[...], v_ref[...], g_ref[...]
+    allowed = seg_k_ref[...] == seg_q_ref[...]
+    products = (grads.astype(jnp.float32) * a_ref[...]).T
+    dq, dk, dv = [], [], []
+    for side in range(2):
+        mine = low if side == 0 else jnp.logical_not(low)
+        zero = jnp.zeros_like(keys)
+        scores = lanes_dot(jnp.where(mine, keys, zero), queries)
+        probs = jnp.where(allowed, jnp.exp(scores - lse_ref[0, side : side + 1, :]), 0.0)
+        dots = jnp.sum(products[side * 64 : (side + 1) * 64, :], axis=0, keepdims=True)
+        dv.append(jnp.dot(probs.astype(jnp.bfloat16), grads, preferred_element_type=jnp.float32))
+        grad_probs = lanes_dot(jnp.where(mine, values, zero), grads)
+        grad_scores = (probs * (grad_probs - dots)).astype(jnp.bfloat16)
+        dk.append(jnp.dot(grad_scores, queries, preferred_element_type=jnp.float32))
+        dq.append(rows_dot(keys, grad_scores)[side * 64 : (side + 1) * 64, :])
+    dq_ref[...] = 0.125 * jnp.concatenate(dq, axis=0).T
+    dk_ref[...] = jnp.where(low, dk[0], dk[1]).astype(dk_ref.dtype)
+    dv_ref[...] = jnp.where(low, dv[0], dv[1]).astype(dv_ref.dtype)
+
+
+def attend_heads_back(queries, keys, values, grads, attended, lse, seg_q, seg_k, kind):
+    frames, width = queries.shape
+    length = keys.shape[0]
+    pairs = width // 128
+    return pl.pallas_call(
+        attend_back_kernel,
+        grid=(pairs,),
+        in_specs=[
+            pl.BlockSpec((1, frames), lambda p: (0, 0)),
+            pl.BlockSpec((length, 1), lambda p: (0, 0)),
+            pl.BlockSpec((frames, 128), lambda p: (0, p)),
+            pl.BlockSpec((length, 128), lambda p: (0, p)),
+            pl.BlockSpec((length, 128), lambda p: (0, p)),
+            pl.BlockSpec((frames, 128), lambda p: (0, p)),
+            pl.BlockSpec((frames, 128), lambda p: (0, p)),
+            pl.BlockSpec((1, 8, frames), lambda p: (p, 0, 0)),
+        ],
+        out_specs=[
+            pl.BlockSpec((frames, 128), lambda p: (0, p)),
+            pl.BlockSpec((length, 128), lambda p: (0, p)),
+            pl.BlockSpec((length, 128), lambda p: (0, p)),
+        ],
+        out_shape=[
+            jax.ShapeDtypeStruct((frames, width), jnp.float32),
+            jax.ShapeDtypeStruct((length, width), kind),
+            jax.ShapeDtypeStruct((length, width), kind),
+        ],
+        compiler_params=pltpu.CompilerParams(vmem_limit_bytes=VMEM_LIMIT),
+        cost_estimate=pl.CostEstimate(
+            flops=20 * pairs * frames * length * 128, bytes_accessed=16 * frames * width, transcendentals=2 * pairs * frames * length
+        ),
+        name="attend_back",
+    )(seg_q.reshape(1, -1), seg_k.reshape(-1, 1), queries, keys, values, grads, attended, lse)
+
+
+AXES = ("y", "c", "z", "x")
+
+
+def device_pairs(place):
+    pairs = []
+    for y in range(2):
+        for c in range(2):
+            for z in range(4):
+                for x in range(2):
+                    ty, tc, tz, tx = place(y, c, z, x)
+                    pairs.append((((y * 2 + c) * 4 + z) * 2 + x, ((ty * 2 + tc) * 4 + tz) * 2 + tx))
+    return pairs
+
+
+def move(values, place):
+    return lax.ppermute(values, AXES, device_pairs(place))
+
+
+def swap_core(values):
+    return lax.ppermute(values, "c", [(0, 1), (1, 0)])
+
+
+def swap_x(values):
+    return lax.ppermute(values, "x", [(0, 1), (1, 0)])
+
+
+def swap_y(values):
+    return lax.ppermute(values, "y", [(0, 1), (1, 0)])
+
+
+def take(values, index, size, axis):
+    return lax.dynamic_slice_in_dim(values, index * size, size, axis)
+
+
+def ordered(index, mine, other, axis):
+    first = jnp.where(index == 0, mine, other)
+    second = jnp.where(index == 0, other, mine)
+    return jnp.concatenate([first, second], axis=axis)
+
+
+def to_rows(blocks, x, z):
+    got = []
+    for turn in range(2):
+        mine = lax.dynamic_index_in_dim(blocks, x ^ turn, 0, keepdims=False)
+        got.append(move(mine, lambda y, c, z, x: (y, z & 1, 2 * c + (x ^ turn), z >> 1)))
+    return ordered(z & 1, got[0], got[1], 0)
+
+
+def from_rows(frames, x, z):
+    half = frames.shape[0] // 2
+    got = []
+    for turn in range(2):
+        mine = take(frames, (z & 1) ^ turn, half, 0)
+        got.append(move(mine, lambda y, c, z, x: (y, z >> 1, 2 * x + c, (z & 1) ^ turn)))
+    return ordered(x, got[0][None], got[1][None], 0)
+
+
+def split_body(
+    feats, segments, labels, conv_weight, w_qkv, w_out, w_up, w_down, head_w, head_b, gains, biases, up_bias
+):
+    y, c, z, x = (lax.axis_index(name) for name in AXES)
+    features = feats.shape[2]
+    half = features // 2
+    frames = 2 * feats.shape[1]
+    chip_frames = 2 * frames
+    tokens = frames
+    rim = KERNEL // 2
+    rise = lax.axis_size("z") * lax.axis_size("x") // 2
+
+    feats_own = to_rows(feats, x, z)
+    labels_own = to_rows(labels, x, z)
+    seg_rows = ordered(c, segments, swap_core(segments), 0)
+    seg_row = lax.dynamic_index_in_dim(seg_rows, z, 0, keepdims=False)
+    seg_chip = take(seg_row, x, chip_frames, 0)
+    seg_far = take(seg_row, 1 - x, chip_frames, 0)
+    seg_wide = jnp.pad(seg_row, (rim, rim), constant_values=-1)
+    seg_ext = lax.dynamic_slice_in_dim(seg_wide, x * chip_frames, chip_frames + 2 * rim, 0)[None]
+
+    def to_chip(values):
+        return ordered(c, take(values, c, half, 1), swap_core(take(values, 1 - c, half, 1)), 0)
+
+    def to_tokens(values):
+        return ordered(c, take(values, c, frames, 0), swap_core(take(values, 1 - c, frames, 0)), 1)
+
+    def with_rim(values):
+        edge = swap_x(jnp.where(x == 0, values[chip_frames - rim :], values[:rim]))
+        empty = jnp.zeros_like(edge)
+        before = jnp.where(x == 0, empty, edge)
+        after = jnp.where(x == 0, edge, empty)
+        return jnp.concatenate([before, values, after], axis=0)[None]
+
+    def both_cores(values):
+        return jnp.concatenate([values, swap_core(values)], axis=0)
+
+    def half_of_both(values):
+        width = values.shape[1] // 2
+        return jnp.concatenate([take(values, c, width, 1), swap_core(take(values, 1 - c, width, 1))], axis=0)
+
+    def to_groups(values):
+        width = half // 2
+        wide = ordered(x, take(values, x, width, 1), swap_x(take(values, 1 - x, width, 1)), 0)
+        return ordered(y, take(wide, y, 128, 1)[None], swap_y(take(wide, 1 - y, 128, 1))[None], 0)
+
+    feats_chip = to_chip(feats_own)
+    feats_group = to_groups(feats_chip)
+    conv_sum = grouped_conv(with_rim(feats_chip), seg_ext, conv_weight, 4 * c, rise, False)
+    conv_sum = conv_sum + take(biases[:, 0], c, half, 0)
+    activated, conv_pull = jax.vjp(gelu_exact, conv_sum)
+    position = to_tokens(feats_chip.astype(jnp.float32) + activated)
+    normed, first_pull = jax.vjp(layer_norm, position, gains[:, 0], biases[:, 1])
+    normed_low = normed.astype(jnp.bfloat16)
+    qkv_bias = jnp.concatenate([biases[:, 2], jnp.zeros((features,), jnp.float32), biases[:, 3]])
+    mixed = (jnp.dot(normed_low, w_qkv, preferred_element_type=jnp.float32) + qkv_bias).astype(jnp.bfloat16)
+    split = mixed.reshape(tokens, 3, 2, half)
+    mine = lax.dynamic_index_in_dim(split, c, 2, keepdims=False).reshape(tokens, 3 * half)
+    theirs = lax.dynamic_index_in_dim(split, 1 - c, 2, keepdims=False).reshape(tokens, 3 * half)
+    mixed_chip = ordered(c, mine, swap_core(theirs), 0)
+    queries = mixed_chip[:, :half]
+    near = mixed_chip[:, half:]
+    far = swap_x(near)
+    both = jnp.concatenate([near, far], axis=0)
+    seg_both = jnp.concatenate([seg_chip, seg_far])
+    attended, lse = attend_heads(queries, both[:, :half], both[:, half:], seg_chip, seg_both)
+    attended_low = to_tokens(attended.astype(jnp.bfloat16))
+    resid = position + jnp.dot(attended_low, w_out, preferred_element_type=jnp.float32) + biases[:, 4]
+    normed_second, second_pull = jax.vjp(layer_norm, resid, gains[:, 1], biases[:, 5])
+    second_low = normed_second.astype(jnp.bfloat16)
+    up_sum = jnp.dot(second_low, w_up, preferred_element_type=jnp.float32) + up_bias
+    up_active, up_pull = jax.vjp(gelu_exact, up_sum)
+    active_low = up_active.astype(jnp.bfloat16)
+    output = resid + jnp.dot(active_low, w_down, preferred_element_type=jnp.float32) + biases[:, 6]
+    output_low = output.astype(jnp.bfloat16)
+    layer_out = from_rows(output_low, x, z)
+    logits = jnp.dot(output_low, head_w, preferred_element_type=jnp.float32) + head_b
+    row_top = jnp.max(logits, axis=-1, keepdims=True)
+    shifted = jnp.exp(logits - row_top)
+    exp_sums = jnp.sum(shifted, axis=-1, keepdims=True)
+    onehot = labels_own[:, None] == jnp.arange(VOCAB, dtype=jnp.int32)[None, :]
+    picked = jnp.sum(jnp.where(onehot, logits, 0.0), axis=-1)
+    local_loss = jnp.sum(row_top[:, 0] + jnp.log(exp_sums[:, 0]) - picked)
+    grad_logits = (shifted / exp_sums - onehot.astype(jnp.float32)).astype(jnp.bfloat16)
+
+    grad_head_w = outer_sum(grad_logits, output_low)
+    grad_head_b = jnp.sum(grad_logits.astype(jnp.float32), axis=0)
+    grad_output = back_product(grad_logits, head_w)
+    grad_output_low = grad_output.astype(jnp.bfloat16)
+    grad_down_bias = jnp.sum(grad_output_low.astype(jnp.float32), axis=0)
+    grad_active = back_product(grad_output_low, w_down)
+    grad_up_low = up_pull(grad_active)[0].astype(jnp.bfloat16)
+    grad_up_bias = jnp.sum(grad_up_low.astype(jnp.float32), axis=0)
+    grad_second = back_product(grad_up_low, w_up)
+    grad_resid_part, grad_gain_second, grad_shift_second = second_pull(grad_second)
+    grad_resid = grad_output + grad_resid_part
+    grad_branch_low = grad_resid.astype(jnp.bfloat16)
+    grad_out_bias = jnp.sum(grad_branch_low.astype(jnp.float32), axis=0)
+    grad_attended = back_product(grad_branch_low, w_out).astype(jnp.bfloat16)
+    grad_heads = to_chip(grad_attended)
+    dq_far, dk_far, dv_far = attend_heads_back(
+        queries, far[:, :half], far[:, half:], grad_heads, attended, lse, seg_chip, seg_far, jnp.bfloat16
+    )
+    got = swap_x(jnp.concatenate([dk_far, dv_far], axis=1)).astype(jnp.float32)
+    dq, dk, dv = attend_heads_back(
+        queries, near[:, :half], near[:, half:], grad_heads, attended, lse, seg_chip, seg_chip, jnp.float32
+    )
+    grad_chip = jnp.concatenate([dq + dq_far, dk + got[:, :half], dv + got[:, half:]], axis=1).astype(jnp.bfloat16)
+    mine = take(grad_chip, c, frames, 0).reshape(tokens, 3, 1, half)
+    theirs = swap_core(take(grad_chip, 1 - c, frames, 0)).reshape(tokens, 3, 1, half)
+    grad_mixed = ordered(c, mine, theirs, 2).reshape(tokens, 3 * features)
+    mixed_sums = jnp.sum(grad_mixed.astype(jnp.float32), axis=0)
+    grad_normed = back_product(grad_mixed, w_qkv)
+    grad_position_part, grad_gain_first, grad_shift_first = first_pull(grad_normed)
+    grad_position = to_chip(grad_resid + grad_position_part)
+    grad_conv_low = conv_pull(grad_position)[0].astype(jnp.bfloat16)
+    grad_conv_bias = jnp.sum(grad_conv_low.astype(jnp.float32), axis=0)
+    grad_group = to_groups(grad_conv_low)
+    conv_input = grouped_conv(with_rim(grad_conv_low), seg_ext, conv_weight, 4 * c, rise, True)
+    grad_feats = from_rows(to_tokens((grad_position + conv_input).astype(jnp.bfloat16)), x, z)
+
+    def reduced(half_grad):
+        rows, width = half_grad.shape
+        quarter = width // 2
+        kept = take(half_grad, y, quarter, 1) + swap_y(take(half_grad, 1 - y, quarter, 1)).astype(jnp.float32)
+        kept = kept.reshape(4, 2, rows // 8, quarter)
+        away = lax.dynamic_index_in_dim(kept, 1 - x, 1, keepdims=False).astype(jnp.bfloat16)
+        stay = lax.dynamic_index_in_dim(kept, x, 1, keepdims=False)
+        stay = (stay + swap_x(away).astype(jnp.float32)).astype(jnp.bfloat16)
+        shard = lax.psum_scatter(stay, "z", scatter_dimension=0, tiled=True)[0]
+        return shard
+
+    def spread(shard):
+        wide = ordered(y, shard, swap_y(shard), 1)
+        return wide, swap_core(wide)
+
+    def weight_grad(left, right):
+        half_grad = outer_sum(left, right)
+        rows, width = half_grad.shape
+        low = half_grad.astype(jnp.bfloat16)
+        mine, theirs = spread(reduced(low))
+        return mine, theirs
+
+    active_both, second_both, attended_both, normed_both = (
+        both_cores(item) for item in (active_low, second_low, attended_low, normed_low)
+    )
+    mine, theirs = weight_grad(active_both, half_of_both(grad_output_low))
+    grad_w_down = ordered(c, mine, theirs, 1).astype(jnp.float32)
+    mine, theirs = weight_grad(second_both, half_of_both(grad_up_low))
+    grad_w_up = ordered(c, mine, theirs, 1).astype(jnp.float32)
+    mine, theirs = weight_grad(attended_both, half_of_both(grad_branch_low))
+    grad_w_out = ordered(c, mine, theirs, 1).astype(jnp.float32)
+    grad_own_first = jnp.concatenate([take(grad_chip, c, frames, 0), take(grad_chip, 1 - c, frames, 0)], axis=0)
+    mine, theirs = weight_grad(normed_both, grad_own_first)
+    mine, theirs = (item.reshape(-1, 3, 1, half) for item in (mine, theirs))
+    grad_w_qkv = ordered(c, mine, theirs, 2).reshape(-1, 3 * features).astype(jnp.float32)
+
+    seg_y = ordered(y, seg_row[None], swap_y(seg_row)[None], 0)
+    pad = ((0, 0), (rim, rim))
+    conv_grad = grouped_conv_weight(
+        jnp.pad(feats_group, pad + ((0, 0),)),
+        jnp.pad(seg_y, pad, constant_values=-1),
+        grad_group.reshape(-1, 128),
+        rise,
+    )
+    conv_grad = lax.psum_scatter(conv_grad.reshape(128, 4, -1), "z", scatter_dimension=1, tiled=True)[:, 0]
+    width = conv_grad.shape[1] // 2
+    conv_grad = ordered(x, take(conv_grad, x, width, 1)[None], swap_x(take(conv_grad, 1 - x, width, 1))[None], 0)
+    conv_grad = ordered(y, conv_grad[:, None], swap_y(conv_grad)[:, None], 1)
+    conv_grad = ordered(c, conv_grad[None], swap_core(conv_grad)[None], 0)
+    grad_conv_weight = conv_grad.reshape(features, width).T.astype(jnp.float32)
+
+    zero_half = jnp.zeros((half,), jnp.float32)
+    conv_bias = jnp.concatenate([jnp.where(c == 0, grad_conv_bias, zero_half), jnp.where(c == 1, grad_conv_bias, zero_half)])
+    last_row = jnp.concatenate([grad_head_b, local_loss[None], jnp.zeros((features - VOCAB - 1,), jnp.float32)])
+    early = jnp.concatenate(
+        [
+            grad_head_w,
+            jnp.stack([grad_gain_second, grad_out_bias, grad_shift_second, grad_down_bias]),
+            grad_up_bias.reshape(4, features),
+            last_row[None],
+        ],
+        axis=0,
+    )
+    late = jnp.stack(
+        [grad_gain_first, conv_bias, grad_shift_first, mixed_sums[:features], mixed_sums[2 * features :]]
+    )
+    early = lax.psum(early, AXES)
+    late = lax.psum(late, AXES)
+    loss = early[VOCAB + 8, VOCAB] / (tokens * 32)
+    head_bias_total = early[VOCAB + 8, :VOCAB]
+    block = 2 * z + x
+    early_part = take(early, block, features // 8, 1)
+    late_part = take(late, block, features // 8, 1)
+    gain_part = jnp.stack([late_part[0], early_part[VOCAB]], axis=1)
+    bias_part = jnp.stack(
+        [
+            late_part[1],
+            late_part[2],
+            late_part[3],
+            late_part[4],
+            early_part[VOCAB + 1],
+            early_part[VOCAB + 2],
+            early_part[VOCAB + 3],
+        ],
+        axis=1,
+    )
+    up_total = early[VOCAB + 4 : VOCAB + 8].reshape(-1)
+    up_part = take(up_total, block, up_total.shape[0] // 8, 0)
+    return (
+        layer_out,
+        loss,
+        grad_feats.astype(jnp.float32),
+        grad_conv_weight,
+        grad_w_qkv,
+        grad_w_out,
+        grad_w_up,
+        grad_w_down,
+        early_part[:VOCAB].T,
+        head_bias_total,
+        gain_part,
+        bias_part,
+        up_part,
+    )
+
+
+def split_solution(mesh):
+    fine = Mesh(mesh.devices.reshape(2, 2, 4, 2), AXES)
+    rows, parts = ("y", "c"), ("z", "x")
+    return jax.shard_map(
+        split_body,
+        mesh=fine,
+        in_specs=(P(rows, parts, None), P(rows, None), P(rows, parts)) + (P(),) * 10,
+        out_specs=(
+            P(rows, parts, None),
+            P(),
+            P(rows, parts, None),
+            P(parts, None),
+            P(parts, None),
+            P(parts, None),
+            P(parts, None),
+            P(parts, None),
+            P(parts, None),
+            P(),
+            P(parts, None),
+            P(parts, None),
+            P(parts),
+        ),
+        check_vma=False,
+    )
+
+
+def solution(mesh):
+    if mesh.shape["dp"] == 4 and mesh.shape["seq"] == 8:
+        return split_solution(mesh)
+    return whole_solution(mesh)

time: 2670 us -> 841 us (0.31)
  waiting for transfers between devices: 1640 us -> 310 us
  local copies, waits for them, and re-layouts: 531 us -> 97.2 us
  Pallas kernels: 0 us -> 131 us
  matrix products: 181 us -> 69 us
  other arithmetic: 167 us -> 76.4 us
  starting transfers between devices: 12.2 us -> 72.4 us
  blocking collectives: 104 us -> 50.7 us
    reduce_scatter x8 -> x5, waiting for transfers between devices: 1440 us -> 7.96 us  [the longest x4 7.96 us: reduced(): shard = lax.psum_scatter(stay, 'z', scatter_dimension=0, tiled=True)[0]]
    ppermute x4 -> x52, waiting for transfers between devices: 0.01 us -> 185 us  [the longest x12 82.4 us: swap_y(): return lax.ppermute(values, 'y', [(0, 1), (1, 0)])]
    all_gather x2 -> x0, waiting for transfers between devices: 138 us -> none  [the longest x1 72 us: body(): key_shard = lax.all_gather(keys, 'seq', axis=1, tiled=True)]
    dynamic_slice x50 -> x23, local copies, waits for them, and re-layouts: 159 us -> 25.9 us  [the longest x19 15 us: take(): return lax.dynamic_slice_in_dim(values, index * size, size, axis)]
    pallas_call x0 -> x6, Pallas kernels: none -> 131 us  [the longest x2 84 us: grouped_conv(): pl.pallas_call(partial(conv_kernel, slots, backward), grid_spec=pltpu.Pre...]
    psum x1, waiting for transfers between devices: 0.01 us -> 117 us  [split_body(): early = lax.psum(early, AXES)]
    dot_general x65 -> x5, matrix products: 126 us -> 26.6 us  [the longest x1 15.6 us: split_body(): jnp.dot(second_low, w_up, preferred_element_type=jnp.float32) + up_bias]
    while x499 -> x0, local copies, waits for them, and re-layouts: 86.5 us -> none
  transfers between devices with their start and end apart: 16 -> 58, of which waited for: 9 -> 20; matrix products, arithmetic and copies ran while one was open for 16% -> 23% of each run, Pallas kernels for 0% -> 11%
where the time goes in v1:
time: 841 us; the launch traced here: 826 us
  waiting for transfers between devices  310 us (37%)
  Pallas kernels  131 us (16%)
  local copies, waits for them, and re-layouts  97.2 us (12%)
  other arithmetic  76.4 us (9%)
  starting transfers between devices  72.4 us (9%)
  matrix products  69 us (8%)
  blocking collectives  50.7 us (6%)
  between operations  19.3 us (2%)
    psum x1, waiting for transfers between devices, split_body(): early = lax.psum(early, AXES)  117 us
    pallas_call x2, Pallas kernels, grouped_conv(): pl.pallas_call(partial(conv_kernel, slots, backward), grid_spec=pltpu.Pre...  84 us
    ppermute x12, waiting for transfers between devices, swap_y(): return lax.ppermute(values, 'y', [(0, 1), (1, 0)])  82.4 us
    ppermute x11, waiting for transfers between devices, swap_x(): return lax.ppermute(values, 'x', [(0, 1), (1, 0)])  79.5 us
    psum x1, blocking collectives, split_body(): late = lax.psum(late, AXES)  50.7 us
    unnamed x137, local copies, waits for them, and re-layouts  29.7 us
    ppermute x11, starting transfers between devices, swap_x(): return lax.ppermute(values, 'x', [(0, 1), (1, 0)])  28.7 us
    dot_general x5, matrix products, back_product(): lax.dot_general(grad_rows, weight, (((1,), (1,)), ((), ())), preferred_el...  26.5 us
  transfers between devices with their start and end apart: 58, of which 20 were waited for; matrix products, arithmetic and copies ran while one was open for 23% of the time, Pallas kernels for 11%

profile of v1, /device:TPU:0, one launch (start us, length us, event | category | flops | bytes accessed | tf_op | source)
XLA Modules:
  0.0 825.8 jit_solution(15414555826035725976)
XLA Ops:
  10.0 4.3 collective-permute-start.1
  14.3 2.7 collective-permute-start.3
  18.4 2.9 collective-permute-start.12
  31.1 2.3 collective-permute-start.2
  34.7 5.7 collective-permute-start.4
  40.6 2.2 collective-permute-done.4
  43.7 39.1 %conv_forth.1 = f32[512,512]{1,0:T(8,128)} custom-call(s32[37]{0:T(128)} %pad_add_fusion.3.meta, bf16[640,512]{1,0:T(8,128)(2,1)} %pad_maximum_fusion.8.x_ref, f32[160,256]{1,0:T(8,128)} %copy.122.seg_ref, bf16[8192,1024]{1,0:T(8,128)(2,1)} %w_ref.3), custom_call_target="tpu_custom_call" | custom-call | flops 6643777536 | bytes 8388608 | tf_op jit(solution)/shard_map/conv_forth/pallas_call | solution.py:675
  82.8 4.2 multiply_add_fusion
  93.8 5.9 fusion.9
  99.7 5.2 reshape.443
  104.9 6.8 constant_dynamic-slice_fusion.24
  111.7 4.6 copy.151
  116.3 2.3 copy.125
  122.0 6.6 collective-permute-done.22
  130.4 4.6 copy.150
  135.1 2.3 copy.126
  142.5 5.7 collective-permute-done.23
  150.4 13.2 %collective-permute-done.7 = bf16[512,1024]{1,0:T(8,128)(2,1)S(1)} collective-permute-done((bf16[512,1024]{1,0:T(8,128)(2,1)S(1)}, bf16[512,1024]{1,0:T(8,128)(2,1)S(1)}, u32[]{:S(2)}, u32[]{:S(2)}) %collective-permute-start.7) | collective-permute-done | bytes 1048608 | tf_op jit(solution)/shard_map/ppermute | solution.py:929
  165.1 10.3 %attend.1 = (f32[512,512]{1,0:T(8,128)}, f32[4,8,512]{2,1,0:T(8,128)}) custom-call(s32[1,512]{1,0:T(1,128)} %copy-done.47, s32[1024,1]{1,0:T(8,128)} %copy.128.seg_k_ref, bf16[512,512]{1,0:T(8,128)(2,1)} %get-tuple-element.132.q_ref, bf16[1024,512]{1,0:T(8,128)(2,1)} %get-tuple-element.128.k_ref, bf16[1024,512]{1,0:T(8,128)(2,1)} %get-tuple-element.127.v_ref), custom_call_target="tpu_custom_call" | custom-call | flops 2147483648 | bytes 2097152 | tf_op jit(solution)/shard_map/attend/pallas_call | solution.py:821
  180.7 15.6 %multiply_convert_fusion = (bf16[256,4096]{1,0:T(8,128)(2,1)}, f32[256,4096]{1,0:T(8,128)S(1)}, f32[256,4096]{1,0:T(8,128)}) fusion(f32[4096]{0:T(1024)S(1)} %copy-done.61, bf16[256,1024]{1,0:T(8,128)(2,1)} %add_convert_fusion.4, bf16[1024,4096]{1,0:T(8,128)(2,1)} %param.19), kind=kOutput, calls=%fused_computation.11 | convolution fusion | flops 2216689664 | bytes 19415040 | tf_op jit(solution)/shard_map/dot_general | solution.py:1033
  196.3 4.1 fusion.21
  204.7 11.8 %convert_reduce_fusion = (f32[4096]{0:T(1024)}, bf16[256,4096]{1,0:T(8,128)(2,1)S(1)}) fusion(f32[256,4096]{1,0:T(8,128)S(1)} %get-tuple-element.112, f32[256,4096]{1,0:T(8,128)} %get-tuple-element.238, bf16[256,1024]{1,0:T(8,128)(2,1)S(1)} %get-tuple-element.106, bf16[4096,1024]{1,0:T(8,128)(2,1)} %param.20), kind=kOutput, calls=%fused_computation.9 | convolution fusion | flops 2164256768 | bytes 19415040 | tf_op jit(solution)/shard_map/dot_general | solution.py:58
  216.5 7.4 multiply_reduce_fusion.2
  230.3 2.6 concatenate.164
  233.4 3.1 constant_dynamic-slice_fusion.6
  237.4 116.5 %all-reduce.5.cloned.1.call-done = f32[41,1024]{1,0:T(8,128)} async-done(((f32[41,1024]{1,0:T(8,128)}), f32[41,1024]{1,0:T(8,128)}) %all-reduce.5.cloned.1.call-update) | async-done | bytes 167952 | tf_op jit(solution)/shard_map/psum | solution.py:1150
  366.2 8.5 %attend_back.3 = (f32[512,512]{1,0:T(8,128)}, bf16[512,512]{1,0:T(8,128)(2,1)}, bf16[512,512]{1,0:T(8,128)(2,1)}) custom-call(s32[1,512]{1,0:T(1,128)} %copy-done.47, s32[512,1]{1,0:T(8,128)} %copy.130.seg_k_ref, bf16[512,512]{1,0:T(8,128)(2,1)} %get-tuple-element.132.q_ref, bf16[512,512]{1,0:T(8,128)(2,1)} %get-tuple-element.147.k_ref, ...), custom_call_target="tpu_custom_call" | custom-call | flops 2684354560 | bytes 4194304 | tf_op jit(solution)/shard_map/attend_back/pallas_call | solution.py:875
  374.7 2.3 pad_maximum_fusion.4
  377.9 8.6 %attend_back.2 = (f32[512,512]{1,0:T(8,128)}, f32[512,512]{1,0:T(8,128)}, f32[512,512]{1,0:T(8,128)}) custom-call(s32[1,512]{1,0:T(1,128)} %copy-done.47, s32[512,1]{1,0:T(8,128)} %copy.129.seg_k_ref, bf16[512,512]{1,0:T(8,128)(2,1)} %get-tuple-element.132.q_ref, bf16[512,512]{1,0:T(8,128)(2,1)} %get-tuple-element.133.k_ref, ...), custom_call_target="tpu_custom_call" | custom-call | flops 2684354560 | bytes 4194304 | tf_op jit(solution)/shard_map/attend_back/pallas_call | solution.py:875
  388.9 18.8 %collective-permute-done.37 = bf16[4,128,256]{2,1,0:T(8,128)(2,1)S(1)} collective-permute-done((bf16[4,128,256]{2,1,0:T(8,128)(2,1)S(1)}, bf16[4,128,256]{2,1,0:T(8,128)(2,1)S(1)}, u32[]{:S(2)}, u32[]{:S(2)}) %collective-permute-start.37) | collective-permute-done | bytes 262176 | tf_op jit(solution)/shard_map/ppermute | solution.py:929
  415.4 6.0 convolution_convert_fusion.1
  421.4 7.9 reduce-scatter.10.cloned.1.call-done
  430.7 3.1 constant_dynamic-slice_fusion.4
  438.4 3.3 convolution_convert_fusion.2
  447.9 5.6 fusion.87
  454.6 61.0 %collective-permute-done.30 = bf16[1024,768]{1,0:T(8,128)(2,1)} collective-permute-done((bf16[1024,768]{1,0:T(8,128)(2,1)}, bf16[1024,768]{1,0:T(8,128)(2,1)}, u32[]{:S(2)}, u32[]{:S(2)}) %collective-permute-start.30) | collective-permute-done | bytes 1572896 | tf_op jit(solution)/shard_map/ppermute | solution.py:933
  520.0 2.3 copy.154
  522.3 2.4 collective-permute-start.31
  528.3 4.7 convert_add_fusion.1
  536.1 10.6 %collective-permute-done.31 = bf16[4,128,768]{1,2,0:T(8,128)(2,1)} collective-permute-done((bf16[4,128,768]{1,2,0:T(8,128)(2,1)}, bf16[4,128,768]{1,2,0:T(8,128)(2,1)}, u32[]{:S(2)}, u32[]{:S(2)}) %collective-permute-start.31) | collective-permute-done | bytes 786464 | tf_op jit(solution)/shard_map/ppermute | solution.py:929
  546.7 2.2 fusion.18
  551.7 2.5 collective-permute-start.43
  556.9 21.2 %collective-permute-done.43 = bf16[4,128,1024]{2,1,0:T(8,128)(2,1)S(1)} collective-permute-done((bf16[4,128,1024]{2,1,0:T(8,128)(2,1)S(1)}, bf16[4,128,1024]{2,1,0:T(8,128)(2,1)S(1)}, u32[]{:S(2)}, u32[]{:S(2)}) %collective-permute-start.43) | collective-permute-done | bytes 1048608 | tf_op jit(solution)/shard_map/ppermute | solution.py:929
  579.6 4.6 convolution_convert_fusion
  588.3 5.4 collective-permute-done.25
  594.7 19.5 %conv_weight_grad.1 = bf16[128,8192]{1,0:T(8,128)(2,1)} custom-call(s32[121]{0:T(128)} %pad_add_fusion.4.meta, bf16[2304,128]{1,0:T(8,128)(2,1)} %bitcast.227, f32[576,256]{1,0:T(8,128)} %copy.139.seg_ref, bf16[2048,128]{1,0:T(8,128)(2,1)} %bitcast.228), custom_call_target="tpu_custom_call" | custom-call | flops 5536481280 | bytes 2097152 | tf_op jit(solution)/shard_map/conv_weight_grad/pallas_call | solution.py:757
  614.2 3.3 copy.162
  618.9 2.1 collective-permute-start.17
  621.0 2.2 collective-permute-done.17
  624.1 44.8 %conv_back.1 = f32[512,512]{1,0:T(8,128)} custom-call(s32[37]{0:T(128)} %pad_add_fusion.3.meta, bf16[640,512]{1,0:T(8,128)(2,1)} %pad_maximum_fusion.9.x_ref, f32[160,256]{1,0:T(8,128)} %copy.122.seg_ref, bf16[8192,1024]{1,0:T(8,128)(2,1)} %w_ref.3), custom_call_target="tpu_custom_call" | custom-call | flops 6643777536 | bytes 8388608 | tf_op jit(solution)/shard_map/conv_back/pallas_call | solution.py:675
  669.0 2.1 convert_add_fusion
  676.7 50.7 %psum.15 = f32[5,1024]{1,0:T(8,128)S(1)} all-reduce(f32[5,1024]{1,0:T(8,128)S(1)} %stack.33), channel_id=1, replica_groups=mesh['y'=2,'c'=2,'z'=4,'x'=2] {'y','c','z','x'}, use_global_device_ids=true, to_apply=%region_37.38 | all-reduce | flops 5120 | bytes 40960 | tf_op jit(solution)/shard_map/psum | solution.py:1151
  728.3 3.5 collective-permute-start.20
  731.8 2.8 fusion.13
  735.9 2.2 collective-permute-start.32
  738.2 21.3 %collective-permute-done.20 = bf16[128,1024]{1,0:T(8,128)(2,1)S(1)} collective-permute-done((bf16[128,1024]{1,0:T(8,128)(2,1)S(1)}, bf16[128,1024]{1,0:T(8,128)(2,1)S(1)}, u32[]{:S(2)}, u32[]{:S(2)}) %collective-permute-start.20) | collective-permute-done | bytes 262176 | tf_op jit(solution)/shard_map/ppermute | solution.py:921
  761.5 3.4 collective-permute-start.33
  764.9 3.5 collective-permute-done.44
  772.5 8.0 collective-permute-start.26
  782.4 4.7 collective-permute-done.26
  791.9 3.0 copy.149
  796.0 6.7 collective-permute-done.27
  809.0 2.3 copy.141
  811.3 5.5 copy.148
  (417 shorter events, 141.9 us)
Async XLA Ops:
  8.0 170.5 %copy-start = (bf16[1024,1024]{1,0:T(8,128)(2,1)S(1)}, bf16[1024,1024]{1,0:T(8,128)(2,1)}, u32[]{:S(2)}) copy-start(bf16[1024,1024]{1,0:T(8,128)(2,1)} %param.18) | copy-start | bytes 6291460
  8.0 345.9 %all-reduce.5.cloned.1.call-start = ((), (), s32[]{:S(2)}) async-start(), calls=%async_computation.5 | async-start | bytes 393216 | tf_op jit(solution)/shard_map/psum | solution.py:1150
  9.3 21.7 %collective-permute-start = (bf16[128,1024]{1,0:T(8,128)(2,1)S(1)}, bf16[128,1024]{1,0:T(8,128)(2,1)S(1)}, u32[]{:S(2)}, u32[]{:S(2)}) collective-permute-start(bf16[128,1024]{1,0:T(8,128)(2,1)S(1)} %get-tuple-element.187), channel_id=1, source_target_pairs={{0,0},{1,2},{2,8},{3,10},{4,1},{5,3},{6,9},{7,11},{8,4},{9,6},{10,... | collective-permute-start | bytes 786440 | tf_op jit(solution)/shard_map/ppermute | solution.py:921
  10.0 21.0 %collective-permute-start.1 = (bf16[128,1024]{1,0:T(8,128)(2,1)S(1)}, bf16[128,1024]{1,0:T(8,128)(2,1)S(1)}, u32[]{:S(2)}, u32[]{:S(2)}) collective-permute-start(bf16[128,1024]{1,0:T(8,128)(2,1)S(1)} %get-tuple-element.186), channel_id=1, source_target_pairs={{0,2},{1,0},{2,10},{3,8},{4,3},{5,1},{6,11},{7,9},{8,6},{9,4},{10,... | collective-permute-start | bytes 786440 | tf_op jit(solution)/shard_map/ppermute | solution.py:921
  14.3 9.0 %collective-permute-start.3 = (s32[2,1024]{1,0:T(2,128)}, s32[2,1024]{1,0:T(2,128)S(1)}, u32[]{:S(2)}, u32[]{:S(2)}) collective-permute-start(s32[2,1024]{1,0:T(2,128)} %param.14), channel_id=1, source_target_pairs={{0,8},{8,0},{1,9},{9,1},{2,10},{10,2},{3,11},{11,3},{4,12},{12,4},... | collective-permute-start | bytes 24584 | tf_op jit(solution)/shard_map/ppermute | solution.py:925
  17.8 5.5 collective-permute-start.11
  18.4 4.8 collective-permute-start.12
  24.1 9.3 %collective-permute-start.21 = (s32[1024]{0:T(1024)S(1)}, s32[1024]{0:T(1024)S(1)}, u32[]{:S(2)}, u32[]{:S(2)}) collective-permute-start(s32[1024]{0:T(1024)S(1)} %bitcast.240), channel_id=1, source_target_pairs={{0,16},{16,0},{1,17},{17,1},{2,18},{18,2},{3,19},{19,3},{4,20},{20... | collective-permute-start | bytes 12296 | tf_op jit(solution)/shard_map/ppermute | solution.py:933
  31.1 3.4 collective-permute-start.2
  34.7 8.1 collective-permute-start.4
  88.8 2.3 collective-permute-start.5
  118.6 18.7 %collective-permute-start.6 = (bf16[256,1536]{1,0:T(8,128)(2,1)}, bf16[256,1536]{1,0:T(8,128)(2,1)}, u32[]{:S(2)}, u32[]{:S(2)}) collective-permute-start(bf16[256,1536]{1,0:T(8,128)(2,1)} %copy.125), channel_id=1, source_target_pairs={{0,8},{8,0},{1,9},{9,1},{2,10},{10,2},{3,11},{11,3},{4,12},{12,4},... | collective-permute-start | bytes 2359304 | tf_op jit(solution)/shard_map/ppermute | solution.py:925
  120.0 8.6 %collective-permute-start.22 = (bf16[512,256]{1,0:T(8,128)(2,1)S(1)}, bf16[512,256]{1,0:T(8,128)(2,1)S(1)}, u32[]{:S(2)}, u32[]{:S(2)}) collective-permute-start(bf16[512,256]{1,0:T(8,128)(2,1)S(1)} %fusion.69), channel_id=1, source_target_pairs={{0,1},{1,0},{2,3},{3,2},{4,5},{5,4},{6,7},{7,6},{8,9},{9,8},{10,11... | collective-permute-start | bytes 786440 | tf_op jit(solution)/shard_map/ppermute | solution.py:929
  139.0 24.6 %collective-permute-start.7 = (bf16[512,1024]{1,0:T(8,128)(2,1)S(1)}, bf16[512,1024]{1,0:T(8,128)(2,1)S(1)}, u32[]{:S(2)}, u32[]{:S(2)}) collective-permute-start(bf16[512,1024]{1,0:T(8,128)(2,1)S(1)} %fusion.24), channel_id=1, source_target_pairs={{0,1},{1,0},{2,3},{3,2},{4,5},{5,4},{6,7},{7,6},{8,9},{9,8},{10,11... | collective-permute-start | bytes 3145736 | tf_op jit(solution)/shard_map/ppermute | solution.py:929
  140.9 7.4 collective-permute-start.23
  149.2 289.2 %collective-permute-start.29 = (bf16[256,1024]{1,0:T(8,128)(2,1)}, bf16[256,1024]{1,0:T(8,128)(2,1)}, u32[]{:S(2)}, u32[]{:S(2)}) collective-permute-start(bf16[256,1024]{1,0:T(8,128)(2,1)} %add_convert_fusion.5), channel_id=1, source_target_pairs={{0,8},{8,0},{1,9},{9,1},{2,10},{10,2},{3,11},{11,3},{4,12},{12,4},... | collective-permute-start | bytes 1572872 | tf_op jit(solution)/shard_map/ppermute | solution.py:925
  176.8 1.6 collective-permute-start.8
  202.5 377.1 %collective-permute-start.46 = (bf16[256,4096]{1,0:T(8,128)(2,1)}, bf16[256,4096]{1,0:T(8,128)(2,1)}, u32[]{:S(2)}, u32[]{:S(2)}) collective-permute-start(bf16[256,4096]{1,0:T(8,128)(2,1)} %get-tuple-element.111), channel_id=1, source_target_pairs={{0,8},{8,0},{1,9},{9,1},{2,10},{10,2},{3,11},{11,3},{4,12},{12,4},... | collective-permute-start | bytes 6291464 | tf_op jit(solution)/shard_map/ppermute | solution.py:925
  202.6 212.4 %collective-permute-start.40 = (bf16[256,1024]{1,0:T(8,128)(2,1)}, bf16[256,1024]{1,0:T(8,128)(2,1)}, u32[]{:S(2)}, u32[]{:S(2)}) collective-permute-start(bf16[256,1024]{1,0:T(8,128)(2,1)} %add_convert_fusion.4), channel_id=1, source_target_pairs={{0,8},{8,0},{1,9},{9,1},{2,10},{10,2},{3,11},{11,3},{4,12},{12,4},... | collective-permute-start | bytes 1572872 | tf_op jit(solution)/shard_map/ppermute | solution.py:925
  227.4 133.8 %collective-permute-start.13 = (bf16[256,512]{1,0:T(8,128)(2,1)}, bf16[256,512]{1,0:T(8,128)(2,1)S(1)}, u32[]{:S(2)}, u32[]{:S(2)}) collective-permute-start(bf16[256,512]{1,0:T(8,128)(2,1)} %constant_dynamic-slice_fusion.18), channel_id=1, source_target_pairs={{0,8},{8,0},{1,9},{9,1},{2,10},{10,2},{3,11},{11,3},{4,12},{12,4},... | collective-permute-start | bytes 786440 | tf_op jit(solution)/shard_map/ppermute | solution.py:925
  227.6 133.7 %copy-start.40 = (bf16[256,1024]{1,0:T(8,128)(2,1)S(1)}, bf16[256,1024]{1,0:T(8,128)(2,1)}, u32[]{:S(2)}) copy-start(bf16[256,1024]{1,0:T(8,128)(2,1)} %copy-done.39) | copy-start | bytes 1572868
  232.9 129.9 %copy-start.38 = (bf16[256,512]{1,0:T(8,128)(2,1)S(1)}, bf16[256,512]{1,0:T(8,128)(2,1)}, u32[]{:S(2)}) copy-start(bf16[256,512]{1,0:T(8,128)(2,1)} %copy-done.37) | copy-start | bytes 786436
  232.9 196.4 %reduce-scatter.10.cloned.1.call-start = ((), (), s32[]{:S(2)}) async-start(), calls=%async_computation.8 | async-start | bytes 327680 | tf_op jit(solution)/shard_map/reduce_scatter | solution.py:1092
  233.0 129.8 %collective-permute-start.34 = (bf16[256,1024]{1,0:T(8,128)(2,1)}, bf16[256,1024]{1,0:T(8,128)(2,1)}, u32[]{:S(2)}, u32[]{:S(2)}) collective-permute-start(bf16[256,1024]{1,0:T(8,128)(2,1)} %pad_maximum_fusion.11), channel_id=1, source_target_pairs={{0,8},{8,0},{1,9},{9,1},{2,10},{10,2},{3,11},{11,3},{4,12},{12,4},... | collective-permute-start | bytes 1572872 | tf_op jit(solution)/shard_map/ppermute | solution.py:925
  361.2 1.5 collective-permute-start.35
  364.6 21.9 %collective-permute-start.36 = (bf16[1024,256]{1,0:T(8,128)(2,1)S(1)}, bf16[1024,256]{1,0:T(8,128)(2,1)S(1)}, u32[]{:S(2)}, u32[]{:S(2)}) collective-permute-start(bf16[1024,256]{1,0:T(8,128)(2,1)S(1)} %constant_dynamic-slice_fusion.7), channel_id=1, source_target_pairs={{0,16},{16,0},{1,17},{17,1},{2,18},{18,2},{3,19},{19,3},{4,20},{20... | collective-permute-start | bytes 1572872 | tf_op jit(solution)/shard_map/ppermute | solution.py:933
  377.0 32.0 %collective-permute-start.14 = (bf16[512,1024]{1,0:T(8,128)(2,1)}, bf16[512,1024]{1,0:T(8,128)(2,1)S(1)}, u32[]{:S(2)}, u32[]{:S(2)}) collective-permute-start(bf16[512,1024]{1,0:T(8,128)(2,1)} %pad_maximum_fusion.4), channel_id=1, source_target_pairs={{0,1},{1,0},{2,3},{3,2},{4,5},{5,4},{6,7},{7,6},{8,9},{9,8},{10,11... | collective-permute-start | bytes 3145736 | tf_op jit(solution)/shard_map/ppermute | solution.py:929
  386.7 21.1 %collective-permute-start.37 = (bf16[4,128,256]{2,1,0:T(8,128)(2,1)S(1)}, bf16[4,128,256]{2,1,0:T(8,128)(2,1)S(1)}, u32[]{:S(2)}, u32[]{:S(2)}) collective-permute-start(bf16[4,128,256]{2,1,0:T(8,128)(2,1)S(1)} %fusion.59), channel_id=1, source_target_pairs={{0,1},{1,0},{2,3},{3,2},{4,5},{5,4},{6,7},{7,6},{8,9},{9,8},{10,11... | collective-permute-start | bytes 786440 | tf_op jit(solution)/shard_map/ppermute | solution.py:929
  407.8 7.2 collective-permute-start.41
  408.5 327.4 %reduce-scatter.8.cloned.1.call-start = ((), (), s32[]{:S(2)}) async-start(), calls=%async_computation.7 | async-start | bytes 983040 | tf_op jit(solution)/shard_map/reduce_scatter | solution.py:1092
  410.0 169.6 %collective-permute-start.47 = (bf16[256,512]{1,0:T(8,128)(2,1)}, bf16[256,512]{1,0:T(8,128)(2,1)}, u32[]{:S(2)}, u32[]{:S(2)}) collective-permute-start(bf16[256,512]{1,0:T(8,128)(2,1)} %get-tuple-element.171), channel_id=1, source_target_pairs={{0,8},{8,0},{1,9},{9,1},{2,10},{10,2},{3,11},{11,3},{4,12},{12,4},... | collective-permute-start | bytes 786440 | tf_op jit(solution)/shard_map/ppermute | solution.py:925
  415.0 20.9 %collective-permute-start.15 = (bf16[256,1536]{1,0:T(8,128)(2,1)}, bf16[256,1536]{1,0:T(8,128)(2,1)}, u32[]{:S(2)}, u32[]{:S(2)}) collective-permute-start(bf16[256,1536]{1,0:T(8,128)(2,1)} %constant_dynamic-slice_fusion.16), channel_id=1, source_target_pairs={{0,8},{8,0},{1,9},{9,1},{2,10},{10,2},{3,11},{11,3},{4,12},{12,4},... | collective-permute-start | bytes 2359304 | tf_op jit(solution)/shard_map/ppermute | solution.py:925
  429.3 4.5 collective-permute-start.38
  433.8 117.3 %collective-permute-start.10 = (bf16[128,1024]{1,0:T(8,128)(2,1)}, bf16[128,1024]{1,0:T(8,128)(2,1)}, u32[]{:S(2)}, u32[]{:S(2)}) collective-permute-start(bf16[128,1024]{1,0:T(8,128)(2,1)} %get-tuple-element.183), channel_id=1, source_target_pairs={{0,1},{1,5},{2,0},{3,4},{4,9},{5,13},{6,8},{7,12},{8,3},{9,7},{10,... | collective-permute-start | bytes 786440 | tf_op jit(solution)/shard_map/ppermute | solution.py:921
  435.9 90.6 %collective-permute-start.42 = (bf16[1024,1024]{1,0:T(8,128)(2,1)}, bf16[1024,1024]{1,0:T(8,128)(2,1)}, u32[]{:S(2)}, u32[]{:S(2)}) collective-permute-start(bf16[1024,1024]{1,0:T(8,128)(2,1)} %constant_dynamic-slice_fusion.4), channel_id=1, source_target_pairs={{0,16},{16,0},{1,17},{17,1},{2,18},{18,2},{3,19},{19,3},{4,20},{20... | collective-permute-start | bytes 6291464 | tf_op jit(solution)/shard_map/ppermute | solution.py:933
  443.1 72.5 %collective-permute-start.30 = (bf16[1024,768]{1,0:T(8,128)(2,1)}, bf16[1024,768]{1,0:T(8,128)(2,1)}, u32[]{:S(2)}, u32[]{:S(2)}) collective-permute-start(bf16[1024,768]{1,0:T(8,128)(2,1)} %constant_dynamic-slice_fusion.12), channel_id=1, source_target_pairs={{0,16},{16,0},{1,17},{17,1},{2,18},{18,2},{3,19},{19,3},{4,20},{20... | collective-permute-start | bytes 4718600 | tf_op jit(solution)/shard_map/ppermute | solution.py:933
  447.9 67.7 %copy-start.27 = (bf16[1024,1536]{1,0:T(8,128)(2,1)S(1)}, bf16[1024,1536]{1,0:T(8,128)(2,1)}, u32[]{:S(2)}) copy-start(bf16[1024,1536]{1,0:T(8,128)(2,1)} %copy-done.26) | copy-start | bytes 9437188
  453.5 62.1 %copy-start.23 = (f32[256,1024]{1,0:T(8,128)}, f32[256,1024]{1,0:T(8,128)S(1)}, u32[]{:S(2)}) copy-start(f32[256,1024]{1,0:T(8,128)S(1)} %get-tuple-element.243) | copy-start | bytes 3145732
  453.5 63.8 %copy-start.53 = (f32[256]{0:T(256)}, f32[256]{0:T(256)S(1)}, u32[]{:S(2)}) copy-start(f32[256]{0:T(256)S(1)} %multiply_multiply_fusion.10) | copy-start | bytes 3076
  522.3 24.4 %collective-permute-start.31 = (bf16[4,128,768]{1,2,0:T(8,128)(2,1)}, bf16[4,128,768]{1,2,0:T(8,128)(2,1)}, u32[]{:S(2)}, u32[]{:S(2)}) collective-permute-start(bf16[4,128,768]{1,2,0:T(8,128)(2,1)} %bitcast.226), channel_id=1, source_target_pairs={{0,1},{1,0},{2,3},{3,2},{4,5},{5,4},{6,7},{7,6},{8,9},{9,8},{10,11... | collective-permute-start | bytes 2359304 | tf_op jit(solution)/shard_map/ppermute | solution.py:929
  527.5 24.2 %collective-permute-start.9 = (bf16[128,1024]{1,0:T(8,128)(2,1)S(1)}, bf16[128,1024]{1,0:T(8,128)(2,1)S(1)}, u32[]{:S(2)}, u32[]{:S(2)}) collective-permute-start(bf16[128,1024]{1,0:T(8,128)(2,1)S(1)} %copy-done.42), channel_id=1, source_target_pairs={{0,0},{1,4},{2,1},{3,5},{4,8},{5,12},{6,9},{7,13},{8,2},{9,6},{10,... | collective-permute-start | bytes 786440 | tf_op jit(solution)/shard_map/ppermute | solution.py:921
  546.7 9.3 %collective-permute-start.39 = (bf16[128,512]{1,0:T(8,128)(2,1)S(1)}, bf16[128,512]{1,0:T(8,128)(2,1)S(1)}, u32[]{:S(2)}, u32[]{:S(2)}) collective-permute-start(bf16[128,512]{1,0:T(8,128)(2,1)S(1)} %copy-done.45), channel_id=1, source_target_pairs={{0,8},{8,0},{1,9},{9,1},{2,10},{10,2},{3,11},{11,3},{4,12},{12,4},... | collective-permute-start | bytes 393224 | tf_op jit(solution)/shard_map/ppermute | solution.py:925
  548.9 211.6 %reduce-scatter.12.cloned.1.call-start = ((), (), s32[]{:S(2)}) async-start(), calls=%async_computation.9 | async-start | bytes 1310720 | tf_op jit(solution)/shard_map/reduce_scatter | solution.py:1092
  551.1 5.0 collective-permute-start.16
  551.7 26.4 %collective-permute-start.43 = (bf16[4,128,1024]{2,1,0:T(8,128)(2,1)S(1)}, bf16[4,128,1024]{2,1,0:T(8,128)(2,1)S(1)}, u32[]{:S(2)}, u32[]{:S(2)}) collective-permute-start(bf16[4,128,1024]{2,1,0:T(8,128)(2,1)S(1)} %fusion.25), channel_id=1, source_target_pairs={{0,1},{1,0},{2,3},{3,2},{4,5},{5,4},{6,7},{7,6},{8,9},{9,8},{10,11... | collective-permute-start | bytes 3145736 | tf_op jit(solution)/shard_map/ppermute | solution.py:929
  556.8 27.4 %collective-permute-start.24 = (bf16[512,256]{1,0:T(8,128)(2,1)S(1)}, bf16[512,256]{1,0:T(8,128)(2,1)S(1)}, u32[]{:S(2)}, u32[]{:S(2)}) collective-permute-start(bf16[512,256]{1,0:T(8,128)(2,1)S(1)} %constant_dynamic-slice_fusion.13), channel_id=1, source_target_pairs={{0,1},{1,0},{2,3},{3,2},{4,5},{5,4},{6,7},{7,6},{8,9},{9,8},{10,11... | collective-permute-start | bytes 786440 | tf_op jit(solution)/shard_map/ppermute | solution.py:929
  579.5 192.1 %reduce-scatter.6.cloned.1.call-start = ((), (), s32[]{:S(2)}) async-start(), calls=%async_computation.6 | async-start | bytes 2621440 | tf_op jit(solution)/shard_map/reduce_scatter | solution.py:1128
  584.4 9.3 %collective-permute-start.25 = (bf16[1024,128]{1,0:T(8,128)(2,1)S(1)}, bf16[1024,128]{1,0:T(8,128)(2,1)S(1)}, u32[]{:S(2)}, u32[]{:S(2)}) collective-permute-start(bf16[1024,128]{1,0:T(8,128)(2,1)S(1)} %fusion.60), channel_id=1, source_target_pairs={{0,16},{16,0},{1,17},{17,1},{2,18},{18,2},{3,19},{19,3},{4,20},{20... | collective-permute-start | bytes 786440 | tf_op jit(solution)/shard_map/ppermute | solution.py:933
  587.3 81.7 %collective-permute-start.48 = (bf16[4096,256]{1,0:T(8,128)(2,1)}, bf16[4096,256]{1,0:T(8,128)(2,1)}, u32[]{:S(2)}, u32[]{:S(2)}) collective-permute-start(bf16[4096,256]{1,0:T(8,128)(2,1)} %constant_dynamic-slice_fusion.1), channel_id=1, source_target_pairs={{0,16},{16,0},{1,17},{17,1},{2,18},{18,2},{3,19},{19,3},{4,20},{20... | collective-permute-start | bytes 6291464 | tf_op jit(solution)/shard_map/ppermute | solution.py:933
  617.5 163.3 %reduce-scatter.14.cloned.1.call-start = ((), (), s32[]{:S(2)}) async-start(), calls=%async_computation.10 | async-start | bytes 1310720 | tf_op jit(solution)/shard_map/reduce_scatter | solution.py:1092
  618.9 4.4 collective-permute-start.17
  674.2 57.7 %collective-permute-start.49 = (bf16[4,512,256]{2,1,0:T(8,128)(2,1)}, bf16[4,512,256]{2,1,0:T(8,128)(2,1)S(1)}, u32[]{:S(2)}, u32[]{:S(2)}) collective-permute-start(bf16[4,512,256]{2,1,0:T(8,128)(2,1)} %fusion.26), channel_id=1, source_target_pairs={{0,1},{1,0},{2,3},{3,2},{4,5},{5,4},{6,7},{7,6},{8,9},{9,8},{10,11... | collective-permute-start | bytes 3145736 | tf_op jit(solution)/shard_map/ppermute | solution.py:929
  676.5 50.9 %collective-permute-start.18 = (bf16[256,512]{1,0:T(8,128)(2,1)S(1)}, bf16[256,512]{1,0:T(8,128)(2,1)S(1)}, u32[]{:S(2)}, u32[]{:S(2)}) collective-permute-start(bf16[256,512]{1,0:T(8,128)(2,1)S(1)} %constant_dynamic-slice_fusion.14), channel_id=1, source_target_pairs={{0,8},{8,0},{1,9},{9,1},{2,10},{10,2},{3,11},{11,3},{4,12},{12,4},... | collective-permute-start | bytes 786440 | tf_op jit(solution)/shard_map/ppermute | solution.py:925
  727.6 10.5 %collective-permute-start.19 = (bf16[128,1024]{1,0:T(8,128)(2,1)S(1)}, bf16[128,1024]{1,0:T(8,128)(2,1)S(1)}, u32[]{:S(2)}, u32[]{:S(2)}) collective-permute-start(bf16[128,1024]{1,0:T(8,128)(2,1)S(1)} %get-tuple-element.178), channel_id=1, source_target_pairs={{0,0},{1,4},{2,1},{3,5},{4,8},{5,12},{6,9},{7,13},{8,2},{9,6},{10,... | collective-permute-start | bytes 786440 | tf_op jit(solution)/shard_map/ppermute | solution.py:921
  728.3 31.1 %collective-permute-start.20 = (bf16[128,1024]{1,0:T(8,128)(2,1)S(1)}, bf16[128,1024]{1,0:T(8,128)(2,1)S(1)}, u32[]{:S(2)}, u32[]{:S(2)}) collective-permute-start(bf16[128,1024]{1,0:T(8,128)(2,1)S(1)} %get-tuple-element.179), channel_id=1, source_target_pairs={{0,1},{1,5},{2,0},{3,4},{4,9},{5,13},{6,8},{7,12},{8,3},{9,7},{10,... | collective-permute-start | bytes 786440 | tf_op jit(solution)/shard_map/ppermute | solution.py:921
  735.9 24.6 %collective-permute-start.32 = (bf16[128,768]{0,1:T(8,128)(2,1)}, bf16[128,768]{0,1:T(8,128)(2,1)S(1)}, u32[]{:S(2)}, u32[]{:S(2)}) collective-permute-start(bf16[128,768]{0,1:T(8,128)(2,1)} %bitcast.231), channel_id=1, source_target_pairs={{0,16},{16,0},{1,17},{17,1},{2,18},{18,2},{3,19},{19,3},{4,20},{20... | collective-permute-start | bytes 589832 | tf_op jit(solution)/shard_map/ppermute | solution.py:933
  760.5 7.9 collective-permute-start.44
  761.5 19.0 %collective-permute-start.33 = (bf16[128,1536]{0,1:T(8,128)(2,1)S(1)}, bf16[128,1536]{0,1:T(8,128)(2,1)S(1)}, u32[]{:S(2)}, u32[]{:S(2)}) collective-permute-start(bf16[128,1536]{0,1:T(8,128)(2,1)S(1)} %pad_maximum_fusion.18), channel_id=1, source_target_pairs={{0,8},{8,0},{1,9},{9,1},{2,10},{10,2},{3,11},{11,3},{4,12},{12,4},... | collective-permute-start | bytes 1179656 | tf_op jit(solution)/shard_map/ppermute | solution.py:925
  770.3 33.7 %collective-permute-start.45 = (bf16[128,2048]{1,0:T(8,128)(2,1)}, bf16[128,2048]{1,0:T(8,128)(2,1)}, u32[]{:S(2)}, u32[]{:S(2)}) collective-permute-start(bf16[128,2048]{1,0:T(8,128)(2,1)} %pad_maximum_fusion.16), channel_id=1, source_target_pairs={{0,8},{8,0},{1,9},{9,1},{2,10},{10,2},{3,11},{11,3},{4,12},{12,4},... | collective-permute-start | bytes 1572872 | tf_op jit(solution)/shard_map/ppermute | solution.py:925
  772.5 14.5 %collective-permute-start.26 = (bf16[128,1024]{1,0:T(8,128)(2,1)S(1)}, bf16[128,1024]{1,0:T(8,128)(2,1)S(1)}, u32[]{:S(2)}, u32[]{:S(2)}) collective-permute-start(bf16[128,1024]{1,0:T(8,128)(2,1)S(1)} %dynamic-slice_bitcast_fusion), channel_id=1, source_target_pairs={{0,1},{1,0},{2,3},{3,2},{4,5},{5,4},{6,7},{7,6},{8,9},{9,8},{10,11... | collective-permute-start | bytes 786440 | tf_op jit(solution)/shard_map/ppermute | solution.py:929
  780.7 14.1 %collective-permute-start.50 = (bf16[512,256]{1,0:T(8,128)(2,1)}, bf16[512,256]{1,0:T(8,128)(2,1)}, u32[]{:S(2)}, u32[]{:S(2)}) collective-permute-start(bf16[512,256]{1,0:T(8,128)(2,1)} %bitcast.230), channel_id=1, source_target_pairs={{0,16},{16,0},{1,17},{17,1},{2,18},{18,2},{3,19},{19,3},{4,20},{20... | collective-permute-start | bytes 786440 | tf_op jit(solution)/shard_map/ppermute | solution.py:933
  788.9 13.7 %collective-permute-start.27 = (bf16[2,128,1024]{2,1,0:T(8,128)(2,1)}, bf16[2,128,1024]{2,1,0:T(8,128)(2,1)}, u32[]{:S(2)}, u32[]{:S(2)}) collective-permute-start(bf16[2,128,1024]{2,1,0:T(8,128)(2,1)} %pad_maximum_fusion.15), channel_id=1, source_target_pairs={{0,16},{16,0},{1,17},{17,1},{2,18},{18,2},{3,19},{19,3},{4,20},{20... | collective-permute-start | bytes 1572872 | tf_op jit(solution)/shard_map/ppermute | solution.py:933
  795.9 10.8 %collective-permute-start.51 = (bf16[512,512]{1,0:T(8,128)(2,1)S(1)}, bf16[512,512]{1,0:T(8,128)(2,1)S(1)}, u32[]{:S(2)}, u32[]{:S(2)}) collective-permute-start(bf16[512,512]{1,0:T(8,128)(2,1)S(1)} %pad_maximum_fusion.17), channel_id=1, source_target_pairs={{0,8},{8,0},{1,9},{9,1},{2,10},{10,2},{3,11},{11,3},{4,12},{12,4},... | collective-permute-start | bytes 1572872 | tf_op jit(solution)/shard_map/ppermute | solution.py:925
  803.9 4.7 collective-permute-start.28
  (58 other events, 516.9 us)
Sparse Core Ops, SparseCore 0:
  233.0 120.8 all-reduce.4
Sparse Core Ops, SparseCore 1:
  408.6 20.6 reduce-scatter.9
  549.0 22.2 reduce-scatter.7
  579.6 25.8 reduce-scatter.11
  617.5 42.1 reduce-scatter.5
  734.8 33.4 reduce-scatter.13

commit v2 on v0

--- a/solution.py
+++ b/solution.py
@@ -4,12 +4,18 @@
 import jax
 import jax.numpy as jnp
 from jax import lax
-from jax.sharding import PartitionSpec as P
+from jax.experimental import pallas as pl
+from jax.experimental.pallas import tpu as pltpu
+from jax.sharding import Mesh, PartitionSpec as P
 
 HEADS = 16
 GROUPS = 16
 KERNEL = 128
 VOCAB = 32
+TAP_BLOCKS = 33
+VMEM_LIMIT = 56 * 1024 * 1024
+DW_UNROLL = 11
+COST_SHARE = 0.001
 
 
 epsilon = 1e-05
@@ -471,7 +477,7 @@
     )
 
 
-def solution(mesh):
+def whole_solution(mesh):
     placed = (
         P("dp", "seq", None),
         P("dp", None),
@@ -508,3 +514,1499 @@
         ),
         check_vma=False,
     )
+
+
+def cost(flops, bytes_accessed, transcendentals):
+    return pl.CostEstimate(
+        flops=int(flops * COST_SHARE), bytes_accessed=int(bytes_accessed * COST_SHARE), transcendentals=int(transcendentals * COST_SHARE)
+    )
+
+
+def lanes_dot(a, b):
+    return lax.dot_general(a, b, (((1,), (1,)), ((), ())), preferred_element_type=jnp.float32)
+
+
+def rows_dot(a, b):
+    return lax.dot_general(a, b, (((0,), (0,)), ((), ())), preferred_element_type=jnp.float32)
+
+
+def attend_parts(side, queries, keys, values, allowed, low):
+    mine = low if side == 0 else jnp.logical_not(low)
+    scores = lanes_dot(jnp.where(mine, keys, jnp.zeros_like(keys)), queries)
+    scores = jnp.where(allowed, scores, masked_score)
+    top = jnp.max(scores, axis=0, keepdims=True)
+    return scores, top
+
+
+def attend_kernel(seg_q_ref, seg_k_ref, q_ref, k_ref, v_ref, mixed_ref, state_ref):
+    queries = q_ref[...] * jnp.bfloat16(0.125)
+    low = lax.broadcasted_iota(jnp.int32, k_ref.shape, 1) < 64
+    allowed = seg_k_ref[...] == seg_q_ref[...]
+    for side in range(2):
+        scores, top = attend_parts(side, queries, k_ref[...], None, allowed, low)
+        weights = jnp.exp(scores - top)
+        state_ref[0, side : side + 1, :] = top
+        state_ref[0, side + 2 : side + 3, :] = jnp.sum(weights, axis=0, keepdims=True)
+        mixed = rows_dot(v_ref[...], weights.astype(jnp.bfloat16))
+        mixed_ref[side * 64 : (side + 1) * 64, :] = mixed[side * 64 : (side + 1) * 64, :]
+
+
+def attend_far_kernel(seg_q_ref, seg_k_ref, q_ref, k_ref, v_ref, mixed_ref, state_ref, out_ref, low_ref, away_ref, lse_ref):
+    queries = q_ref[...] * jnp.bfloat16(0.125)
+    low = lax.broadcasted_iota(jnp.int32, k_ref.shape, 1) < 64
+    allowed = seg_k_ref[...] == seg_q_ref[...]
+    pieces = []
+    for side in range(2):
+        scores, top = attend_parts(side, queries, k_ref[...], None, allowed, low)
+        near_top = state_ref[0, side : side + 1, :]
+        top = jnp.maximum(top, near_top)
+        weights = jnp.exp(scores - top)
+        rescale = jnp.exp(near_top - top)
+        total = state_ref[0, side + 2 : side + 3, :] * rescale + jnp.sum(weights, axis=0, keepdims=True)
+        mixed = rows_dot(v_ref[...], weights.astype(jnp.bfloat16))[side * 64 : (side + 1) * 64, :]
+        pieces.append((mixed + mixed_ref[side * 64 : (side + 1) * 64, :] * rescale) / total)
+        lse_ref[0, side : side + 1, :] = top + jnp.log(total)
+    attended = jnp.concatenate(pieces, axis=0).T
+    own = low_ref.shape[0]
+    out_ref[...] = attended
+    low_ref[...] = attended[:own, :].astype(jnp.bfloat16)
+    away_ref[...] = attended[own:, :].astype(jnp.bfloat16)
+
+
+def attend_specs(frames, length, pairs):
+    return [
+        pl.BlockSpec((1, frames), lambda p: (0, 0)),
+        pl.BlockSpec((length, 1), lambda p: (0, 0)),
+        pl.BlockSpec((frames, 128), lambda p: (0, p)),
+        pl.BlockSpec((length, 128), lambda p: (0, p)),
+        pl.BlockSpec((length, 128), lambda p: (0, pairs + p)),
+    ]
+
+
+def attend_cost(frames, length, pairs, products):
+    return cost(
+        flops=4 * products * pairs * frames * length * 128,
+        bytes_accessed=16 * frames * pairs * 128,
+        transcendentals=2 * pairs * frames * length,
+    )
+
+
+def attend_near(queries, pair, seg_q, seg_k):
+    frames, width = queries.shape
+    length = pair.shape[0]
+    pairs = width // 128
+    return pl.pallas_call(
+        attend_kernel,
+        grid=(pairs,),
+        in_specs=attend_specs(frames, length, pairs),
+        out_specs=[
+            pl.BlockSpec((128, frames), lambda p: (p, 0)),
+            pl.BlockSpec((1, 8, frames), lambda p: (p, 0, 0)),
+        ],
+        out_shape=[
+            jax.ShapeDtypeStruct((width, frames), jnp.float32),
+            jax.ShapeDtypeStruct((pairs, 8, frames), jnp.float32),
+        ],
+        compiler_params=pltpu.CompilerParams(vmem_limit_bytes=VMEM_LIMIT),
+        cost_estimate=attend_cost(frames, length, pairs, 2),
+        name="attend_near",
+    )(seg_q.reshape(1, -1), seg_k.reshape(-1, 1), queries, pair, pair)
+
+
+def attend_far(queries, pair, seg_q, seg_k, mixed, state):
+    frames, width = queries.shape
+    length = pair.shape[0]
+    pairs = width // 128
+    return pl.pallas_call(
+        attend_far_kernel,
+        grid=(pairs,),
+        in_specs=attend_specs(frames, length, pairs)
+        + [
+            pl.BlockSpec((128, frames), lambda p: (p, 0)),
+            pl.BlockSpec((1, 8, frames), lambda p: (p, 0, 0)),
+        ],
+        out_specs=[
+            pl.BlockSpec((frames, 128), lambda p: (0, p)),
+            pl.BlockSpec((frames // 2, 128), lambda p: (0, p)),
+            pl.BlockSpec((frames // 2, 128), lambda p: (0, p)),
+            pl.BlockSpec((1, 8, frames), lambda p: (p, 0, 0)),
+        ],
+        out_shape=[
+            jax.ShapeDtypeStruct((frames, width), jnp.float32),
+            jax.ShapeDtypeStruct((frames // 2, width), jnp.bfloat16),
+            jax.ShapeDtypeStruct((frames // 2, width), jnp.bfloat16),
+            jax.ShapeDtypeStruct((pairs, 8, frames), jnp.float32),
+        ],
+        compiler_params=pltpu.CompilerParams(vmem_limit_bytes=VMEM_LIMIT),
+        cost_estimate=attend_cost(frames, length, pairs, 2),
+        name="attend_far",
+    )(seg_q.reshape(1, -1), seg_k.reshape(-1, 1), queries, pair, pair, mixed, state)
+
+
+def attend_back_kernel(seg_q_ref, seg_k_ref, q_ref, k_ref, v_ref, g_ref, a_ref, lse_ref, after_ref, dq_ref, dkv_ref):
+    queries = q_ref[...] * jnp.bfloat16(0.125)
+    key_count = k_ref.shape[0]
+    low = lax.broadcasted_iota(jnp.int32, (key_count, 128), 1) < 64
+    keys, values, grads = k_ref[...], v_ref[...], g_ref[...]
+    allowed = seg_k_ref[...] == seg_q_ref[...]
+    products = (grads.astype(jnp.float32) * a_ref[...]).T
+    dq, dk, dv = [], [], []
+    for side in range(2):
+        mine = low if side == 0 else jnp.logical_not(low)
+        zero = jnp.zeros_like(keys)
+        scores = lanes_dot(jnp.where(mine, keys, zero), queries)
+        probs = jnp.where(allowed, jnp.exp(scores - lse_ref[0, side : side + 1, :]), 0.0)
+        dots = jnp.sum(products[side * 64 : (side + 1) * 64, :], axis=0, keepdims=True)
+        dv.append(jnp.dot(probs.astype(jnp.bfloat16), grads, preferred_element_type=jnp.float32))
+        grad_probs = lanes_dot(jnp.where(mine, values, zero), grads)
+        grad_scores = (probs * (grad_probs - dots)).astype(jnp.bfloat16)
+        dk.append(jnp.dot(grad_scores, queries, preferred_element_type=jnp.float32))
+        dq.append(rows_dot(keys, grad_scores)[side * 64 : (side + 1) * 64, :])
+    dq_ref[...] = 0.125 * jnp.concatenate(dq, axis=0).T
+    dkv_ref[0] = jnp.where(low, dk[0], dk[1]).astype(dkv_ref.dtype)
+    dkv_ref[1] = jnp.where(low, dv[0], dv[1]).astype(dkv_ref.dtype)
+
+
+def attend_back(queries, pair, grads, attended, lse, seg_q, seg_k, kind, after):
+    frames, width = queries.shape
+    length = pair.shape[0]
+    pairs = width // 128
+    return pl.pallas_call(
+        attend_back_kernel,
+        grid=(pairs,),
+        in_specs=attend_specs(frames, length, pairs)
+        + [
+            pl.BlockSpec((frames, 128), lambda p: (0, p)),
+            pl.BlockSpec((frames, 128), lambda p: (0, p)),
+            pl.BlockSpec((1, 8, frames), lambda p: (p, 0, 0)),
+            pl.BlockSpec(memory_space=pl.ANY),
+        ],
+        out_specs=[
+            pl.BlockSpec((frames, 128), lambda p: (0, p)),
+            pl.BlockSpec((2, length, 128), lambda p: (0, 0, p)),
+        ],
+        out_shape=[
+            jax.ShapeDtypeStruct((frames, width), jnp.float32),
+            jax.ShapeDtypeStruct((2, length, width), kind),
+        ],
+        compiler_params=pltpu.CompilerParams(vmem_limit_bytes=VMEM_LIMIT),
+        cost_estimate=attend_cost(frames, length, pairs, 5),
+        name="attend_back",
+    )(seg_q.reshape(1, -1), seg_k.reshape(-1, 1), queries, pair, pair, grads, attended, lse, after)
+
+
+def phi_parts(values):
+    below = 0.5 * (1.0 + lax.erf(values * (0.5**0.5)))
+    density = jnp.exp(-0.5 * values * values) * (1.0 / math.sqrt(2.0 * math.pi))
+    return below, density
+
+
+def norm_parts(values):
+    center = values - jnp.mean(values, axis=-1, keepdims=True)
+    scale = lax.rsqrt(jnp.mean(center * center, axis=-1, keepdims=True) + epsilon)
+    return center * scale, scale
+
+
+def norm_back(grad, hat, scale, gain):
+    inner = grad * gain
+    mean_inner = jnp.mean(inner, axis=-1, keepdims=True)
+    mean_hat = jnp.mean(inner * hat, axis=-1, keepdims=True)
+    return (inner - mean_inner - hat * mean_hat) * scale
+
+
+def column_sum(values):
+    return jnp.sum(values, axis=0, keepdims=True)
+
+
+def by_core(core, mine, other):
+    return jnp.where(core == 0, mine, other), jnp.where(core == 0, other, mine)
+
+
+def mix_kernel(first, meta, *refs):
+    if first:
+        mine_ref, other_ref, gain_ref, shift_ref, w_ref, bias_ref, theirs_ref, ours_ref, normed_ref, position_ref = refs
+    else:
+        normed_ref, w_ref, bias_ref, theirs_ref, ours_ref = refs
+    step = pl.program_id(0)
+    half = w_ref.shape[1]
+    if first:
+
+        @pl.when(step == 0)
+        def _():
+            left, right = by_core(meta[0], mine_ref[...], other_ref[...])
+            position_ref[:, :half] = left
+            position_ref[:, half:] = right
+            hat, _ = norm_parts(position_ref[...])
+            normed_ref[...] = (hat * gain_ref[...] + shift_ref[...]).astype(jnp.bfloat16)
+
+    block = jnp.dot(normed_ref[...], w_ref[...], preferred_element_type=jnp.float32) + bias_ref[...]
+    block = block.astype(jnp.bfloat16)
+    parts = theirs_ref.shape[1] // half
+
+    @pl.when(step < parts)
+    def _():
+        theirs_ref[:, pl.ds(pl.multiple_of(step * half, half), half)] = block
+
+    @pl.when(step >= parts)
+    def _():
+        ours_ref[:, pl.ds(pl.multiple_of((step - parts) * half, half), half)] = block
+
+
+def mix_rows(core, sources, weight, bias, begin, parts):
+    first = len(sources) > 1
+    tokens = sources[0].shape[0]
+    features = weight.shape[0]
+    half = features // 2
+
+    def column(i, meta):
+        return 2 * (begin + i % parts) + jnp.where(i < parts, 1 - meta[0], meta[0])
+
+    whole = lambda shape: pl.BlockSpec(shape, lambda i, meta: (0, 0))
+    out_specs = [whole((tokens, parts * half))] * 2
+    out_shape = [jax.ShapeDtypeStruct((tokens, parts * half), jnp.bfloat16)] * 2
+    if first:
+        out_specs = out_specs + [whole((tokens, features))] * 2
+        out_shape = out_shape + [jax.ShapeDtypeStruct((tokens, features), kind) for kind in (jnp.bfloat16, jnp.float32)]
+    return pl.pallas_call(
+        partial(mix_kernel, first),
+        grid_spec=pltpu.PrefetchScalarGridSpec(
+            num_scalar_prefetch=1,
+            grid=(2 * parts,),
+            in_specs=[whole(item.shape) for item in sources]
+            + [
+                pl.BlockSpec((features, half), lambda i, meta: (0, column(i, meta))),
+                pl.BlockSpec((1, half), lambda i, meta: (0, column(i, meta))),
+            ],
+            out_specs=out_specs,
+        ),
+        out_shape=out_shape,
+        compiler_params=pltpu.CompilerParams(vmem_limit_bytes=VMEM_LIMIT, dimension_semantics=("arbitrary",)),
+        cost_estimate=cost(
+            flops=4 * parts * tokens * half * features, bytes_accessed=4 * parts * half * features, transcendentals=0
+        ),
+        name="norm_keys_values" if first else "queries",
+    )(core, *sources, weight, bias)
+
+
+def unmix_kernel(
+    meta, mine_ref, other_ref, w_ref, position_ref, resid_ref, gain_ref, *refs
+):
+    ours_ref, theirs_ref, sums_ref, total = refs[-4:]
+    step = pl.program_id(0)
+    half = theirs_ref.shape[1]
+
+    @pl.when(step == 0)
+    def _():
+        total[...] = jnp.zeros_like(total)
+
+    block = jnp.where(step < 3, mine_ref[...], other_ref[...])
+    total[...] += lanes_dot(block, w_ref[...])
+
+    @pl.when(step == 5)
+    def _():
+        grad = total[...]
+        hat, scale = norm_parts(position_ref[...])
+        sums_ref[0:1, :] = column_sum(grad * hat)
+        sums_ref[1:2, :] = column_sum(grad)
+        sums_ref[2:8, :] = jnp.zeros((6, 2 * half), jnp.float32)
+        result = resid_ref[...] + norm_back(grad, hat, scale, gain_ref[...])
+        low_half, high_half = result[:, :half], result[:, half:]
+        ours_ref[...] = jnp.where(meta[0] == 0, low_half, high_half)
+        theirs_ref[...] = jnp.where(meta[0] == 0, high_half, low_half)
+
+
+def unmix_rows(core, mine, other, weight, position, grad_resid, gain, after):
+    tokens, features = position.shape
+    half = features // 2
+
+    def column(i, meta):
+        return 2 * (i % 3) + jnp.where(i < 3, meta[0], 1 - meta[0])
+
+    whole = lambda shape: pl.BlockSpec(shape, lambda i, meta: (0, 0))
+    return pl.pallas_call(
+        unmix_kernel,
+        grid_spec=pltpu.PrefetchScalarGridSpec(
+            num_scalar_prefetch=1,
+            grid=(6,),
+            in_specs=[
+                pl.BlockSpec((tokens, half), lambda i, meta: (0, i % 3)),
+                pl.BlockSpec((tokens, half), lambda i, meta: (0, i % 3)),
+                pl.BlockSpec((features, half), lambda i, meta: (0, column(i, meta))),
+                whole((tokens, features)),
+                whole((tokens, features)),
+                whole((1, features)),
+            ]
+            + [pl.BlockSpec(memory_space=pl.ANY)] * len(after),
+            out_specs=[whole((tokens, half)), whole((tokens, half)), whole((8, features))],
+            scratch_shapes=[pltpu.VMEM((tokens, features), jnp.float32)],
+        ),
+        out_shape=[
+            jax.ShapeDtypeStruct((tokens, half), jnp.float32),
+            jax.ShapeDtypeStruct((tokens, half), jnp.float32),
+            jax.ShapeDtypeStruct((8, features), jnp.float32),
+        ],
+        compiler_params=pltpu.CompilerParams(vmem_limit_bytes=VMEM_LIMIT, dimension_semantics=("arbitrary",)),
+        cost_estimate=cost(flops=12 * tokens * half * features, bytes_accessed=14 * half * features, transcendentals=0),
+        name="qkv_and_norm_back",
+    )(core, mine, other, weight, position, grad_resid, gain, *after)
+
+
+def pack_places(features, width):
+    places, at = {}, 0
+    for name, size in (
+        ("active", width), ("second", features), ("attended", features), ("up", width // 2),
+        ("out", features // 2), ("branch", features // 2),
+    ):
+        places[name] = at
+        at += size
+    places["all"] = at
+    return places
+
+
+def middle_kernel(
+    meta, mine_ref, other_ref, position_ref, w_out_ref, w_up_ref, w_down_ref, up_bias_ref, head_w_ref, head_b_ref,
+    labels_ref, rows_ref, after_a, after_b,
+    pack_ref, output_ref, out_low_ours, up_ours, branch_ours, att_ours, att_theirs, resid_grad_ref, sums_ref,
+    up_sums_ref, head_ref, last_ref,
+    resid, total, slope, grad_out, grad_low,
+):
+    step = pl.program_id(0)
+    chunks = slope.shape[0]
+    core = meta[0]
+    half = mine_ref.shape[1]
+    features = 2 * half
+    chunk_width = slope.shape[2]
+    places = pack_places(features, chunks * chunk_width)
+
+    def at(name, size):
+        return slice(places[name], places[name] + size)
+
+    second_at, attended_at = at("second", features), at("attended", features)
+
+    def store_halves(ours, theirs, values):
+        low_half, high_half = values[:, :half], values[:, half:]
+        ours[...] = jnp.where(core == 0, low_half, high_half)
+        theirs[...] = jnp.where(core == 0, high_half, low_half)
+
+    @pl.when(step == 0)
+    def _():
+        left, right = by_core(core, mine_ref[...].astype(jnp.float32), other_ref[...].astype(jnp.float32))
+        pack_ref[:, places["attended"] : places["attended"] + half] = left.astype(jnp.bfloat16)
+        pack_ref[:, places["attended"] + half : places["attended"] + features] = right.astype(jnp.bfloat16)
+        resid[...] = (
+            position_ref[...]
+            + jnp.dot(pack_ref[:, attended_at], w_out_ref[...], preferred_element_type=jnp.float32)
+            + rows_ref[2:3, :]
+        )
+        hat, _ = norm_parts(resid[...])
+        pack_ref[:, second_at] = (hat * rows_ref[0:1, :] + rows_ref[1:2, :]).astype(jnp.bfloat16)
+        total[...] = jnp.zeros_like(total)
+
+    @pl.when(step < chunks)
+    def _():
+        raised = jnp.dot(pack_ref[:, second_at], w_up_ref[...], preferred_element_type=jnp.float32) + up_bias_ref[...]
+        below, density = phi_parts(raised)
+        slope[step] = below + raised * density
+        active = (raised * below).astype(jnp.bfloat16)
+        pack_ref[:, pl.ds(pl.multiple_of(places["active"] + step * chunk_width, chunk_width), chunk_width)] = active
+        total[...] += jnp.dot(active, w_down_ref[...], preferred_element_type=jnp.float32)
+
+    @pl.when(step == chunks - 1)
+    def _():
+        low = (resid[...] + total[...] + rows_ref[3:4, :]).astype(jnp.bfloat16)
+        output_ref[...] = low
+        logits = jnp.dot(low, head_w_ref[...], preferred_element_type=jnp.float32) + head_b_ref[...]
+        top = jnp.max(logits, axis=-1, keepdims=True)
+        shifted = jnp.exp(logits - top)
+        sums = jnp.sum(shifted, axis=-1, keepdims=True)
+        onehot = labels_ref[...] == lax.broadcasted_iota(jnp.int32, logits.shape, 1)
+        picked = jnp.sum(jnp.where(onehot, logits, 0.0), axis=-1, keepdims=True)
+        loss = jnp.sum(top + jnp.log(sums) - picked)
+        grad_logits = (shifted / sums - onehot.astype(jnp.float32)).astype(jnp.bfloat16)
+        head_ref[...] = rows_dot(grad_logits, low)
+        last_ref[...] = jnp.zeros_like(last_ref)
+        last_ref[0:1, 0:VOCAB] = column_sum(grad_logits.astype(jnp.float32))
+        last_ref[1:2, :] = jnp.full((1, 128), loss, jnp.float32)
+        grad = lanes_dot(grad_logits, head_w_ref[...])
+        grad_out[...] = grad
+        grad_low[...] = grad.astype(jnp.bfloat16)
+        store_halves(out_low_ours, pack_ref.at[:, at("out", half)], grad_low[...])
+        sums_ref[3:4, :] = column_sum(grad_low[...].astype(jnp.float32))
+        sums_ref[4:8, :] = jnp.zeros((4, 2 * half), jnp.float32)
+        total[...] = jnp.zeros_like(total)
+
+    @pl.when(step >= chunks)
+    def _():
+        chunk = 2 * chunks - 1 - step
+        grad = lanes_dot(grad_low[...], w_down_ref[...]) * slope[chunk]
+        low = grad.astype(jnp.bfloat16)
+        up_sums_ref[0] = jnp.broadcast_to(column_sum(low.astype(jnp.float32)), up_sums_ref.shape[1:])
+        total[...] += lanes_dot(low, w_up_ref[...])
+        ours = (chunk >= chunks // 2) == (core == 1)
+
+        @pl.when(ours)
+        def _():
+            up_ours[...] = low
+
+        @pl.when(jnp.logical_not(ours))
+        def _():
+            place = places["up"] + (chunk & (chunks // 2 - 1)) * chunk_width
+            pack_ref[:, pl.ds(pl.multiple_of(place, chunk_width), chunk_width)] = low
+
+    @pl.when(step == 2 * chunks - 1)
+    def _():
+        hat, scale = norm_parts(resid[...])
+        grad = total[...]
+        sums_ref[0:1, :] = column_sum(grad * hat)
+        sums_ref[2:3, :] = column_sum(grad)
+        result = grad_out[...] + norm_back(grad, hat, scale, rows_ref[0:1, :])
+        resid_grad_ref[...] = result
+        branch = result.astype(jnp.bfloat16)
+        store_halves(branch_ours, pack_ref.at[:, at("branch", half)], branch)
+        sums_ref[1:2, :] = column_sum(branch.astype(jnp.float32))
+        store_halves(att_ours, att_theirs, lanes_dot(branch, w_out_ref[...]).astype(jnp.bfloat16))
+
+
+def middle(core, mine, other, position, w_out, w_up, w_down, up_bias, head_w, head_b, labels, rows, after):
+    tokens, features = position.shape
+    half = features // 2
+    width = w_up.shape[1]
+    chunks = 8
+    chunk = width // chunks
+    vocab = head_w.shape[1]
+    last = 2 * chunks - 1
+
+    def part(i):
+        return jnp.where(i < chunks, i, last - i)
+
+    def own_up(i, meta):
+        back = part(jnp.maximum(i, chunks))
+        return jnp.where(meta[0] == 0, jnp.minimum(back, chunks // 2 - 1), jnp.maximum(back - chunks // 2, 0))
+
+    whole = lambda shape: pl.BlockSpec(shape, lambda i, meta: tuple(0 for _ in shape))
+    low = lambda *shape: jax.ShapeDtypeStruct(shape, jnp.bfloat16)
+    full = lambda *shape: jax.ShapeDtypeStruct(shape, jnp.float32)
+    return pl.pallas_call(
+        middle_kernel,
+        grid_spec=pltpu.PrefetchScalarGridSpec(
+            num_scalar_prefetch=1,
+            grid=(2 * chunks,),
+            in_specs=[
+                whole((tokens, half)),
+                whole((tokens, half)),
+                whole((tokens, features)),
+                whole((features, features)),
+                pl.BlockSpec((features, chunk), lambda i, meta: (0, part(i))),
+                pl.BlockSpec((chunk, features), lambda i, meta: (part(i), 0)),
+                pl.BlockSpec((1, chunk), lambda i, meta: (0, part(i))),
+                whole((features, vocab)),
+                whole((1, vocab)),
+                whole((tokens, 1)),
+                whole((8, features)),
+                pl.BlockSpec(memory_space=pl.ANY),
+                pl.BlockSpec(memory_space=pl.ANY),
+            ],
+            out_specs=[
+                whole((tokens, pack_places(features, width)["all"])),
+                whole((tokens, features)),
+                whole((tokens, half)),
+                pl.BlockSpec((tokens, chunk), lambda i, meta: (0, own_up(i, meta))),
+                whole((tokens, half)),
+                whole((tokens, half)),
+                whole((tokens, half)),
+                whole((tokens, features)),
+                whole((8, features)),
+                pl.BlockSpec((1, 8, chunk), lambda i, meta: (part(jnp.maximum(i, chunks)), 0, 0)),
+                whole((vocab, features)),
+                whole((8, 128)),
+            ],
+            scratch_shapes=[
+                pltpu.VMEM((tokens, features), jnp.float32),
+                pltpu.VMEM((tokens, features), jnp.float32),
+                pltpu.VMEM((chunks, tokens, chunk), jnp.float32),
+                pltpu.VMEM((tokens, features), jnp.float32),
+                pltpu.VMEM((tokens, features), jnp.bfloat16),
+            ],
+        ),
+        out_shape=[
+            low(tokens, pack_places(features, width)["all"]),
+            low(tokens, features),
+            low(tokens, half),
+            low(tokens, width // 2),
+            low(tokens, half),
+            low(tokens, half),
+            low(tokens, half),
+            full(tokens, features),
+            full(8, features),
+            full(chunks, 8, chunk),
+            full(vocab, features),
+            full(8, 128),
+        ],
+        compiler_params=pltpu.CompilerParams(vmem_limit_bytes=VMEM_LIMIT, dimension_semantics=("arbitrary",)),
+        cost_estimate=cost(
+            flops=8 * tokens * features * width, bytes_accessed=8 * features * width, transcendentals=2 * tokens * width
+        ),
+        name="middle",
+    )(core, mine, other, position, w_out, w_up, w_down, up_bias, head_w, head_b, labels, rows, *after)
+
+
+def conv_grad_kernel(meta, ours_ref, got_ref, slope_ref, *refs):
+    position_ref, grad_ref, edge_ref, own_ref, to_x_ref, to_y_ref, to_xy_ref, sums_ref = refs[-8:]
+    core, y, x = meta[0], meta[1], meta[2]
+    frames = ours_ref.shape[0]
+    rim = edge_ref.shape[0]
+    ours, got = ours_ref[...], got_ref[...]
+    position_ref[0:frames, :] = jnp.where(core == 0, ours, got)
+    position_ref[frames:, :] = jnp.where(core == 0, got, ours)
+    grad_ref[...] = (position_ref[...] * slope_ref[...]).astype(jnp.bfloat16)
+    edge_ref[...] = jnp.where(x == 0, grad_ref[2 * frames - rim :, :], grad_ref[0:rim, :])
+    sums_ref[...] = jnp.broadcast_to(column_sum(grad_ref[...].astype(jnp.float32)), sums_ref.shape)
+    for ref, yy, xx in ((own_ref, y, x), (to_x_ref, y, 1 - x), (to_y_ref, 1 - y, x), (to_xy_ref, 1 - y, 1 - x)):
+        ref[...] = grad_ref[:, pl.ds(pl.multiple_of(256 * xx + 128 * yy, 128), 128)]
+
+
+def conv_grad_rows(meta, ours, got, slope, after):
+    frames, half = ours.shape
+    operands = (ours, got, slope)
+    shapes = [((2 * frames, half), jnp.float32), ((2 * frames, half), jnp.bfloat16), ((KERNEL // 2, half), jnp.bfloat16)]
+    shapes += [((2 * frames, 128), jnp.bfloat16)] * 4 + [((8, half), jnp.float32)]
+    return pl.pallas_call(
+        conv_grad_kernel,
+        grid_spec=pltpu.PrefetchScalarGridSpec(
+            num_scalar_prefetch=1,
+            grid=(1,),
+            in_specs=[pl.BlockSpec(item.shape, lambda i, m: (0, 0)) for item in operands]
+            + [pl.BlockSpec(memory_space=pl.ANY)] * len(after),
+            out_specs=[pl.BlockSpec(shape, lambda i, m: (0, 0)) for shape, _ in shapes],
+        ),
+        out_shape=[jax.ShapeDtypeStruct(shape, kind) for shape, kind in shapes],
+        compiler_params=pltpu.CompilerParams(vmem_limit_bytes=VMEM_LIMIT, dimension_semantics=("arbitrary",)),
+        cost_estimate=cost(flops=0, bytes_accessed=4000000, transcendentals=0),
+        name="conv_grad_rows",
+    )(meta, *operands, *after)
+
+
+def weight_kernel(tasks, out_count, carries, meta, *refs):
+    refs = list(refs)
+    step = pl.program_id(0)
+    if carries:
+        carried_ref = refs.pop()
+        carry_ref = refs.pop(-1 - out_count)
+
+        @pl.when(step == 0)
+        def _():
+            carried_ref[...] = carry_ref[...]
+
+    inputs = []
+    for task in tasks:
+        inputs.append([refs.pop(0) for _ in range(5 if task["add"] is not None else 4)])
+    outs = refs[-out_count:]
+    begin = 0
+    for task, ins in zip(tasks, inputs):
+        rows, columns = task["rows"], task["columns"]
+
+        def store(where, values, at, task=task):
+            index, column = where
+            size = values.shape[0]
+            span = pl.ds(pl.multiple_of(at * size, size), size)
+            outs[index][span, column : column + values.shape[1]] = values.astype(jnp.bfloat16)
+
+        @pl.when(jnp.logical_and(step >= begin, step < begin + task["blocks"]))
+        def _(task=task, ins=ins, begin=begin, store=store, rows=rows, columns=columns):
+            total = rows_dot(ins[0][...], ins[2][...]) + rows_dot(ins[1][...], ins[3][...])
+            if task["add"] is not None:
+                total = total + ins[4][...].astype(jnp.float32)
+            at = step - begin + task["place"]
+            if task["split"] is None:
+                store(task["outs"][0], total, at)
+                return
+            if task["split"] == "columns":
+                first, second = total[:, : columns // 2], total[:, columns // 2 :]
+            else:
+                blocks = total.reshape(-1, 2, task["unit"], columns)
+                first, second = (blocks[:, k].reshape(rows // 2, columns) for k in range(2))
+            bit = task["bit"](meta)
+            store(task["outs"][0], jnp.where(bit == 0, second, first), at)
+            store(task["outs"][1], jnp.where(bit == 0, first, second), at)
+
+        begin = begin + task["blocks"]
+
+
+def weight_task(
+    outs, left, right, rows, blocks, row_of, columns, column_of, add=None, add_of=None, split=None, bit=None, unit=0, place=0
+):
+    return dict(
+        outs=outs, left=left, right=right, rows=rows, blocks=blocks, row_of=row_of, columns=columns,
+        column_of=column_of, add=add, add_of=add_of, split=split, bit=bit, unit=unit, place=place,
+    )
+
+
+def weight_parts(meta, tasks, shapes, name, after, carry=None):
+    in_specs, operands = [], []
+    begin, flops, moved = 0, 0, 0
+    for task in tasks:
+        rows, columns, blocks = task["rows"], task["columns"], task["blocks"]
+        tokens = task["left"][0][0].shape[0]
+
+        def local(i, begin=begin, blocks=blocks):
+            return jnp.clip(i - begin, 0, blocks - 1)
+
+        for array, base in task["left"]:
+            in_specs.append(
+                pl.BlockSpec(
+                    (tokens, rows), lambda i, m, t=task, local=local, base=base: (0, base // t["rows"] + t["row_of"](local(i), m))
+                )
+            )
+            operands.append(array)
+        for array, base in task["right"]:
+            in_specs.append(
+                pl.BlockSpec((tokens, columns), lambda i, m, t=task, base=base: (0, base // t["columns"] + t["column_of"](m)))
+            )
+            operands.append(array)
+        if task["add"] is not None:
+            in_specs.append(pl.BlockSpec((rows, columns), lambda i, m, t=task, local=local: t["add_of"](local(i), m)))
+            operands.append(task["add"])
+        begin += blocks
+        flops += 4 * tokens * rows * blocks * columns
+        moved += 2 * rows * blocks * columns + 4 * tokens * (rows * blocks + columns)
+    in_specs.append(pl.BlockSpec(memory_space=pl.ANY))
+    operands.append(after)
+    out_shapes = list(shapes)
+    if carry is not None:
+        in_specs.append(pl.BlockSpec(carry.shape, lambda i, m: (0, 0)))
+        operands.append(carry)
+        out_shapes.append(carry.shape)
+    return pl.pallas_call(
+        partial(weight_kernel, tasks, len(shapes), carry is not None),
+        grid_spec=pltpu.PrefetchScalarGridSpec(
+            num_scalar_prefetch=1,
+            grid=(begin,),
+            in_specs=in_specs,
+            out_specs=[pl.BlockSpec(shape, lambda i, m: (0, 0)) for shape in out_shapes],
+        ),
+        out_shape=[jax.ShapeDtypeStruct(shape, jnp.bfloat16) for shape in out_shapes],
+        compiler_params=pltpu.CompilerParams(vmem_limit_bytes=VMEM_LIMIT, dimension_semantics=("arbitrary",)),
+        cost_estimate=cost(flops=flops, bytes_accessed=moved, transcendentals=0),
+        name=name,
+    )(meta, *operands)
+
+
+def flip_kernel(meta, in_ref, out_ref):
+    out_ref[...] = in_ref[0].astype(jnp.float32).T
+
+
+def flip_columns(meta, pieces):
+    count, width, rows = pieces.shape
+
+    def column(i, m):
+        return 4 * (m[0] ^ (i >> 2)) + 2 * (i & 1) + (m[1] ^ ((i >> 1) & 1))
+
+    return pl.pallas_call(
+        flip_kernel,
+        grid_spec=pltpu.PrefetchScalarGridSpec(
+            num_scalar_prefetch=1,
+            grid=(count,),
+            in_specs=[pl.BlockSpec((1, width, rows), lambda i, m: (i, 0, 0))],
+            out_specs=pl.BlockSpec((rows, width), lambda i, m: (0, column(i, m))),
+        ),
+        out_shape=jax.ShapeDtypeStruct((rows, count * width), jnp.float32),
+        compiler_params=pltpu.CompilerParams(vmem_limit_bytes=VMEM_LIMIT, dimension_semantics=("arbitrary",)),
+        cost_estimate=cost(flops=0, bytes_accessed=6 * count * width * rows, transcendentals=0),
+        name="flip_columns",
+    )(meta, pieces)
+
+
+def small_kernel(meta, head_ref, mid_ref, first_ref, conv_ref, ours_ref, got_ref, up_ref, last_ref, after_ref, out_ref):
+    core = meta[0]
+    half = conv_ref.shape[1]
+    zero = jnp.zeros((1, half), jnp.float32)
+
+    def wide(left, right):
+        return jnp.concatenate([left, right], axis=1)
+
+    def halves(part):
+        ours = ours_ref[0:1, part * half : (part + 1) * half]
+        got = got_ref[0:1, part * half : (part + 1) * half]
+        return wide(jnp.where(core == 0, ours, got), jnp.where(core == 0, got, ours))
+
+    conv = conv_ref[0:1, :]
+    rows = jnp.concatenate(
+        [
+            mid_ref[0:4, :],
+            first_ref[0:2, :],
+            wide(jnp.where(core == 0, conv, zero), jnp.where(core == 0, zero, conv)),
+            halves(0),
+            halves(2),
+        ],
+        axis=0,
+    )
+    unit = out_ref.shape[2]
+    for j in range(8):
+        span = slice(j * unit, (j + 1) * unit)
+        out_ref[j, 0:VOCAB, :] = head_ref[:, span]
+        out_ref[j, VOCAB : VOCAB + 9, :] = rows[:, span]
+        for r in range(4):
+            out_ref[j, VOCAB + 9 + r : VOCAB + 10 + r, :] = up_ref[j, 0:1, r * unit : (r + 1) * unit]
+        out_ref[j, VOCAB + 13 : VOCAB + 15, :] = last_ref[0:2, :]
+        out_ref[j, VOCAB + 15 : VOCAB + 16, :] = last_ref[2:3, :]
+
+
+def small_sums(meta, head, mid, first, conv, ours, got, up, last, after):
+    operands = (head, mid, first, conv, ours, got, up, last)
+    return pl.pallas_call(
+        small_kernel,
+        grid_spec=pltpu.PrefetchScalarGridSpec(
+            num_scalar_prefetch=1,
+            grid=(1,),
+            in_specs=[pl.BlockSpec(item.shape, lambda i, m, n=item.ndim: (0,) * n) for item in operands]
+            + [pl.BlockSpec(memory_space=pl.ANY)],
+            out_specs=pl.BlockSpec((8, 48, 128), lambda i, m: (0, 0, 0)),
+        ),
+        out_shape=jax.ShapeDtypeStruct((8, 48, 128), jnp.float32),
+        compiler_params=pltpu.CompilerParams(vmem_limit_bytes=VMEM_LIMIT, dimension_semantics=("arbitrary",)),
+        cost_estimate=cost(flops=0, bytes_accessed=400000, transcendentals=0),
+        name="small_sums",
+    )(meta, *operands, after)
+
+
+def tile_lists(seg_ext, rise):
+    row_count = seg_ext.shape[0]
+    frames = seg_ext.shape[1] - KERNEL
+    tiles = frames // 64
+    center = seg_ext[:, KERNEL // 2 : KERNEL // 2 + frames].reshape(row_count, tiles, 64)
+    first = center[:, :, 0].reshape(-1)
+    counts = (center[:, :, 63].reshape(-1) - first + 1).astype(jnp.int32)
+    ends = jnp.cumsum(counts)
+    slots = row_count * (tiles + rise)
+    slot = jnp.arange(slots, dtype=jnp.int32)
+    tile = jnp.sum((slot[:, None] >= ends[None, :]).astype(jnp.int32), axis=1)
+    used = tile < row_count * tiles
+    tile = jnp.minimum(tile, row_count * tiles - 1)
+    onehot = tile[:, None] == jnp.arange(row_count * tiles, dtype=jnp.int32)[None, :]
+    begin = jnp.sum(jnp.where(onehot, (ends - counts)[None, :], 0), axis=1)
+    number = jnp.sum(jnp.where(onehot, first[None, :], 0), axis=1) + slot - begin
+    number = jnp.where(used, number, -2)
+    in_block = tile + (tile // tiles) * (KERNEL // 64)
+    return in_block.astype(jnp.int32), tile.astype(jnp.int32), number.astype(jnp.int32)
+
+
+def lane_low(rows):
+    return lax.broadcasted_iota(jnp.int32, (rows, 128), 1) < 64
+
+
+def half_roll(block):
+    return pltpu.roll(block, 64, 1)
+
+
+def quad_rows(src, rows, side):
+    low = lane_low(rows)
+    parts = [src[pl.ds(j, rows, stride=4), :] for j in range(4)]
+    halves = []
+    for a, b in ((0, 1), (2, 3)):
+        if side == 0:
+            halves.append(jnp.where(low, parts[a], half_roll(parts[b])))
+        else:
+            halves.append(jnp.where(low, half_roll(parts[a]), parts[b]))
+    return halves
+
+
+def conv_setup(meta, slots, seg_ref, flat, shifts, masks):
+    rows4 = seg_ref.shape[0]
+    blocks = rows4 // 16
+    one, zero = jnp.ones((16, 256), jnp.bfloat16), jnp.zeros((16, 256), jnp.bfloat16)
+    flat[0:rows4, :] = seg_ref[...]
+    flat[rows4:, :] = jnp.zeros((16, 256), jnp.float32)
+    for p in range(16):
+        shifts[p] = flat[pl.ds(p, rows4), :].astype(jnp.bfloat16).reshape(blocks, 16, 256)
+
+    @pl.loop(0, slots)
+    def _(v):
+        at = meta[1 + v]
+        number = jnp.full((16, 256), meta[1 + 2 * slots + v].astype(jnp.float32), jnp.float32).astype(jnp.bfloat16)
+        row = pl.multiple_of(v * 16, 16)
+        for b in range(TAP_BLOCKS):
+            ids = shifts[b % 16, at + b // 16]
+            masks[pl.ds(row, 16), b * 256 : (b + 1) * 256] = jnp.where(ids == number, one, zero)
+
+
+def conv_shifts(wide, side, flat, shifts):
+    rows4 = shifts.shape[1] * 16
+    halves = quad_rows(wide, rows4, side)
+    flat[0:rows4, 0:128] = halves[0]
+    flat[0:rows4, 128:256] = halves[1]
+    for p in range(16):
+        shifts[p] = flat[pl.ds(p, rows4), :].astype(jnp.bfloat16).reshape(rows4 // 16, 16, 256)
+
+
+def conv_patch(places, b, shifts, masks):
+    span = slice(b * 256, (b + 1) * 256)
+    pieces = [
+        shifts[b % 16, at + b // 16] * masks[v * 16 : (v + 1) * 16, span] for v, at in enumerate(places)
+    ]
+    return jnp.concatenate(pieces, axis=0)
+
+
+def conv_taps(w_ref, side, b, taps):
+    rows = 256
+    low = lane_low(rows)
+    depth = w_ref.shape[0]
+    zero = jnp.zeros((64, 128), jnp.bfloat16)
+    if b == 0:
+        here, before = w_ref[0:rows, :], jnp.concatenate([zero, w_ref[0 : rows - 64, :]], axis=0)
+    elif b * rows < depth:
+        here, before = w_ref[b * rows : (b + 1) * rows, :], w_ref[b * rows - 64 : (b + 1) * rows - 64, :]
+    else:
+        here, before = jnp.concatenate([zero] * 4, axis=0), jnp.concatenate([w_ref[depth - 64 :, :]] + [zero] * 3, axis=0)
+    block = jnp.where(low, here, half_roll(before)) if side == 0 else jnp.where(low, half_roll(here), before)
+    taps[128 + b * rows : 128 + (b + 1) * rows, :] = block
+    return jnp.concatenate([block, taps[b * rows : (b + 1) * rows, :]], axis=1)
+
+
+def conv_kernel(slots, backward, meta, x_ref, seg_ref, w_ref, extra_ref, *refs):
+    refs = refs[1:] if backward else refs
+    o_ref, *refs = refs
+    if backward:
+        wide, flat, shifts, masks, taps, sums, outs = refs
+    else:
+        slope_ref, wide, flat, shifts, masks, taps, sums, outs = refs
+
+    @pl.when(pl.program_id(0) == 0)
+    def _():
+        conv_setup(meta, slots, seg_ref, flat, shifts, masks)
+
+    wide[...] = x_ref[...].astype(jnp.float32)
+    taps[0:128, :] = jnp.zeros((128, 128), jnp.bfloat16)
+    out_rows = o_ref.shape[0] // 4
+    places = [meta[1 + v] for v in range(slots)]
+    for side in range(2):
+        conv_shifts(wide, side, flat, shifts)
+        total = jnp.zeros((256, slots * 16) if backward else (slots * 16, 256), jnp.float32)
+        for b in range(TAP_BLOCKS):
+            weight = conv_taps(w_ref, side, b, taps)
+            if backward:
+                total = total + lanes_dot(weight, conv_patch(places, TAP_BLOCKS - 1 - b, shifts, masks))
+            else:
+                total = total + jnp.dot(
+                    conv_patch(places, b, shifts, masks), weight, preferred_element_type=jnp.float32
+                )
+        sums[...] = total.T if backward else total
+
+        @pl.loop(0, slots)
+        def _(v):
+            to = pl.ds(pl.multiple_of(meta[1 + slots + v] * 16, 16), 16)
+            row = pl.ds(pl.multiple_of(v * 16, 16), 16)
+            keep = masks[row, 16 * 256 : 17 * 256].astype(jnp.float32) > 0.5
+            outs[side, to, :] = jnp.where(keep, sums[row, :], outs[side, to, :])
+
+    low = lane_low(out_rows)
+    for half in range(2):
+        zero_side = outs[0, :, half * 128 : (half + 1) * 128]
+        one_side = outs[1, :, half * 128 : (half + 1) * 128]
+        wide[pl.ds(2 * half, out_rows, stride=4), :] = jnp.where(low, zero_side, half_roll(one_side))
+        wide[pl.ds(2 * half + 1, out_rows, stride=4), :] = jnp.where(low, half_roll(zero_side), one_side)
+    result = wide[0 : 4 * out_rows, :]
+    if backward:
+        o_ref[...] = (extra_ref[...] + result).astype(o_ref.dtype)
+    else:
+        result = result + extra_ref[...]
+        below, density = phi_parts(result)
+        center = x_ref[KERNEL // 2 : KERNEL // 2 + 4 * out_rows, :].astype(jnp.float32)
+        o_ref[...] = center + result * below
+        slope_ref[...] = below + result * density
+
+
+def seg_quads(seg_ext):
+    quads = seg_ext.astype(jnp.float32).reshape(-1, 4)
+    return jnp.repeat(quads, 64, axis=1)
+
+
+def grouped_conv(x_ext, seg_ext, weight, extra, first_pair, rise, backward, after=None):
+    row_count, length, width = x_ext.shape
+    frames = length - KERNEL
+    pairs = width // 128
+    in_block, tile, number = tile_lists(seg_ext, rise)
+    slots = in_block.shape[0]
+    meta = jnp.concatenate([jnp.reshape(first_pair, (1,)).astype(jnp.int32), in_block, tile, number])
+    rows4 = row_count * length // 4
+    out4 = row_count * frames // 4
+    depth = TAP_BLOCKS * 256
+    return pl.pallas_call(
+        partial(conv_kernel, slots, backward),
+        grid_spec=pltpu.PrefetchScalarGridSpec(
+            num_scalar_prefetch=1,
+            grid=(pairs,),
+            in_specs=[
+                pl.BlockSpec((row_count * length, 128), lambda p, meta: (0, p)),
+                pl.BlockSpec((rows4, 256), lambda p, meta: (0, 0)),
+                pl.BlockSpec((weight.shape[0], 128), lambda p, meta: (0, meta[0] + p)),
+                pl.BlockSpec((extra.shape[0], 128), lambda p, meta: (0, p)),
+            ]
+            + [pl.BlockSpec(memory_space=pl.ANY)] * (1 if backward else 0),
+            out_specs=[pl.BlockSpec((row_count * frames, 128), lambda p, meta: (0, p))] * (1 if backward else 2),
+            scratch_shapes=[
+                pltpu.VMEM((row_count * length, 128), jnp.float32),
+                pltpu.VMEM((rows4 + 16, 256), jnp.float32),
+                pltpu.VMEM((16, rows4 // 16, 16, 256), jnp.bfloat16),
+                pltpu.VMEM((slots * 16, depth), jnp.bfloat16),
+                pltpu.VMEM((128 + depth, 128), jnp.bfloat16),
+                pltpu.VMEM((slots * 16, 256), jnp.float32),
+                pltpu.VMEM((2, out4, 256), jnp.float32),
+            ],
+        ),
+        out_shape=[jax.ShapeDtypeStruct((row_count * frames, width), jnp.bfloat16 if backward else jnp.float32)]
+        * (1 if backward else 2),
+        compiler_params=pltpu.CompilerParams(vmem_limit_bytes=VMEM_LIMIT, dimension_semantics=("arbitrary",)),
+        cost_estimate=cost(
+            flops=2 * pairs * 2 * slots * 16 * 256 * depth, bytes_accessed=pairs * weight.shape[0] * 256, transcendentals=0
+        ),
+        name="conv_back" if backward else "conv_forth",
+    )(meta, x_ext.reshape(row_count * length, width), seg_quads(seg_ext), weight, extra, *([after] if backward else []))
+
+
+def at_block(b):
+    return pl.ds(b * 256, 256) if isinstance(b, int) else pl.ds(pl.multiple_of(b * 256, 256), 256)
+
+
+def id_block(number):
+    return jnp.full((16, 256), number, jnp.float32).astype(jnp.bfloat16)
+
+
+def conv_ids(seg_ref, flat, ids):
+    rows4 = seg_ref.shape[0]
+    flat[0:rows4, :] = seg_ref[...]
+    flat[rows4:, :] = jnp.zeros((16, 256), jnp.float32)
+    for p in range(16):
+        ids[p] = flat[pl.ds(p, rows4), :].astype(jnp.bfloat16).reshape(rows4 // 16, 16, 256)
+
+
+def conv_cut(places, numbers, b, shifts, ids):
+    nothing = jnp.zeros((16, 256), jnp.bfloat16)
+    pieces = []
+    for at, number in zip(places, numbers):
+        same = ids[b & 15, at + (b >> 4)] == id_block(number)
+        pieces.append(jnp.where(same, shifts[b & 15, at + (b >> 4)], nothing))
+    return jnp.concatenate(pieces, axis=0)
+
+
+def conv_weight_kernel(slots, meta, x_ref, seg_ref, g_ref, after_ref, o_ref, wide, wide_g, flat, shifts, masks, quads, picks, sums):
+    @pl.when(pl.program_id(0) == 0)
+    def _():
+        conv_ids(seg_ref, flat, masks)
+
+    wide[...] = x_ref[...].astype(jnp.float32)
+    wide_g[...] = g_ref[...].astype(jnp.float32)
+    out_rows = g_ref.shape[0] // 4
+    low = lane_low(64)
+    places = [meta[1 + v] for v in range(slots)]
+    numbers = [meta[1 + 2 * slots + v].astype(jnp.float32) for v in range(slots)]
+    nothing = jnp.zeros((16, 256), jnp.bfloat16)
+    for side in range(2):
+        conv_shifts(wide, side, flat, shifts)
+        halves = quad_rows(wide_g, out_rows, side)
+        quads[:, 0:128] = halves[0].astype(jnp.bfloat16)
+        quads[:, 128:256] = halves[1].astype(jnp.bfloat16)
+
+        for v in range(slots):
+            at = pl.ds(pl.multiple_of(meta[1 + slots + v] * 16, 16), 16)
+            same = masks[0, places[v] + 1] == id_block(numbers[v])
+            picks[v * 16 : (v + 1) * 16, :] = jnp.where(same, quads[at, :], nothing)
+
+        turned = picks[...].T
+
+        @pl.loop(0, TAP_BLOCKS, unroll=DW_UNROLL)
+        def _(b):
+            sums[:, at_block(b)] = jnp.dot(
+                turned, conv_cut(places, numbers, b, shifts, masks), preferred_element_type=jnp.float32
+            )
+
+        def piece(j, q):
+            return sums[j * 64 : (j + 1) * 64, q * 128 : (q + 1) * 128]
+
+        def odd(q):
+            return half_roll(piece(1, q) + piece(3, q + 1))
+
+        left = odd(0)
+        for q in range(2 * (TAP_BLOCKS - 1)):
+            right = odd(q + 1)
+            part = piece(0, q) + piece(2, q + 1) + jnp.where(low, left, right)
+            columns = slice(q % 16 * 128, (q % 16 + 1) * 128)
+            o_ref[q // 16, side * 64 : (side + 1) * 64, columns] = part.astype(o_ref.dtype)
+            left = right
+
+
+def grouped_conv_weight(x_ext, seg_ext, grad, rise, after):
+    row_count, length, width = x_ext.shape
+    frames = length - KERNEL
+    pairs = width // 128
+    in_block, tile, number = tile_lists(seg_ext, rise)
+    slots = in_block.shape[0]
+    meta = jnp.concatenate([jnp.zeros((1,), jnp.int32), in_block, tile, number])
+    rows4 = row_count * length // 4
+    out4 = row_count * frames // 4
+    depth = TAP_BLOCKS * 256
+    return pl.pallas_call(
+        partial(conv_weight_kernel, slots),
+        grid_spec=pltpu.PrefetchScalarGridSpec(
+            num_scalar_prefetch=1,
+            grid=(pairs,),
+            in_specs=[
+                pl.BlockSpec((row_count * length, 128), lambda p, meta: (0, p)),
+                pl.BlockSpec((rows4, 256), lambda p, meta: (0, 0)),
+                pl.BlockSpec((row_count * frames, 128), lambda p, meta: (0, p)),
+                pl.BlockSpec(memory_space=pl.ANY),
+            ],
+            out_specs=pl.BlockSpec((4, 128, KERNEL * 16), lambda p, meta: (0, p, 0)),
+            scratch_shapes=[
+                pltpu.VMEM((row_count * length, 128), jnp.float32),
+                pltpu.VMEM((row_count * frames, 128), jnp.float32),
+                pltpu.VMEM((rows4 + 16, 256), jnp.float32),
+                pltpu.VMEM((16, rows4 // 16, 16, 256), jnp.bfloat16),
+                pltpu.VMEM((16, rows4 // 16, 16, 256), jnp.bfloat16),
+                pltpu.VMEM((out4, 256), jnp.bfloat16),
+                pltpu.VMEM((slots * 16, 256), jnp.bfloat16),
+                pltpu.VMEM((256, depth), jnp.float32),
+            ],
+        ),
+        out_shape=jax.ShapeDtypeStruct((4, width, KERNEL * 16), jnp.bfloat16),
+        compiler_params=pltpu.CompilerParams(vmem_limit_bytes=VMEM_LIMIT, dimension_semantics=("arbitrary",)),
+        cost_estimate=cost(
+            flops=2 * pairs * 2 * slots * 16 * 256 * depth, bytes_accessed=width * KERNEL * 128, transcendentals=0
+        ),
+        name="conv_weight_grad",
+    )(meta, x_ext.reshape(row_count * length, width), seg_quads(seg_ext), grad, after)
+
+
+AXES = ("y", "c", "z", "x")
+
+
+def device_pairs(place):
+    pairs = []
+    for y in range(2):
+        for c in range(2):
+            for z in range(4):
+                for x in range(2):
+                    ty, tc, tz, tx = place(y, c, z, x)
+                    pairs.append((((y * 2 + c) * 4 + z) * 2 + x, ((ty * 2 + tc) * 4 + tz) * 2 + tx))
+    return pairs
+
+
+def move(values, place):
+    return lax.ppermute(values, AXES, device_pairs(place))
+
+
+def swap_core(values):
+    return lax.ppermute(values, "c", [(0, 1), (1, 0)])
+
+
+def swap_x(values):
+    return lax.ppermute(values, "x", [(0, 1), (1, 0)])
+
+
+def swap_y(values):
+    return lax.ppermute(values, "y", [(0, 1), (1, 0)])
+
+
+def swap_xy(values):
+    return lax.ppermute(values, ("y", "x"), [(0, 3), (3, 0), (1, 2), (2, 1)])
+
+
+def swap_z1(values):
+    return lax.ppermute(values, "z", [(0, 1), (1, 0), (2, 3), (3, 2)])
+
+
+def swap_z2(values):
+    return lax.ppermute(values, "z", [(0, 2), (2, 0), (1, 3), (3, 1)])
+
+
+def take(values, index, size, axis):
+    return lax.dynamic_slice_in_dim(values, index * size, size, axis)
+
+
+def once(values, *earlier):
+    return lax.optimization_barrier((values,) + earlier)[0]
+
+
+def ordered(index, mine, other, axis):
+    first = jnp.where(index == 0, mine, other)
+    second = jnp.where(index == 0, other, mine)
+    return jnp.concatenate([first, second], axis=axis)
+
+
+def to_rows(blocks, x, z):
+    got = []
+    for turn in range(2):
+        mine = lax.dynamic_index_in_dim(blocks, x ^ turn, 0, keepdims=False)
+        got.append(move(mine, lambda y, c, z, x: (y, z & 1, 2 * c + (x ^ turn), z >> 1)))
+    flip = (z & 1) == 0
+    return jnp.where(flip, got[0], got[1]), jnp.where(flip, got[1], got[0])
+
+
+def from_rows(frames, x, z):
+    half = frames.shape[0] // 2
+    got = []
+    for turn in range(2):
+        mine = take(frames, (z & 1) ^ turn, half, 0)
+        got.append(move(mine, lambda y, c, z, x: (y, z >> 1, 2 * x + c, (z & 1) ^ turn)))
+    return ordered(x, got[0][None], got[1][None], 0)
+
+
+def split_body(
+    feats, segments, labels, conv_weight, w_qkv, w_out, w_up, w_down, head_w, head_b, gains, biases, up_bias
+):
+    y, c, z, x = (lax.axis_index(name) for name in AXES)
+    block, features = feats.shape[1:]
+    half = features // 2
+    frames = 2 * block
+    chip_frames = 2 * frames
+    tokens = frames
+    rim = KERNEL // 2
+    rise = lax.axis_size("z") * lax.axis_size("x") // 2
+    meta = jnp.stack([c, y, x, z]).astype(jnp.int32)
+
+    label_rows = jnp.pad(labels.astype(jnp.bfloat16)[:, None, :], ((0, 0), (0, 15), (0, features - block)))
+    first_block, second_block = to_rows(jnp.concatenate([feats, label_rows], axis=1), x, z)
+    feats_own = jnp.concatenate([first_block[:block], second_block[:block]], axis=0)
+    labels_own = jnp.concatenate([first_block[block, :block], second_block[block, :block]]).astype(jnp.int32)
+    seg_rows = ordered(c, segments, swap_core(segments), 0)
+    seg_row = lax.dynamic_index_in_dim(seg_rows, z, 0, keepdims=False)
+    seg_halves = seg_row.reshape(2, 2, frames)
+    seg_near = lax.dynamic_index_in_dim(seg_halves, x, 0, keepdims=False)
+    seg_far = lax.dynamic_index_in_dim(seg_halves, 1 - x, 0, keepdims=False)
+    seg_near, seg_far = (jnp.where(c == 0, item, item[::-1]).reshape(-1) for item in (seg_near, seg_far))
+    seg_wide = jnp.pad(seg_row, (rim, rim), constant_values=-1)
+    seg_ext = lax.dynamic_slice_in_dim(seg_wide, x * chip_frames, chip_frames + 2 * rim, 0)[None]
+
+    def to_chip(values):
+        return ordered(c, take(values, c, half, 1), swap_core(take(values, 1 - c, half, 1)), 0)
+
+    def rimmed(values, edge):
+        empty = jnp.zeros_like(edge)
+        before = jnp.where(x == 0, empty, edge)
+        after = jnp.where(x == 0, edge, empty)
+        return jnp.concatenate([before, values, after], axis=0)[None]
+
+    def with_rim(values):
+        return rimmed(values, swap_x(jnp.where(x == 0, values[chip_frames - rim :], values[:rim])))
+
+    def grouped(own, got_x, got_y, got_xy):
+        return ordered(y, ordered(x, own, got_x, 0)[None], ordered(x, got_y, got_xy, 0)[None], 0)
+
+    def to_groups(values):
+        def part(yy, xx):
+            return lax.dynamic_slice_in_dim(values, 256 * xx + 128 * yy, 128, 1)
+
+        return grouped(
+            part(y, x), swap_x(part(y, 1 - x)), swap_y(part(1 - y, x)), swap_xy(part(1 - y, 1 - x))
+        )
+
+    shift_bias = biases.T
+    qkv_bias = jnp.concatenate([shift_bias[2], jnp.zeros((features,), jnp.float32), shift_bias[3]])[None]
+    gain_rows = gains.T
+    feats_chip = to_chip(feats_own)
+    position_chip, slope = grouped_conv(
+        with_rim(feats_chip), seg_ext, conv_weight, take(shift_bias[0:1], c, half, 1), 4 * c, rise, False
+    )
+    theirs, ours, normed, position = mix_rows(
+        meta,
+        (
+            take(position_chip, c, frames, 0),
+            swap_core(take(position_chip, 1 - c, frames, 0)),
+            gain_rows[0:1],
+            shift_bias[1:2],
+        ),
+        w_qkv,
+        qkv_bias,
+        1,
+        2,
+    )
+    near = jnp.concatenate([ours, swap_core(theirs)], axis=0)
+    got_normed = swap_core(normed)
+    far = swap_x(near)
+    theirs, ours = mix_rows(meta, (normed,), w_qkv, qkv_bias, 0, 1)
+    queries = jnp.concatenate([ours, swap_core(theirs)], axis=0)
+    mixed, state = attend_near(queries, near, seg_near, seg_near)
+    attended, attended_ours, attended_away, lse = attend_far(queries, far, seg_near, seg_far, mixed, state)
+    feats_group = jnp.pad(to_groups(feats_chip), ((0, 0), (rim, rim), (0, 0)))
+    seg_pair = ordered(y, seg_row[None], swap_y(seg_row)[None], 0)
+    seg_pair = jnp.pad(seg_pair, ((0, 0), (rim, rim)), constant_values=-1)
+    zero_row = jnp.zeros((features,), jnp.float32)
+    rows = jnp.stack([gain_rows[1], shift_bias[5], shift_bias[4], shift_bias[6]] + [zero_row] * 4)
+    (
+        pack, output_low, out_ours, up_ours, branch_ours, att_ours, att_theirs, grad_resid, mid_sums, up_sums,
+        grad_head_w, last,
+    ) = middle(
+        meta,
+        attended_ours,
+        swap_core(attended_away),
+        position,
+        w_out,
+        w_up,
+        w_down,
+        up_bias[None],
+        head_w,
+        head_b[None],
+        labels_own[:, None],
+        rows,
+        (feats_group, seg_pair),
+    )
+
+    grad_heads = jnp.concatenate([att_ours, swap_core(att_theirs)], axis=0)
+    dq_far, dkv_far = attend_back(queries, far, grad_heads, attended, lse, seg_near, seg_far, jnp.bfloat16, att_ours)
+    got_kv = swap_x(dkv_far)
+
+    C, Y, X, Z = 0, 1, 2, 3
+    places = pack_places(features, w_up.shape[1])
+    got_pack = swap_core(pack)
+    up_pair = ((up_ours, 0), (got_pack, places["up"]))
+    down_pair = ((out_ours, 0), (got_pack, places["out"]))
+    branch_pair = ((branch_ours, 0), (got_pack, places["branch"]))
+    second_pair, active_pair, attended_pair = (
+        ((pack, places[name]), (got_pack, places[name])) for name in ("second", "active", "attended")
+    )
+    unit = features // 8
+    down_rows = w_down.shape[0] // 4
+    up_wide = w_up.shape[1] // 4
+    quarter = half // 2
+    eighth = 3 * half // 4
+    up_low, up_high, down_away, down_home = weight_parts(
+        meta,
+        [
+            weight_task([(0, 0)], second_pair, up_pair, half, 1, lambda i, m: 0, up_wide, lambda m: 1 - m[Y]),
+            weight_task(
+                [(2, 0)], active_pair, down_pair, down_rows, 1,
+                lambda i, m: 2 * (1 - (m[Z] >> 1)) + 1 - (m[Z] & 1), half, lambda m: 0,
+            ),
+            weight_task([(1, 0)], second_pair, up_pair, half, 1, lambda i, m: 1, up_wide, lambda m: 1 - m[Y]),
+            weight_task(
+                [(3, 0)], active_pair, down_pair, down_rows, 1,
+                lambda i, m: 2 * (m[Z] >> 1) + 1 - (m[Z] & 1), half, lambda m: 0,
+            ),
+        ],
+        [(half, up_wide), (half, up_wide), (down_rows, half), (down_rows, half)],
+        "weight_first",
+        dkv_far,
+    )
+    got_up_low, got_down_away = swap_y(up_low), swap_z1(down_away)
+    got_up_high, got_down_home = swap_y(up_high), swap_z1(down_home)
+    dq, dkv = attend_back(queries, near, grad_heads, attended, lse, seg_near, seg_near, jnp.float32, down_home)
+
+    def mixed_grad(part):
+        piece = slice(part * frames, (part + 1) * frames)
+        return jnp.concatenate(
+            [
+                dq[piece] + dq_far[piece],
+                dkv[0, piece] + got_kv[0, piece].astype(jnp.float32),
+                dkv[1, piece] + got_kv[1, piece].astype(jnp.float32),
+            ],
+            axis=1,
+        ).astype(jnp.bfloat16)
+
+    grad_theirs = mixed_grad(1)
+    grad_got = swap_core(grad_theirs)
+    grad_ours = mixed_grad(0)
+    position_ours, position_theirs, first_sums = unmix_rows(
+        meta, grad_ours, grad_got, w_qkv, position, grad_resid, gain_rows[0:1], (got_up_low, got_down_away)
+    )
+    grad_position, grad_conv, edge, own_part, to_x, to_y, to_xy, conv_bias = conv_grad_rows(
+        meta, position_ours, swap_core(position_theirs), slope, (got_up_high, got_down_home)
+    )
+    grad_rim = rimmed(grad_conv, swap_x(edge))
+    grad_group = grouped(own_part, swap_x(to_x), swap_y(to_y), swap_xy(to_xy))
+
+    x_bit, y_bit = (lambda m: m[X]), (lambda m: m[Y])
+    up_send, up_kept, down_send, down_kept = weight_parts(
+        meta,
+        [
+            weight_task(
+                [(0, 0), (1, 0)], second_pair, up_pair, half, 1, lambda i, m: 0, up_wide, lambda m: m[Y],
+                got_up_low, lambda i, m: (0, 0), "rows", x_bit, unit,
+            ),
+            weight_task(
+                [(0, 0), (1, 0)], second_pair, up_pair, half, 1, lambda i, m: 1, up_wide, lambda m: m[Y],
+                got_up_high, lambda i, m: (0, 0), "rows", x_bit, unit, 1,
+            ),
+            weight_task(
+                [(2, 0)], active_pair, down_pair, down_rows, 1,
+                lambda i, m: 2 * (1 - (m[Z] >> 1)) + (m[Z] & 1), half, lambda m: 0, got_down_away, lambda i, m: (0, 0),
+            ),
+            weight_task(
+                [(3, 0)], active_pair, down_pair, down_rows, 1,
+                lambda i, m: 2 * (m[Z] >> 1) + (m[Z] & 1), half, lambda m: 0, got_down_home, lambda i, m: (0, 0),
+            ),
+        ],
+        [(half, up_wide), (half, up_wide), (down_rows, half), (down_rows, half)],
+        "weight_second",
+        grad_conv,
+    )
+    up_got, down_got = swap_x(up_send), swap_z2(down_send)
+    conv_grad = grouped_conv_weight(feats_group, seg_pair, grad_group.reshape(-1, 128), rise, up_kept)
+
+    normed_pair = ((normed, 0), (got_normed, 0))
+    qkv_pair = ((grad_ours, 0), (grad_theirs, 0))
+    a_first, b_first, output_late = weight_parts(
+        meta,
+        [
+            weight_task([(0, 0)], normed_pair, qkv_pair, features, 1, lambda i, m: 0, eighth, lambda m: 1 - m[Y]),
+            weight_task(
+                [(0, eighth)], attended_pair, branch_pair, features, 1, lambda i, m: 0, quarter, lambda m: 1 - m[Y]
+            ),
+            weight_task([(1, 0)], normed_pair, qkv_pair, unit, 4, lambda i, m: 2 * i + 1 - m[X], 2 * eighth, lambda m: 1),
+        ],
+        [(features, eighth + quarter), (half, 2 * eighth)],
+        "weight_qkv_first",
+        conv_grad,
+        output_low,
+    )
+    layer_out = from_rows(output_late, x, z)
+    got_a, got_b = swap_y(a_first), swap_x(b_first)
+
+    (conv_input,) = grouped_conv(grad_rim, seg_ext, conv_weight, grad_position, 4 * c, rise, True, a_first)
+    away = swap_core(take(conv_input, 1 - c, frames, 0))
+    grad_feats = from_rows(ordered(c, take(conv_input, c, frames, 0), away, 1), x, z)
+    a_send, b_send, qkv_kept = weight_parts(
+        meta,
+        [
+            weight_task(
+                [(0, 0), (2, 0)], normed_pair, qkv_pair, features, 1, lambda i, m: 0, eighth, lambda m: m[Y],
+                got_a, lambda i, m: (0, 0), "rows", x_bit, unit,
+            ),
+            weight_task(
+                [(0, eighth), (2, eighth)], attended_pair, branch_pair, features, 1, lambda i, m: 0, 128,
+                lambda m: 2 * m[Y], got_a, lambda i, m: (0, eighth // 128), "rows", x_bit, unit,
+            ),
+            weight_task(
+                [(0, eighth + 128), (2, eighth + 128)], attended_pair, branch_pair, features, 1, lambda i, m: 0, 128,
+                lambda m: 2 * m[Y] + 1, got_a, lambda i, m: (0, eighth // 128 + 1), "rows", x_bit, unit,
+            ),
+            weight_task(
+                [(1, 0), (2, eighth + quarter)], normed_pair, qkv_pair, unit, 4, lambda i, m: 2 * i + m[X], 2 * eighth,
+                lambda m: 1, got_b, lambda i, m: (i, 0), "columns", y_bit,
+            ),
+        ],
+        [(half, eighth + quarter), (half, eighth), (half, 2 * eighth + quarter)],
+        "weight_qkv_second",
+        conv_input,
+    )
+    a_got, b_got = swap_x(a_send), swap_y(b_send)
+
+    def fold(kept, got, axis, bit, swap):
+        total = kept.astype(jnp.float32) + got.astype(jnp.float32)
+        send = lax.dynamic_index_in_dim(total, 1 - bit, axis, keepdims=False).astype(jnp.bfloat16)
+        return lax.dynamic_index_in_dim(total, bit, axis, keepdims=False), swap(send)
+
+    def add(kept, got):
+        return (kept + got.astype(jnp.float32)).astype(jnp.bfloat16)
+
+    def spread(shard):
+        other = swap_y(shard)
+        return jnp.where(y == 0, shard, other), jnp.where(y == 0, other, shard)
+
+    kept, got = (item.reshape(2, 2, unit, up_wide) for item in (up_kept, up_got))
+    kept, got = fold(kept, got, 1, z & 1, swap_z1)
+    kept, got = fold(kept, got, 0, z >> 1, swap_z2)
+    mine = jnp.concatenate(spread(add(kept, got)), axis=1)
+    grad_w_up = ordered(c, mine, swap_core(mine), 1).astype(jnp.float32)
+
+    kept, got = (item.reshape(2, down_rows // 2, half) for item in (down_kept, down_got))
+    kept, got = fold(kept, got, 0, x, swap_x)
+    mine = add(kept, got)
+    mine = add(mine.astype(jnp.float32), swap_y(mine))
+    grad_w_down = ordered(c, mine, swap_core(mine), 1).astype(jnp.float32)
+
+    qkv_got = jnp.concatenate([a_got, b_got], axis=1)
+    kept, got = fold(qkv_kept.reshape(2, 2, unit, -1), qkv_got.reshape(2, 2, unit, -1), 1, z & 1, swap_z1)
+    kept, got = fold(kept, got, 0, z >> 1, swap_z2)
+    low_half, high_half = spread(add(kept, got))
+    out_at = eighth + quarter
+    mine = jnp.concatenate(
+        [
+            low_half[:, :eighth], high_half[:, :eighth], low_half[:, out_at:], high_half[:, out_at:],
+            low_half[:, eighth:out_at], high_half[:, eighth:out_at],
+        ],
+        axis=1,
+    )
+    theirs = swap_core(mine)
+    left, right = jnp.where(c == 0, mine, theirs), jnp.where(c == 0, theirs, mine)
+    grad_w_qkv = jnp.concatenate(
+        [piece[:, part * half : (part + 1) * half] for part in range(3) for piece in (left, right)], axis=1
+    ).astype(jnp.float32)
+    grad_w_out = jnp.concatenate([left[:, 3 * half :], right[:, 3 * half :]], axis=1).astype(jnp.float32)
+
+    pieces = conv_grad.reshape(2, 2, 128, -1)
+    mine = lax.dynamic_index_in_dim(pieces, z & 1, 1, keepdims=False)
+    got = swap_z1(lax.dynamic_index_in_dim(pieces, 1 - (z & 1), 1, keepdims=False))
+    mine, got = fold(mine, got, 0, z >> 1, swap_z2)
+    shard = (mine + got.astype(jnp.float32)).astype(jnp.bfloat16)
+    width = shard.shape[1] // 2
+    shard = ordered(x, take(shard, x, width, 1)[None], swap_x(take(shard, 1 - x, width, 1))[None], 0)
+    shard = jnp.concatenate([shard, swap_y(shard)], axis=0)
+    grad_conv_weight = flip_columns(meta, jnp.concatenate([shard, swap_core(shard)], axis=0))
+
+    own_sums, got_sums = (jnp.sum(item.astype(jnp.float32), axis=0, keepdims=True) for item in (grad_ours, grad_got))
+    total = small_sums(
+        meta, grad_head_w, mid_sums, first_sums, conv_bias, own_sums, got_sums, up_sums, last, b_send
+    )
+    total = total + swap_core(total)
+    total = total + swap_y(total)
+    total = total.reshape(2, 2, 2, -1, unit)
+
+    def half_sum(values, axis, bit, swap):
+        mine = lax.dynamic_index_in_dim(values, bit, axis, keepdims=False)
+        return mine + swap(lax.dynamic_index_in_dim(values, 1 - bit, axis, keepdims=False))
+
+    total = half_sum(total, 2, x, swap_x)
+    total = half_sum(total, 1, z & 1, swap_z1)
+    total = half_sum(total, 0, z >> 1, swap_z2)
+    v = VOCAB
+    loss = total[v + 14, 0] / (tokens * 32)
+    gain_part = jnp.stack([total[v + 4], total[v]], axis=1)
+    bias_part = jnp.stack(
+        [total[v + 6], total[v + 5], total[v + 7], total[v + 8], total[v + 1], total[v + 2], total[v + 3]], axis=1
+    )
+    return (
+        layer_out,
+        loss,
+        grad_feats.astype(jnp.float32),
+        grad_conv_weight,
+        grad_w_qkv,
+        grad_w_out,
+        grad_w_up,
+        grad_w_down,
+        total[:v].T,
+        total[v + 13, :v],
+        gain_part,
+        bias_part,
+        total[v + 9 : v + 13].reshape(-1),
+    )
+
+
+def split_solution(mesh):
+    fine = Mesh(mesh.devices.reshape(2, 2, 4, 2), AXES)
+    rows, parts = ("y", "c"), ("z", "x")
+    return jax.shard_map(
+        split_body,
+        mesh=fine,
+        in_specs=(P(rows, parts, None), P(rows, None), P(rows, parts)) + (P(),) * 10,
+        out_specs=(
+            P(rows, parts, None),
+            P(),
+            P(rows, parts, None),
+            P(parts, None),
+            P(parts, None),
+            P(parts, None),
+            P(parts, None),
+            P(parts, None),
+            P(parts, None),
+            P(),
+            P(parts, None),
+            P(parts, None),
+            P(parts),
+        ),
+        check_vma=False,
+    )
+
+
+def solution(mesh):
+    if mesh.shape["dp"] == 4 and mesh.shape["seq"] == 8:
+        return split_solution(mesh)
+    return whole_solution(mesh)

time: 2670 us -> 505 us (0.19)
  waiting for transfers between devices: 1640 us -> 108 us
  local copies, waits for them, and re-layouts: 531 us -> 31.6 us
  Pallas kernels: 0 us -> 203 us
  matrix products: 181 us -> 0 us
  other arithmetic: 167 us -> 40.3 us
  blocking collectives: 104 us -> 0 us
  starting transfers between devices: 12.2 us -> 108 us
    reduce_scatter x8 -> x0, waiting for transfers between devices: 1440 us -> none  [the longest x1 544 us: body(): lax.psum_scatter(grad_conv_weight, 'seq', scatter_dimension=0, tiled=True)]
    pallas_call x0 -> x18, Pallas kernels: none -> 203 us  [the longest x2 52.2 us: grouped_conv(): pl.pallas_call(partial(conv_kernel, slots, backward), grid_spec=pltpu.Pre...]
    dot_general x75 -> x0, matrix products: 181 us -> none  [the longest x5 29.1 us: outer_sum(): lax.dot_general(left_side, right_side, (((0,), (0,)), ((), ())), preferre...]
    dynamic_slice x50 -> x5, local copies, waits for them, and re-layouts: 159 us -> 3.75 us  [take(): return lax.dynamic_slice_in_dim(values, index * size, size, axis)]
    all_gather x2 -> x0, waiting for transfers between devices: 138 us -> none  [the longest x1 72 us: body(): key_shard = lax.all_gather(keys, 'seq', axis=1, tiled=True)]
    ppermute x4 -> x60, waiting for transfers between devices: 0.01 us -> 108 us  [the longest x12 28.2 us: swap_y(): return lax.ppermute(values, 'y', [(0, 1), (1, 0)])]
    reshape x4 -> x10, local copies, waits for them, and re-layouts: 102 us -> 3.21 us  [the longest x2 1.85 us: seg_quads(): return jnp.repeat(quads, 64, axis=1)]
    ppermute x4 -> x60, starting transfers between devices: 10.9 us -> 108 us  [the longest x12 26.7 us: swap_x(): return lax.ppermute(values, 'x', [(0, 1), (1, 0)])]
  transfers between devices with their start and end apart: 16 -> 60, of which waited for: 9 -> 21; matrix products, arithmetic and copies ran while one was open for 16% -> 11% of each run, Pallas kernels for 0% -> 28%
where the time goes in v2:
time: 505 us; the launch traced here: 496 us
  Pallas kernels  203 us (40%)
  starting transfers between devices  108 us (21%)
  waiting for transfers between devices  108 us (21%)
  other arithmetic  40.3 us (8%)
  local copies, waits for them, and re-layouts  31.6 us (6%)
    pallas_call x2, Pallas kernels, grouped_conv(): pl.pallas_call(partial(conv_kernel, slots, backward), grid_spec=pltpu.Pre...  52.2 us
    pallas_call x4, Pallas kernels, weight_parts(): pl.pallas_call(partial(weight_kernel, tasks, len(shapes), carry is not No...  37.5 us
    pallas_call x1, Pallas kernels, middle(): pl.pallas_call(middle_kernel, grid_spec=pltpu.PrefetchScalarGridSpec(num_...  31 us
    ppermute x12, waiting for transfers between devices, swap_y(): return lax.ppermute(values, 'y', [(0, 1), (1, 0)])  28.2 us
    ppermute x12, starting transfers between devices, swap_x(): return lax.ppermute(values, 'x', [(0, 1), (1, 0)])  26.7 us
    ppermute x6, starting transfers between devices, move(): return lax.ppermute(values, AXES, device_pairs(place))  23.4 us
    ppermute x6, waiting for transfers between devices, swap_z1(): return lax.ppermute(values, 'z', [(0, 1), (1, 0), (2, 3), (3, 2)])  21.4 us
    pallas_call x1, Pallas kernels, grouped_conv_weight(): pl.pallas_call(partial(conv_weight_kernel, slots), grid_spec=pltpu.Prefet...  17.2 us
  transfers between devices with their start and end apart: 60, of which 21 were waited for; matrix products, arithmetic and copies ran while one was open for 11% of the time, Pallas kernels for 28%

profile of v2, /device:TPU:0, one launch (start us, length us, event | category | flops | bytes accessed | tf_op | source)
XLA Modules:
  0.0 495.7 jit_solution(8973662516151111129)
XLA Ops:
  3.3 4.3 collective-permute-start.2
  7.6 2.7 collective-permute-start
  19.8 6.8 %collective-permute-start.4 = (bf16[64,512]{1,0:T(8,128)(2,1)S(1)}, bf16[64,512]{1,0:T(8,128)(2,1)S(1)}, u32[]{:S(2)}, u32[]{:S(2)}) collective-permute-start(bf16[64,512]{1,0:T(8,128)(2,1)S(1)} %slice_select_fusion), channel_id=1, source_target_pairs={{0,1},{1,0},{2,3},{3,2},{4,5},{5,4},{6,7},{7,6},{8,9},{9,8},{10,11... | collective-permute-start | bytes 196616 | tf_op jit(solution)/shard_map/ppermute | solution.py:1602
  27.1 1.8 collective-permute-done.4
  29.9 23.9 %conv_forth.1 = (f32[512,512]{1,0:T(8,128)}, f32[512,512]{1,0:T(8,128)}) custom-call(s32[37]{0:T(128)} %pad_add_fusion.2.meta, bf16[640,512]{1,0:T(8,128)(2,1)} %pad_maximum_fusion.4.x_ref, f32[160,256]{1,0:T(8,128)} %copy.111.seg_ref, bf16[8192,1024]{1,0:T(8,128)(2,1)} %w_ref.5, f32[1,512]{1,0:T(1,128)} %constant_dynamic-slice_fusion.8.extra_ref), custom_call_target="tpu_custom_call" | custom-call | flops 6643777 | bytes 8388 | tf_op jit(solution)/shard_map/conv_forth/pallas_call | solution.py:1433
  53.7 2.1 constant_dynamic-slice_fusion.6
  57.0 1.5 collective-permute-start.14
  61.3 6.9 %norm_keys_values.1 = (bf16[256,1024]{1,0:T(8,128)(2,1)}, bf16[256,1024]{1,0:T(8,128)(2,1)}, bf16[256,1024]{1,0:T(8,128)(2,1)}, f32[256,1024]{1,0:T(8,128)}) custom-call(s32[4]{0:T(128)} %pad_add_fusion.1.meta, f32[256,512]{1,0:T(8,128)} %get-tuple-element.149.refs_0_, f32[256,512]{1,0:T(8,128)} %copy-done.22, ...), custom_call_target="tpu_custom_call" | custom-call | flops 1073741 | bytes 4194 | tf_op jit(solution)/shard_map/norm_keys_values/pallas_call | solution.py:770
  68.5 1.9 collective-permute-start.11
  75.7 3.3 collective-permute-start.13
  79.8 3.8 queries.1
  83.6 16.0 %collective-permute-done.13 = bf16[512,128]{1,0:T(8,128)(2,1)S(1)} collective-permute-done((bf16[512,128]{1,0:T(8,128)(2,1)}, bf16[512,128]{1,0:T(8,128)(2,1)S(1)}, u32[]{:S(2)}, u32[]{:S(2)}) %collective-permute-start.13) | collective-permute-done | bytes 131104 | tf_op jit(solution)/shard_map/ppermute | solution.py:1610
  101.4 6.9 %attend_near.1 = (f32[512,512]{1,0:T(8,128)}, f32[4,8,512]{2,1,0:T(8,128)}) custom-call(s32[1,512]{1,0:T(1,128)} %bitcast.200, s32[512,1]{1,0:T(8,128)} %bitcast.189, bf16[512,512]{1,0:T(8,128)(2,1)} %copy-done.6, bf16[512,1024]{1,0:T(8,128)(2,1)} %copy-done, bf16[512,1024]{1,0:T(8,128)(2,1)} %copy-done), custom_call_target="tpu_custom_call" | custom-call | flops 1073741 | bytes 4194 | tf_op jit(solution)/shard_map/attend_near/pallas_call | solution.py:598
  109.3 7.6 %attend_far.1 = (f32[512,512]{1,0:T(8,128)}, bf16[256,512]{1,0:T(8,128)(2,1)}, bf16[256,512]{1,0:T(8,128)(2,1)}, f32[4,8,512]{2,1,0:T(8,128)}) custom-call(s32[1,512]{1,0:T(1,128)} %bitcast.201, s32[512,1]{1,0:T(8,128)} %bitcast.191, bf16[512,512]{1,0:T(8,128)(2,1)} %copy-done.6, bf16[512,1024]{1,0:T(8,128)(2,1)} %copy-done.3, bf16[512,1024]{1,0:T(8,128)(2,1)} %copy-done.3, ...), custom_call_target="tpu_custom_call" | custom-call | flops 1073741 | bytes 4194 | tf_op jit(solution)/shard_map/attend_far/pallas_call | solution.py:620
  119.4 31.0 %middle.1 = (bf16[256,9216]{1,0:T(8,128)(2,1)}, bf16[256,1024]{1,0:T(8,128)(2,1)}, bf16[256,512]{1,0:T(8,128)(2,1)}, bf16[256,2048]{1,0:T(8,128)(2,1)}, bf16[256...) custom-call(s32[4]{0:T(128)} %pad_add_fusion.1.meta, ...), custom_call_target="tpu_custom_call" | custom-call | flops 8589934 | bytes 33554 | tf_op jit(solution)/shard_map/middle/pallas_call | solution.py:989
  152.0 4.2 collective-permute-done.15
  156.9 8.5 %attend_back.2 = (f32[512,512]{1,0:T(8,128)}, bf16[2,512,512]{2,1,0:T(8,128)(2,1)}) custom-call(s32[1,512]{1,0:T(1,128)} %bitcast.202, s32[512,1]{1,0:T(8,128)} %bitcast.192, bf16[512,512]{1,0:T(8,128)(2,1)} %copy-done.6, bf16[512,1024]{1,0:T(8,128)(2,1)} %copy-done.3, bf16[512,1024]{1,0:T(8,128)(2,1)} %copy-done.3, bf16[512,512]{1,0:T(8,128)(2,1)} %copy-done.14, ...), custom_call_target="tpu_custom_call" | custom-call | flops 2684354 | bytes 4194 | tf_op jit(solution)/shard_map/attend_back/pallas_call | solution.py:674
  165.5 1.6 collective-permute-start.17
  167.2 8.9 %weight_first.1 = (bf16[512,1024]{1,0:T(8,128)(2,1)}, bf16[512,1024]{1,0:T(8,128)(2,1)}, bf16[1024,512]{1,0:T(8,128)(2,1)}, bf16[1024,512]{1,0:T(8,128)(2,1)}) custom-call(s32[4]{0:T(128)} %pad_add_fusion.1.meta, bf16[256,9216]{1,0:T(8,128)(2,1)} %get-tuple-element.83.refs_0_.refs_4_.refs_8_.refs_12_.refs_5_.refs_10_.refs_15_, ...), custom_call_target="tpu_custom_call" | custom-call | flops 2147483 | bytes 10485 | tf_op jit(solution)/shard_map/weight_first/pallas_call | solution.py:1179
  176.1 1.6 collective-permute-start.19
  179.1 8.6 %attend_back.3 = (f32[512,512]{1,0:T(8,128)}, f32[2,512,512]{2,1,0:T(8,128)}) custom-call(s32[1,512]{1,0:T(1,128)} %bitcast.203, s32[512,1]{1,0:T(8,128)} %bitcast.190, bf16[512,512]{1,0:T(8,128)(2,1)} %copy-done.6, bf16[512,1024]{1,0:T(8,128)(2,1)} %copy-done, bf16[512,1024]{1,0:T(8,128)(2,1)} %copy-done, bf16[512,512]{1,0:T(8,128)(2,1)} %copy-done.14, ...), custom_call_target="tpu_custom_call" | custom-call | flops 2684354 | bytes 4194 | tf_op jit(solution)/shard_map/attend_back/pallas_call | solution.py:674
  187.7 1.5 add_convert_fusion.3
  189.2 1.9 collective-permute-done.17
  194.2 1.6 collective-permute-start.22
  196.1 2.0 convert_reduce_fusion.1
  198.0 4.4 collective-permute-done.19.refs_0_.refs_4_
  202.4 1.6 collective-permute-done.20.refs_1_.refs_14_
  204.0 9.8 %qkv_and_norm_back.1 = (f32[256,512]{1,0:T(8,128)}, f32[256,512]{1,0:T(8,128)}, f32[8,1024]{1,0:T(8,128)}) custom-call(s32[4]{0:T(128)} %pad_add_fusion.1.meta, bf16[256,1536]{1,0:T(8,128)(2,1)} %get-tuple-element.131.mine_ref.refs_2_.refs_10_.refs_17_, bf16[256,1536]{1,0:T(8,128)(2,1)} %collective-permute-done.18.other_ref, bf16[1024,3072]{1,0:T(8,128)(2,1)} %w_ref.4, ...), custom_call_target="tpu_custom_call" | custom-call | flops 1610612 | bytes 7340 | tf_op jit(solution)/shard_map/qkv_and_norm_back/pallas_call | solution.py:826
  217.3 6.6 %collective-permute-done.22.refs_0_.refs_9_ = bf16[512,1024]{1,0:T(8,128)(2,1)S(1)} collective-permute-done((bf16[512,1024]{1,0:T(8,128)(2,1)}, bf16[512,1024]{1,0:T(8,128)(2,1)S(1)}, u32[]{:S(2)}, u32[]{:S(2)}) %collective-permute-start.22) | collective-permute-done | bytes 1048608 | tf_op jit(solution)/shard_map/ppermute | solution.py:1606
  226.1 3.8 conv_grad_rows.1
  232.2 1.7 collective-permute-start.24
  235.7 10.3 %weight_second.1 = (bf16[512,1024]{1,0:T(8,128)(2,1)}, bf16[512,1024]{1,0:T(8,128)(2,1)}, bf16[1024,512]{1,0:T(8,128)(2,1)}, bf16[1024,512]{1,0:T(8,128)(2,1)}) custom-call(s32[4]{0:T(128)} %pad_add_fusion.1.meta, bf16[256,9216]{1,0:T(8,128)(2,1)} %get-tuple-element.83.refs_0_.refs_4_.refs_8_.refs_12_.refs_5_.refs_10_.refs_15_, ...), custom_call_target="tpu_custom_call" | custom-call | flops 2147483 | bytes 10485 | tf_op jit(solution)/shard_map/weight_second/pallas_call | solution.py:1179
  246.0 2.3 collective-permute-start.56
  250.5 17.2 %conv_weight_grad.1.refs_12_ = bf16[4,128,2048]{2,1,0:T(8,128)(2,1)} custom-call(s32[121]{0:T(128)} %pad_add_fusion.3.meta, bf16[2304,128]{1,0:T(8,128)(2,1)} %bitcast.187, f32[576,256]{1,0:T(8,128)} %copy.122.seg_ref, bf16[2048,128]{1,0:T(8,128)(2,1)} %bitcast.193, bf16[512,1024]{1,0:T(8,128)(2,1)} %get-tuple-element.104.after_ref), custom_call_target="tpu_custom_call" | custom-call | flops 5536481 | bytes 2097 | tf_op jit(solution)/shard_map/conv_weight_grad/pallas_call | solution.py:1547
  268.5 8.3 %weight_qkv_first.1 = (bf16[1024,640]{1,0:T(8,128)(2,1)}, bf16[512,768]{1,0:T(8,128)(2,1)}, bf16[256,1024]{1,0:T(8,128)(2,1)}) custom-call(s32[4]{0:T(128)} %pad_add_fusion.1.meta, bf16[256,1024]{1,0:T(8,128)(2,1)} %get-tuple-element.69.refs_0_.refs_8_.refs_15_, bf16[256,1024]{1,0:T(8,128)(2,1)} %copy-done.7, ...), custom_call_target="tpu_custom_call" | custom-call | flops 1073741 | bytes 6160 | tf_op jit(solution)/shard_map/weight_qkv_first/pallas_call | solution.py:1179
  277.4 28.3 %conv_back.1.refs_20_ = bf16[512,512]{1,0:T(8,128)(2,1)} custom-call(s32[37]{0:T(128)} %pad_add_fusion.2.meta, bf16[640,512]{1,0:T(8,128)(2,1)} %pad_maximum_fusion.5.x_ref, f32[160,256]{1,0:T(8,128)} %copy.111.seg_ref, bf16[8192,1024]{1,0:T(8,128)(2,1)} %w_ref.5, f32[512,512]{1,0:T(8,128)} %get-tuple-element.116.extra_ref, ...), custom_call_target="tpu_custom_call" | custom-call | flops 6643777 | bytes 8388 | tf_op jit(solution)/shard_map/conv_back/pallas_call | solution.py:1433
  308.4 4.1 collective-permute-start.28
  313.4 9.7 %collective-permute-done.28 = bf16[128,1024]{1,0:T(8,128)(2,1)S(1)} collective-permute-done((bf16[128,1024]{1,0:T(8,128)(2,1)S(1)}, bf16[128,1024]{1,0:T(8,128)(2,1)S(1)}, u32[]{:S(2)}, u32[]{:S(2)}) %collective-permute-start.28) | collective-permute-done | bytes 262176 | tf_op jit(solution)/shard_map/ppermute | solution.py:1594
  323.1 12.9 %collective-permute-start.39 = (bf16[128,1024]{1,0:T(8,128)(2,1)S(1)}, bf16[128,1024]{1,0:T(8,128)(2,1)S(1)}, u32[]{:S(2)}, u32[]{:S(2)}) collective-permute-start(bf16[128,1024]{1,0:T(8,128)(2,1)S(1)} %get-tuple-element.173), channel_id=1, source_target_pairs={{0,1},{1,5},{2,0},{3,4},{4,9},{5,13},{6,8},{7,12},{8,3},{9,7},{10,... | collective-permute-start | bytes 786440 | tf_op jit(solution)/shard_map/ppermute | solution.py:1594
  336.9 2.9 collective-permute-start.30
  339.9 9.6 %collective-permute-start.40 = (bf16[2,128,2048]{2,1,0:T(8,128)(2,1)S(1)}, bf16[2,128,2048]{2,1,0:T(8,128)(2,1)S(1)}, u32[]{:S(2)}, u32[]{:S(2)}) collective-permute-start(bf16[2,128,2048]{2,1,0:T(8,128)(2,1)S(1)} %dynamic-slice_bitcast_fusion), channel_id=1, source_target_pairs={{0,2},{2,0},{4,6},{6,4},{1,3},{3,1},{5,7},{7,5},{8,10},{10,8},{12,... | collective-permute-start | bytes 3145736 | tf_op jit(solution)/shard_map/ppermute | solution.py:1614
  350.7 1.6 convert_add_fusion.1
  353.2 8.3 %collective-permute-start.57 = (bf16[512,512]{1,0:T(8,128)(2,1)}, bf16[512,512]{1,0:T(8,128)(2,1)S(1)}, u32[]{:S(2)}, u32[]{:S(2)}) collective-permute-start(bf16[512,512]{1,0:T(8,128)(2,1)} %fusion.9), channel_id=1, source_target_pairs={{0,1},{1,0},{2,3},{3,2},{4,5},{5,4},{6,7},{7,6},{8,9},{9,8},{10,11... | collective-permute-start | bytes 1572872 | tf_op jit(solution)/shard_map/ppermute | solution.py:1602
  361.5 1.6 convert_add_fusion.2
  364.6 10.5 %collective-permute-done.40 = bf16[2,128,2048]{2,1,0:T(8,128)(2,1)S(1)} collective-permute-done((bf16[2,128,2048]{2,1,0:T(8,128)(2,1)S(1)}, bf16[2,128,2048]{2,1,0:T(8,128)(2,1)S(1)}, u32[]{:S(2)}, u32[]{:S(2)}) %collective-permute-start.40) | collective-permute-done | bytes 1048608 | tf_op jit(solution)/shard_map/ppermute | solution.py:1614
  376.3 13.9 %collective-permute-start.41 = (bf16[128,2048]{1,0:T(8,128)(2,1)}, bf16[128,2048]{1,0:T(8,128)(2,1)}, u32[]{:S(2)}, u32[]{:S(2)}) collective-permute-start(bf16[128,2048]{1,0:T(8,128)(2,1)} %fusion.8), channel_id=1, source_target_pairs={{0,4},{4,0},{2,6},{6,2},{1,5},{5,1},{3,7},{7,3},{8,12},{12,8},{10,... | collective-permute-start | bytes 1572872 | tf_op jit(solution)/shard_map/ppermute | solution.py:1618
  391.2 10.1 %weight_qkv_second.1 = (bf16[512,640]{1,0:T(8,128)(2,1)}, bf16[512,384]{1,0:T(8,128)(2,1)}, bf16[512,1024]{1,0:T(8,128)(2,1)}) custom-call(s32[4]{0:T(128)} %pad_add_fusion.1.meta, bf16[256,1024]{1,0:T(8,128)(2,1)} %get-tuple-element.69.refs_0_.refs_8_.refs_15_, bf16[256,1024]{1,0:T(8,128)(2,1)} %copy-done.7, ...), custom_call_target="tpu_custom_call" | custom-call | flops 1073741 | bytes 7208 | tf_op jit(solution)/shard_map/weight_qkv_second/pallas_call | solution.py:1179
  401.3 1.6 collective-permute-start.46
  402.9 2.4 small_sums.1
  412.1 13.9 %collective-permute-done.33 = f32[8,48,128]{2,1,0:T(8,128)S(1)} collective-permute-done((f32[8,48,128]{2,1,0:T(8,128)S(1)}, f32[8,48,128]{2,1,0:T(8,128)S(1)}, u32[]{:S(2)}, u32[]{:S(2)}) %collective-permute-start.33) | collective-permute-done | bytes 196640 | tf_op jit(solution)/shard_map/ppermute | solution.py:1606
  426.0 1.7 collective-permute-start.42
  428.9 7.1 %collective-permute-done.34 = f32[2,2,48,128]{3,2,1,0:T(8,128)S(1)} collective-permute-done((f32[2,2,48,128]{3,2,1,0:T(8,128)S(1)}, f32[2,2,48,128]{3,2,1,0:T(8,128)S(1)}, u32[]{:S(2)}, u32[]{:S(2)}) %collective-permute-start.34) | collective-permute-done | bytes 98336 | tf_op jit(solution)/shard_map/ppermute | solution.py:1602
  436.7 2.6 collective-permute-start.35
  439.4 1.9 collective-permute-done.35
  442.3 3.9 collective-permute-done.36
  451.6 1.5 convert_add_fusion.3
  453.2 2.1 collective-permute-start.47
  458.5 6.1 %collective-permute-done.47 = bf16[2,128,1024]{2,1,0:T(8,128)(2,1)S(1)} collective-permute-done((bf16[2,128,1024]{2,1,0:T(8,128)(2,1)S(1)}, bf16[2,128,1024]{2,1,0:T(8,128)(2,1)S(1)}, u32[]{:S(2)}, u32[]{:S(2)}) %collective-permute-start.47) | collective-permute-done | bytes 524320 | tf_op jit(solution)/shard_map/ppermute | solution.py:1614
  465.1 9.8 %collective-permute-done.48 = bf16[128,1024]{1,0:T(8,128)(2,1)S(1)} collective-permute-done((bf16[128,1024]{1,0:T(8,128)(2,1)S(1)}, bf16[128,1024]{1,0:T(8,128)(2,1)S(1)}, u32[]{:S(2)}, u32[]{:S(2)}) %collective-permute-start.48) | collective-permute-done | bytes 262176 | tf_op jit(solution)/shard_map/ppermute | solution.py:1618
  476.5 1.6 maximum_convert_fusion.1
  478.1 3.3 collective-permute-done.49
  481.6 1.5 maximum_convert_fusion
  483.2 1.5 pad_maximum_fusion.in_ref
  484.7 7.1 %flip_columns.1 = f32[1024,1024]{1,0:T(8,128)} custom-call(s32[4]{0:T(128)} %pad_add_fusion.1.meta, bf16[8,128,1024]{2,1,0:T(8,128)(2,1)} %pad_maximum_fusion.in_ref), custom_call_target="tpu_custom_call" | custom-call | bytes 6291 | tf_op jit(solution)/shard_map/flip_columns/pallas_call | solution.py:1204
  (306 shorter events, 81.7 us)
Async XLA Ops:
  2.6 13.0 %collective-permute-start.1 = (bf16[144,1024]{1,0:T(8,128)(2,1)S(1)}, bf16[144,1024]{1,0:T(8,128)(2,1)S(1)}, u32[]{:S(2)}, u32[]{:S(2)}) collective-permute-start(bf16[144,1024]{1,0:T(8,128)(2,1)S(1)} %get-tuple-element.161), channel_id=1, source_target_pairs={{0,0},{1,2},{2,8},{3,10},{4,1},{5,3},{6,9},{7,11},{8,4},{9,6},{10,... | collective-permute-start | bytes 884744 | tf_op jit(solution)/shard_map/ppermute | solution.py:1594
  3.3 13.6 %collective-permute-start.2 = (bf16[144,1024]{1,0:T(8,128)(2,1)S(1)}, bf16[144,1024]{1,0:T(8,128)(2,1)S(1)}, u32[]{:S(2)}, u32[]{:S(2)}) collective-permute-start(bf16[144,1024]{1,0:T(8,128)(2,1)S(1)} %get-tuple-element.160), channel_id=1, source_target_pairs={{0,2},{1,0},{2,10},{3,8},{4,3},{5,1},{6,11},{7,9},{8,6},{9,4},{10,... | collective-permute-start | bytes 884744 | tf_op jit(solution)/shard_map/ppermute | solution.py:1594
  7.6 6.0 %collective-permute-start = (s32[2,1024]{1,0:T(2,128)S(1)}, s32[2,1024]{1,0:T(2,128)S(1)}, u32[]{:S(2)}, u32[]{:S(2)}) collective-permute-start(s32[2,1024]{1,0:T(2,128)S(1)} %copy-done.30), channel_id=1, source_target_pairs={{0,8},{8,0},{1,9},{9,1},{2,10},{10,2},{3,11},{11,3},{4,12},{12,4},... | collective-permute-start | bytes 24584 | tf_op jit(solution)/shard_map/ppermute | solution.py:1598
  17.0 2.6 collective-permute-start.3
  19.8 9.2 %collective-permute-start.4 = (bf16[64,512]{1,0:T(8,128)(2,1)S(1)}, bf16[64,512]{1,0:T(8,128)(2,1)S(1)}, u32[]{:S(2)}, u32[]{:S(2)}) collective-permute-start(bf16[64,512]{1,0:T(8,128)(2,1)S(1)} %slice_select_fusion), channel_id=1, source_target_pairs={{0,1},{1,0},{2,3},{3,2},{4,5},{5,4},{6,7},{7,6},{8,9},{9,8},{10,11... | collective-permute-start | bytes 196616 | tf_op jit(solution)/shard_map/ppermute | solution.py:1602
  55.8 4.7 collective-permute-start.5
  57.0 11.4 %collective-permute-start.14 = (s32[1024]{0:T(1024)S(1)}, s32[1024]{0:T(1024)S(1)}, u32[]{:S(2)}, u32[]{:S(2)}) collective-permute-start(s32[1024]{0:T(1024)S(1)} %bitcast.205), channel_id=1, source_target_pairs={{0,16},{16,0},{1,17},{17,1},{2,18},{18,2},{3,19},{19,3},{4,20},{20... | collective-permute-start | bytes 12296 | tf_op jit(solution)/shard_map/ppermute | solution.py:1606
  68.2 3.3 collective-permute-start.8
  68.5 5.9 %collective-permute-start.11 = (bf16[512,128]{1,0:T(8,128)(2,1)S(1)}, bf16[512,128]{1,0:T(8,128)(2,1)S(1)}, u32[]{:S(2)}, u32[]{:S(2)}) collective-permute-start(bf16[512,128]{1,0:T(8,128)(2,1)S(1)} %fusion.26), channel_id=1, source_target_pairs={{0,1},{1,0},{2,3},{3,2},{4,5},{5,4},{6,7},{7,6},{8,9},{9,8},{10,11... | collective-permute-start | bytes 393224 | tf_op jit(solution)/shard_map/ppermute | solution.py:1602
  71.5 36.8 %collective-permute-start.9 = (bf16[512,1024]{1,0:T(8,128)(2,1)S(1)}, bf16[512,1024]{1,0:T(8,128)(2,1)S(1)}, u32[]{:S(2)}, u32[]{:S(2)}) collective-permute-start(bf16[512,1024]{1,0:T(8,128)(2,1)S(1)} %constant_dynamic-update-slice_fusion.2.k_ref.v_ref), channel_id=1, source_target_pairs={{0,1},{1,0},{2,3},{3,2},{4,5},{5,4},{6,7},{7,6},{8,9},{9,8},{10,11... | collective-permute-start | bytes 3145736 | tf_op jit(solution)/shard_map/ppermute | solution.py:1602
  75.2 8.4 %collective-permute-start.12 = (bf16[512,128]{1,0:T(8,128)(2,1)}, bf16[512,128]{1,0:T(8,128)(2,1)S(1)}, u32[]{:S(2)}, u32[]{:S(2)}) collective-permute-start(bf16[512,128]{1,0:T(8,128)(2,1)} %get-tuple-element.182), channel_id=1, source_target_pairs={{0,16},{16,0},{1,17},{17,1},{2,18},{18,2},{3,19},{19,3},{4,20},{20... | collective-permute-start | bytes 393224 | tf_op jit(solution)/shard_map/ppermute | solution.py:1606
  75.7 23.9 %collective-permute-start.13 = (bf16[512,128]{1,0:T(8,128)(2,1)}, bf16[512,128]{1,0:T(8,128)(2,1)S(1)}, u32[]{:S(2)}, u32[]{:S(2)}) collective-permute-start(bf16[512,128]{1,0:T(8,128)(2,1)} %get-tuple-element.183), channel_id=1, source_target_pairs={{0,17},{17,0},{1,16},{16,1},{2,19},{19,2},{3,18},{18,3},{4,21},{21... | collective-permute-start | bytes 393224 | tf_op jit(solution)/shard_map/ppermute | solution.py:1610
  83.6 17.0 %collective-permute-start.7 = (bf16[256,512]{1,0:T(8,128)(2,1)}, bf16[256,512]{1,0:T(8,128)(2,1)S(1)}, u32[]{:S(2)}, u32[]{:S(2)}) collective-permute-start(bf16[256,512]{1,0:T(8,128)(2,1)} %get-tuple-element.71), channel_id=1, source_target_pairs={{0,8},{8,0},{1,9},{9,1},{2,10},{10,2},{3,11},{11,3},{4,12},{12,4},... | collective-permute-start | bytes 786440 | tf_op jit(solution)/shard_map/ppermute | solution.py:1598
  116.9 1.8 collective-permute-start.10
  150.4 16.7 %collective-permute-start.16 = (bf16[256,9216]{1,0:T(8,128)(2,1)}, bf16[256,9216]{1,0:T(8,128)(2,1)}, u32[]{:S(2)}, u32[]{:S(2)}) collective-permute-start(bf16[256,9216]{1,0:T(8,128)(2,1)} %get-tuple-element.83.refs_0_.refs_4_.refs_8_.refs_12_.refs_5_.refs_10_.refs_15_), channel_id=1, source_target_pairs={{0,8},{8,0},{1,9},{9,1},{2,10},{10,2},{3,11},{11,3},{4,12},{12,4},... | collective-permute-start | bytes 14155784 | tf_op jit(solution)/shard_map/ppermute | solution.py:1598
  150.6 5.5 %collective-permute-start.15 = (bf16[256,512]{1,0:T(8,128)(2,1)}, bf16[256,512]{1,0:T(8,128)(2,1)S(1)}, u32[]{:S(2)}, u32[]{:S(2)}) collective-permute-start(bf16[256,512]{1,0:T(8,128)(2,1)} %get-tuple-element.80), channel_id=1, source_target_pairs={{0,8},{8,0},{1,9},{9,1},{2,10},{10,2},{3,11},{11,3},{4,12},{12,4},... | collective-permute-start | bytes 786440 | tf_op jit(solution)/shard_map/ppermute | solution.py:1598
  165.5 25.7 %collective-permute-start.17 = (bf16[2,512,512]{2,1,0:T(8,128)(2,1)}, bf16[2,512,512]{2,1,0:T(8,128)(2,1)S(1)}, u32[]{:S(2)}, u32[]{:S(2)}) collective-permute-start(bf16[2,512,512]{2,1,0:T(8,128)(2,1)} %get-tuple-element.86.refs_16_), channel_id=1, source_target_pairs={{0,1},{1,0},{2,3},{3,2},{4,5},{5,4},{6,7},{7,6},{8,9},{9,8},{10,11... | collective-permute-start | bytes 3145736 | tf_op jit(solution)/shard_map/ppermute | solution.py:1602
  176.1 26.3 %collective-permute-start.19 = (bf16[512,1024]{1,0:T(8,128)(2,1)}, bf16[512,1024]{1,0:T(8,128)(2,1)}, u32[]{:S(2)}, u32[]{:S(2)}) collective-permute-start(bf16[512,1024]{1,0:T(8,128)(2,1)} %get-tuple-element.93), channel_id=1, source_target_pairs={{0,16},{16,0},{1,17},{17,1},{2,18},{18,2},{3,19},{19,3},{4,20},{20... | collective-permute-start | bytes 3145736 | tf_op jit(solution)/shard_map/ppermute | solution.py:1606
  177.6 26.4 %collective-permute-start.20 = (bf16[1024,512]{1,0:T(8,128)(2,1)}, bf16[1024,512]{1,0:T(8,128)(2,1)}, u32[]{:S(2)}, u32[]{:S(2)}) collective-permute-start(bf16[1024,512]{1,0:T(8,128)(2,1)} %get-tuple-element.94), channel_id=1, source_target_pairs={{0,2},{2,0},{4,6},{6,4},{1,3},{3,1},{5,7},{7,5},{8,10},{10,8},{12,... | collective-permute-start | bytes 3145736 | tf_op jit(solution)/shard_map/ppermute | solution.py:1614
  192.4 5.7 %collective-permute-start.18 = (bf16[256,1536]{1,0:T(8,128)(2,1)S(1)}, bf16[256,1536]{1,0:T(8,128)(2,1)}, u32[]{:S(2)}, u32[]{:S(2)}) collective-permute-start(bf16[256,1536]{1,0:T(8,128)(2,1)S(1)} %pad_maximum_fusion.3.refs_3_.refs_11_.refs_18_), channel_id=1, source_target_pairs={{0,8},{8,0},{1,9},{9,1},{2,10},{10,2},{3,11},{11,3},{4,12},{12,4},... | collective-permute-start | bytes 2359304 | tf_op jit(solution)/shard_map/ppermute | solution.py:1598
  193.0 32.2 %collective-permute-start.23 = (bf16[1024,512]{1,0:T(8,128)(2,1)}, bf16[1024,512]{1,0:T(8,128)(2,1)S(1)}, u32[]{:S(2)}, u32[]{:S(2)}) collective-permute-start(bf16[1024,512]{1,0:T(8,128)(2,1)} %get-tuple-element.87.after_ref), channel_id=1, source_target_pairs={{0,2},{2,0},{4,6},{6,4},{1,3},{3,1},{5,7},{7,5},{8,10},{10,8},{12,... | collective-permute-start | bytes 3145736 | tf_op jit(solution)/shard_map/ppermute | solution.py:1614
  194.2 29.7 %collective-permute-start.22 = (bf16[512,1024]{1,0:T(8,128)(2,1)}, bf16[512,1024]{1,0:T(8,128)(2,1)S(1)}, u32[]{:S(2)}, u32[]{:S(2)}) collective-permute-start(bf16[512,1024]{1,0:T(8,128)(2,1)} %get-tuple-element.98), channel_id=1, source_target_pairs={{0,16},{16,0},{1,17},{17,1},{2,18},{18,2},{3,19},{19,3},{4,20},{20... | collective-permute-start | bytes 3145736 | tf_op jit(solution)/shard_map/ppermute | solution.py:1606
  213.8 11.4 %collective-permute-start.21 = (f32[256,512]{1,0:T(8,128)}, f32[256,512]{1,0:T(8,128)}, u32[]{:S(2)}, u32[]{:S(2)}) collective-permute-start(f32[256,512]{1,0:T(8,128)} %get-tuple-element.96), channel_id=1, source_target_pairs={{0,8},{8,0},{1,9},{9,1},{2,10},{10,2},{3,11},{11,3},{4,12},{12,4},... | collective-permute-start | bytes 1572872 | tf_op jit(solution)/shard_map/ppermute | solution.py:1598
  216.2 51.6 %collective-permute-start.6 = (bf16[256,1024]{1,0:T(8,128)(2,1)S(1)}, bf16[256,1024]{1,0:T(8,128)(2,1)S(1)}, u32[]{:S(2)}, u32[]{:S(2)}) collective-permute-start(bf16[256,1024]{1,0:T(8,128)(2,1)S(1)} %copy-done.4), channel_id=1, source_target_pairs={{0,8},{8,0},{1,9},{9,1},{2,10},{10,2},{3,11},{11,3},{4,12},{12,4},... | collective-permute-start | bytes 1572872 | tf_op jit(solution)/shard_map/ppermute | solution.py:1598
  229.9 16.0 %collective-permute-start.31 = (bf16[64,512]{1,0:T(8,128)(2,1)}, bf16[64,512]{1,0:T(8,128)(2,1)S(1)}, u32[]{:S(2)}, u32[]{:S(2)}) collective-permute-start(bf16[64,512]{1,0:T(8,128)(2,1)} %get-tuple-element.115), channel_id=1, source_target_pairs={{0,1},{1,0},{2,3},{3,2},{4,5},{5,4},{6,7},{7,6},{8,9},{9,8},{10,11... | collective-permute-start | bytes 196616 | tf_op jit(solution)/shard_map/ppermute | solution.py:1602
  232.2 17.0 %collective-permute-start.24 = (bf16[512,128]{1,0:T(8,128)(2,1)}, bf16[512,128]{1,0:T(8,128)(2,1)S(1)}, u32[]{:S(2)}, u32[]{:S(2)}) collective-permute-start(bf16[512,128]{1,0:T(8,128)(2,1)} %get-tuple-element.100), channel_id=1, source_target_pairs={{0,1},{1,0},{2,3},{3,2},{4,5},{5,4},{6,7},{7,6},{8,9},{9,8},{10,11... | collective-permute-start | bytes 393224 | tf_op jit(solution)/shard_map/ppermute | solution.py:1602
  233.8 15.6 %collective-permute-start.25 = (bf16[512,128]{1,0:T(8,128)(2,1)}, bf16[512,128]{1,0:T(8,128)(2,1)S(1)}, u32[]{:S(2)}, u32[]{:S(2)}) collective-permute-start(bf16[512,128]{1,0:T(8,128)(2,1)} %get-tuple-element.101), channel_id=1, source_target_pairs={{0,16},{16,0},{1,17},{17,1},{2,18},{18,2},{3,19},{19,3},{4,20},{20... | collective-permute-start | bytes 393224 | tf_op jit(solution)/shard_map/ppermute | solution.py:1606
  234.5 15.0 %collective-permute-start.26 = (bf16[512,128]{1,0:T(8,128)(2,1)}, bf16[512,128]{1,0:T(8,128)(2,1)S(1)}, u32[]{:S(2)}, u32[]{:S(2)}) collective-permute-start(bf16[512,128]{1,0:T(8,128)(2,1)} %get-tuple-element.102), channel_id=1, source_target_pairs={{0,17},{17,0},{1,16},{16,1},{2,19},{19,2},{3,18},{18,3},{4,21},{21... | collective-permute-start | bytes 393224 | tf_op jit(solution)/shard_map/ppermute | solution.py:1610
  246.0 104.7 %collective-permute-start.56 = (bf16[1024,512]{1,0:T(8,128)(2,1)}, bf16[1024,512]{1,0:T(8,128)(2,1)}, u32[]{:S(2)}, u32[]{:S(2)}) collective-permute-start(bf16[1024,512]{1,0:T(8,128)(2,1)} %get-tuple-element.122), channel_id=1, source_target_pairs={{0,4},{4,0},{2,6},{6,2},{1,5},{5,1},{3,7},{7,3},{8,12},{12,8},{10,... | collective-permute-start | bytes 3145736 | tf_op jit(solution)/shard_map/ppermute | solution.py:1618
  249.1 112.4 %collective-permute-start.51 = (bf16[512,1024]{1,0:T(8,128)(2,1)}, bf16[512,1024]{1,0:T(8,128)(2,1)}, u32[]{:S(2)}, u32[]{:S(2)}) collective-permute-start(bf16[512,1024]{1,0:T(8,128)(2,1)} %get-tuple-element.120), channel_id=1, source_target_pairs={{0,1},{1,0},{2,3},{3,2},{4,5},{5,4},{6,7},{7,6},{8,9},{9,8},{10,11... | collective-permute-start | bytes 3145736 | tf_op jit(solution)/shard_map/ppermute | solution.py:1602
  276.8 113.4 %collective-permute-start.29 = (bf16[1024,640]{1,0:T(8,128)(2,1)}, bf16[1024,640]{1,0:T(8,128)(2,1)S(1)}, u32[]{:S(2)}, u32[]{:S(2)}) collective-permute-start(bf16[1024,640]{1,0:T(8,128)(2,1)} %get-tuple-element.113.refs_0_), channel_id=1, source_target_pairs={{0,16},{16,0},{1,17},{17,1},{2,18},{18,2},{3,19},{19,3},{4,20},{20... | collective-permute-start | bytes 3932168 | tf_op jit(solution)/shard_map/ppermute | solution.py:1606
  277.4 29.4 %copy-start.23 = (bf16[256,1024]{1,0:T(8,128)(2,1)S(1)}, bf16[256,1024]{1,0:T(8,128)(2,1)}, u32[]{:S(2)}) copy-start(bf16[256,1024]{1,0:T(8,128)(2,1)} %get-tuple-element.106) | copy-start | bytes 1572868
  277.4 30.2 %copy-start.2 = (bf16[4,128,2048]{2,1,0:T(8,128)(2,1)S(1)}, bf16[4,128,2048]{2,1,0:T(8,128)(2,1)}, u32[]{:S(2)}) copy-start(bf16[4,128,2048]{2,1,0:T(8,128)(2,1)} %conv_weight_grad.1.refs_12_) | copy-start | bytes 6291460
  306.8 1.6 collective-permute-start.37
  306.9 5.8 %collective-permute-start.27 = (bf16[128,1024]{1,0:T(8,128)(2,1)S(1)}, bf16[128,1024]{1,0:T(8,128)(2,1)S(1)}, u32[]{:S(2)}, u32[]{:S(2)}) collective-permute-start(bf16[128,1024]{1,0:T(8,128)(2,1)S(1)} %get-tuple-element.176), channel_id=1, source_target_pairs={{0,0},{1,4},{2,1},{3,5},{4,8},{5,12},{6,9},{7,13},{8,2},{9,6},{10,... | collective-permute-start | bytes 786440 | tf_op jit(solution)/shard_map/ppermute | solution.py:1594
  308.4 28.5 %copy-start.31 = (bf16[512,768]{1,0:T(8,128)(2,1)S(1)}, bf16[512,768]{1,0:T(8,128)(2,1)}, u32[]{:S(2)}) copy-start(bf16[512,768]{1,0:T(8,128)(2,1)} %get-tuple-element.114) | copy-start | bytes 2359300
  308.4 14.7 %collective-permute-start.28 = (bf16[128,1024]{1,0:T(8,128)(2,1)S(1)}, bf16[128,1024]{1,0:T(8,128)(2,1)S(1)}, u32[]{:S(2)}, u32[]{:S(2)}) collective-permute-start(bf16[128,1024]{1,0:T(8,128)(2,1)S(1)} %get-tuple-element.177), channel_id=1, source_target_pairs={{0,1},{1,5},{2,0},{3,4},{4,9},{5,13},{6,8},{7,12},{8,3},{9,7},{10,... | collective-permute-start | bytes 786440 | tf_op jit(solution)/shard_map/ppermute | solution.py:1594
  312.7 24.2 %collective-permute-start.38 = (bf16[128,1024]{1,0:T(8,128)(2,1)S(1)}, bf16[128,1024]{1,0:T(8,128)(2,1)S(1)}, u32[]{:S(2)}, u32[]{:S(2)}) collective-permute-start(bf16[128,1024]{1,0:T(8,128)(2,1)S(1)} %get-tuple-element.172), channel_id=1, source_target_pairs={{0,0},{1,4},{2,1},{3,5},{4,8},{5,12},{6,9},{7,13},{8,2},{9,6},{10,... | collective-permute-start | bytes 786440 | tf_op jit(solution)/shard_map/ppermute | solution.py:1594
  323.1 16.8 %collective-permute-start.39 = (bf16[128,1024]{1,0:T(8,128)(2,1)S(1)}, bf16[128,1024]{1,0:T(8,128)(2,1)S(1)}, u32[]{:S(2)}, u32[]{:S(2)}) collective-permute-start(bf16[128,1024]{1,0:T(8,128)(2,1)S(1)} %get-tuple-element.173), channel_id=1, source_target_pairs={{0,1},{1,5},{2,0},{3,4},{4,9},{5,13},{6,8},{7,12},{8,3},{9,7},{10,... | collective-permute-start | bytes 786440 | tf_op jit(solution)/shard_map/ppermute | solution.py:1594
  336.9 53.3 %collective-permute-start.30 = (bf16[512,768]{1,0:T(8,128)(2,1)S(1)}, bf16[512,768]{1,0:T(8,128)(2,1)}, u32[]{:S(2)}, u32[]{:S(2)}) collective-permute-start(bf16[512,768]{1,0:T(8,128)(2,1)S(1)} %copy-done.31), channel_id=1, source_target_pairs={{0,1},{1,0},{2,3},{3,2},{4,5},{5,4},{6,7},{7,6},{8,9},{9,8},{10,11... | collective-permute-start | bytes 2359304 | tf_op jit(solution)/shard_map/ppermute | solution.py:1602
  339.9 35.2 %collective-permute-start.40 = (bf16[2,128,2048]{2,1,0:T(8,128)(2,1)S(1)}, bf16[2,128,2048]{2,1,0:T(8,128)(2,1)S(1)}, u32[]{:S(2)}, u32[]{:S(2)}) collective-permute-start(bf16[2,128,2048]{2,1,0:T(8,128)(2,1)S(1)} %dynamic-slice_bitcast_fusion), channel_id=1, source_target_pairs={{0,2},{2,0},{4,6},{6,4},{1,3},{3,1},{5,7},{7,5},{8,10},{10,8},{12,... | collective-permute-start | bytes 3145736 | tf_op jit(solution)/shard_map/ppermute | solution.py:1614
  353.2 52.1 %collective-permute-start.57 = (bf16[512,512]{1,0:T(8,128)(2,1)}, bf16[512,512]{1,0:T(8,128)(2,1)S(1)}, u32[]{:S(2)}, u32[]{:S(2)}) collective-permute-start(bf16[512,512]{1,0:T(8,128)(2,1)} %fusion.9), channel_id=1, source_target_pairs={{0,1},{1,0},{2,3},{3,2},{4,5},{5,4},{6,7},{7,6},{8,9},{9,8},{10,11... | collective-permute-start | bytes 1572872 | tf_op jit(solution)/shard_map/ppermute | solution.py:1602
  364.1 43.3 %collective-permute-start.52 = (bf16[2,128,1024]{2,1,0:T(8,128)(2,1)}, bf16[2,128,1024]{2,1,0:T(8,128)(2,1)}, u32[]{:S(2)}, u32[]{:S(2)}) collective-permute-start(bf16[2,128,1024]{2,1,0:T(8,128)(2,1)} %fusion.11), channel_id=1, source_target_pairs={{0,2},{2,0},{4,6},{6,4},{1,3},{3,1},{5,7},{7,5},{8,10},{10,8},{12,... | collective-permute-start | bytes 1572872 | tf_op jit(solution)/shard_map/ppermute | solution.py:1614
  376.3 33.2 %collective-permute-start.41 = (bf16[128,2048]{1,0:T(8,128)(2,1)}, bf16[128,2048]{1,0:T(8,128)(2,1)}, u32[]{:S(2)}, u32[]{:S(2)}) collective-permute-start(bf16[128,2048]{1,0:T(8,128)(2,1)} %fusion.8), channel_id=1, source_target_pairs={{0,4},{4,0},{2,6},{6,2},{1,5},{5,1},{3,7},{7,3},{8,12},{12,8},{10,... | collective-permute-start | bytes 1572872 | tf_op jit(solution)/shard_map/ppermute | solution.py:1618
  401.3 50.3 %collective-permute-start.46 = (bf16[512,384]{1,0:T(8,128)(2,1)}, bf16[512,384]{1,0:T(8,128)(2,1)}, u32[]{:S(2)}, u32[]{:S(2)}) collective-permute-start(bf16[512,384]{1,0:T(8,128)(2,1)} %get-tuple-element.117.after_ref), channel_id=1, source_target_pairs={{0,16},{16,0},{1,17},{17,1},{2,18},{18,2},{3,19},{19,3},{4,20},{20... | collective-permute-start | bytes 1179656 | tf_op jit(solution)/shard_map/ppermute | solution.py:1606
  405.3 4.0 collective-permute-start.32
  406.1 45.5 %collective-permute-start.45 = (bf16[512,640]{1,0:T(8,128)(2,1)}, bf16[512,640]{1,0:T(8,128)(2,1)}, u32[]{:S(2)}, u32[]{:S(2)}) collective-permute-start(bf16[512,640]{1,0:T(8,128)(2,1)} %get-tuple-element.119), channel_id=1, source_target_pairs={{0,1},{1,0},{2,3},{3,2},{4,5},{5,4},{6,7},{7,6},{8,9},{9,8},{10,11... | collective-permute-start | bytes 1966088 | tf_op jit(solution)/shard_map/ppermute | solution.py:1602
  407.4 49.2 %collective-permute-start.58 = (bf16[512,512]{1,0:T(8,128)(2,1)S(1)}, bf16[512,512]{1,0:T(8,128)(2,1)}, u32[]{:S(2)}, u32[]{:S(2)}) collective-permute-start(bf16[512,512]{1,0:T(8,128)(2,1)S(1)} %fusion.2), channel_id=1, source_target_pairs={{0,16},{16,0},{1,17},{17,1},{2,18},{18,2},{3,19},{19,3},{4,20},{20... | collective-permute-start | bytes 1572872 | tf_op jit(solution)/shard_map/ppermute | solution.py:1606
  409.4 18.4 %collective-permute-start.53 = (bf16[128,1024]{1,0:T(8,128)(2,1)S(1)}, bf16[128,1024]{1,0:T(8,128)(2,1)S(1)}, u32[]{:S(2)}, u32[]{:S(2)}) collective-permute-start(bf16[128,1024]{1,0:T(8,128)(2,1)S(1)} %fusion.19), channel_id=1, source_target_pairs={{0,4},{4,0},{2,6},{6,2},{1,5},{5,1},{3,7},{7,3},{8,12},{12,8},{10,... | collective-permute-start | bytes 786440 | tf_op jit(solution)/shard_map/ppermute | solution.py:1618
  409.5 16.5 %collective-permute-start.33 = (f32[8,48,128]{2,1,0:T(8,128)S(1)}, f32[8,48,128]{2,1,0:T(8,128)S(1)}, u32[]{:S(2)}, u32[]{:S(2)}) collective-permute-start(f32[8,48,128]{2,1,0:T(8,128)S(1)} %add.307), channel_id=1, source_target_pairs={{0,16},{16,0},{1,17},{17,1},{2,18},{18,2},{3,19},{19,3},{4,20},{20... | collective-permute-start | bytes 589832 | tf_op jit(solution)/shard_map/ppermute | solution.py:1606
  426.0 10.7 %collective-permute-start.42 = (bf16[128,1024]{1,0:T(8,128)(2,1)S(1)}, bf16[128,1024]{1,0:T(8,128)(2,1)S(1)}, u32[]{:S(2)}, u32[]{:S(2)}) collective-permute-start(bf16[128,1024]{1,0:T(8,128)(2,1)S(1)} %constant_dynamic-slice_fusion), channel_id=1, source_target_pairs={{0,1},{1,0},{2,3},{3,2},{4,5},{5,4},{6,7},{7,6},{8,9},{9,8},{10,11... | collective-permute-start | bytes 786440 | tf_op jit(solution)/shard_map/ppermute | solution.py:1602
  427.7 23.9 %copy-start.18 = (bf16[512,1024]{1,0:T(8,128)(2,1)S(1)}, bf16[512,1024]{1,0:T(8,128)(2,1)}, u32[]{:S(2)}) copy-start(bf16[512,1024]{1,0:T(8,128)(2,1)} %get-tuple-element.118) | copy-start | bytes 3145732
  427.8 8.2 %collective-permute-start.34 = (f32[2,2,48,128]{3,2,1,0:T(8,128)S(1)}, f32[2,2,48,128]{3,2,1,0:T(8,128)S(1)}, u32[]{:S(2)}, u32[]{:S(2)}) collective-permute-start(f32[2,2,48,128]{3,2,1,0:T(8,128)S(1)} %dynamic-slice_bitcast_fusion.3), channel_id=1, source_target_pairs={{0,1},{1,0},{2,3},{3,2},{4,5},{5,4},{6,7},{7,6},{8,9},{9,8},{10,11... | collective-permute-start | bytes 294920 | tf_op jit(solution)/shard_map/ppermute | solution.py:1602
  436.0 19.3 %collective-permute-start.54 = (bf16[128,1024]{1,0:T(8,128)(2,1)}, bf16[128,1024]{1,0:T(8,128)(2,1)}, u32[]{:S(2)}, u32[]{:S(2)}) collective-permute-start(bf16[128,1024]{1,0:T(8,128)(2,1)} %fusion.12), channel_id=1, source_target_pairs={{0,16},{16,0},{1,17},{17,1},{2,18},{18,2},{3,19},{19,3},{4,20},{20... | collective-permute-start | bytes 786440 | tf_op jit(solution)/shard_map/ppermute | solution.py:1606
  436.7 4.6 collective-permute-start.35
  441.4 4.8 collective-permute-start.36
  446.2 12.1 %collective-permute-start.43 = (bf16[2,128,1024]{2,1,0:T(8,128)(2,1)}, bf16[2,128,1024]{2,1,0:T(8,128)(2,1)S(1)}, u32[]{:S(2)}, u32[]{:S(2)}) collective-permute-start(bf16[2,128,1024]{2,1,0:T(8,128)(2,1)} %pad_maximum_fusion.8), channel_id=1, source_target_pairs={{0,16},{16,0},{1,17},{17,1},{2,18},{18,2},{3,19},{19,3},{4,20},{20... | collective-permute-start | bytes 1572872 | tf_op jit(solution)/shard_map/ppermute | solution.py:1606
  453.2 11.3 %collective-permute-start.47 = (bf16[2,128,1024]{2,1,0:T(8,128)(2,1)S(1)}, bf16[2,128,1024]{2,1,0:T(8,128)(2,1)S(1)}, u32[]{:S(2)}, u32[]{:S(2)}) collective-permute-start(bf16[2,128,1024]{2,1,0:T(8,128)(2,1)S(1)} %fusion.10), channel_id=1, source_target_pairs={{0,2},{2,0},{4,6},{6,4},{1,3},{3,1},{5,7},{7,5},{8,10},{10,8},{12,... | collective-permute-start | bytes 1572872 | tf_op jit(solution)/shard_map/ppermute | solution.py:1614
  456.4 8.4 %collective-permute-start.55 = (bf16[128,2048]{1,0:T(8,128)(2,1)S(1)}, bf16[128,2048]{1,0:T(8,128)(2,1)S(1)}, u32[]{:S(2)}, u32[]{:S(2)}) collective-permute-start(bf16[128,2048]{1,0:T(8,128)(2,1)S(1)} %pad_maximum_fusion.9), channel_id=1, source_target_pairs={{0,8},{8,0},{1,9},{9,1},{2,10},{10,2},{3,11},{11,3},{4,12},{12,4},... | collective-permute-start | bytes 1572872 | tf_op jit(solution)/shard_map/ppermute | solution.py:1598
  457.7 18.7 %collective-permute-start.59 = (bf16[512,512]{1,0:T(8,128)(2,1)S(1)}, bf16[512,512]{1,0:T(8,128)(2,1)S(1)}, u32[]{:S(2)}, u32[]{:S(2)}) collective-permute-start(bf16[512,512]{1,0:T(8,128)(2,1)S(1)} %add_convert_fusion), channel_id=1, source_target_pairs={{0,8},{8,0},{1,9},{9,1},{2,10},{10,2},{3,11},{11,3},{4,12},{12,4},... | collective-permute-start | bytes 1572872 | tf_op jit(solution)/shard_map/ppermute | solution.py:1598
  458.4 24.8 %collective-permute-start.44 = (bf16[4,128,1024]{2,1,0:T(8,128)(2,1)S(1)}, bf16[4,128,1024]{2,1,0:T(8,128)(2,1)S(1)}, u32[]{:S(2)}, u32[]{:S(2)}) collective-permute-start(bf16[4,128,1024]{2,1,0:T(8,128)(2,1)S(1)} %pad_maximum_fusion.1), channel_id=1, source_target_pairs={{0,8},{8,0},{1,9},{9,1},{2,10},{10,2},{3,11},{11,3},{4,12},{12,4},... | collective-permute-start | bytes 3145736 | tf_op jit(solution)/shard_map/ppermute | solution.py:1598
  464.7 10.1 %collective-permute-start.48 = (bf16[128,1024]{1,0:T(8,128)(2,1)S(1)}, bf16[128,1024]{1,0:T(8,128)(2,1)S(1)}, u32[]{:S(2)}, u32[]{:S(2)}) collective-permute-start(bf16[128,1024]{1,0:T(8,128)(2,1)S(1)} %fusion.18), channel_id=1, source_target_pairs={{0,4},{4,0},{2,6},{6,2},{1,5},{5,1},{3,7},{7,3},{8,12},{12,8},{10,... | collective-permute-start | bytes 786440 | tf_op jit(solution)/shard_map/ppermute | solution.py:1618
  475.0 6.4 %collective-permute-start.49 = (bf16[128,1024]{1,0:T(8,128)(2,1)S(1)}, bf16[128,1024]{1,0:T(8,128)(2,1)S(1)}, u32[]{:S(2)}, u32[]{:S(2)}) collective-permute-start(bf16[128,1024]{1,0:T(8,128)(2,1)S(1)} %fusion.13), channel_id=1, source_target_pairs={{0,16},{16,0},{1,17},{17,1},{2,18},{18,2},{3,19},{19,3},{4,20},{20... | collective-permute-start | bytes 786440 | tf_op jit(solution)/shard_map/ppermute | solution.py:1606
  481.6 10.2 %collective-permute-start.50 = (bf16[128,2048]{1,0:T(8,128)(2,1)S(1)}, bf16[128,2048]{1,0:T(8,128)(2,1)S(1)}, u32[]{:S(2)}, u32[]{:S(2)}) collective-permute-start(bf16[128,2048]{1,0:T(8,128)(2,1)S(1)} %slice_dynamic-update-slice_fusion.10), channel_id=1, source_target_pairs={{0,8},{8,0},{1,9},{9,1},{2,10},{10,2},{3,11},{11,3},{4,12},{12,4},... | collective-permute-start | bytes 1572872 | tf_op jit(solution)/shard_map/ppermute | solution.py:1598
  (28 other events, 173.6 us)
